TPU v7x, 256 devices: a whole 4x4x8 slice. The times are simulated.
256 devices in a mesh: mer: 64 (over z, x, core), blk: 4 (over y).
Axes of the slice: x: 4, y: 4, z: 8, core: 2. Of those that a mesh axis runs over, the one named last changes fastest.
Arguments:
- disp_now: float32 [8000, 2, 2048], P('mer', None, 'blk'), may hold values from -6 to 6
- disp_prev: float32 [8000, 2, 2048], P('mer', None, 'blk'), may hold values from -6 to 6
- kappa: bfloat16 [8000, 4096], P('mer', 'blk'), may hold values from 0.5 to 4
- radius: float32 [8000], P('mer'), may hold values from 50 to 2000
- fwd_strain: bfloat16 [2, 3, 8000, 4096], P(None, None, 'mer', 'blk'), may hold values from -6 to 6
- order_bucket: int32 [320], P('mer'), may hold values from 0 to 3
- shared_nodes: int32 [64, 2, 5], P('mer'), may hold values from 0 to 124
- region_map: int32 [320], P('mer'), may hold values from 0 to 4095
Outputs:
- displacement: float32 [8000, 2, 2048], P('mer', None, 'blk')
- kernel: float32 [4096, 1024], P('mer', 'blk')
Inputs may be any that keep to these rules, and one draw needn't show every extreme that they name: `shared_nodes`: entry k of row 1 of partition i and entry k of row 0 of partition i + 1 name the same physical node; row 0 of the first and row 1 of the last partition name no partner.
All inputs are finite; a program needn't handle non-finite values.
Results may differ from a plain program's by a relative error of at most 0.0031.
The roundings to bfloat16 on the way count: a program that leaves them out, or rounds other values in their place, can miss the bound.
Values may be sent and summed in bfloat16 or wider, within the bound.
No kernel may reach another device: no remote copies, remote signals or barrier semaphores. Data moves between devices by JAX's collectives and lax.ppermute only.
A program may use at most 128 MiB of HBM per device.

v0:
```python
import math

import jax
import jax.numpy as jnp
import numpy as np
from jax import lax
from jax.sharding import PartitionSpec as P

MAXO = 2048
STEPS = 2
REG_DEV = 64
SECT_DEV = 256


time_step_sq = 0.0004
kernel_scale = 0.0001
bucket_orders = (8, 64, 512, 2048)


def shifted(x, axis, by):
    devices = lax.axis_size(axis)
    pairs = [(i, i + by) for i in range(devices) if 0 <= i + by < devices]
    return lax.ppermute(x, axis, pairs)


def gll_tables():
    nodes = np.array([-1.0, -math.sqrt(3.0 / 7.0), 0.0, math.sqrt(3.0 / 7.0), 1.0])
    weights_line = np.array([0.1, 49.0 / 90.0, 32.0 / 45.0, 49.0 / 90.0, 0.1])
    legendre = (35.0 * nodes**4 - 30.0 * nodes**2 + 3.0) / 8.0
    deriv = np.zeros((5, 5))
    for row_index in range(5):
        for col_index in range(5):
            if row_index != col_index:
                deriv[row_index, col_index] = (
                    legendre[row_index]
                    / legendre[col_index]
                    / (nodes[row_index] - nodes[col_index])
                )
    deriv[0, 0] = -5.0
    deriv[4, 4] = 5.0
    return (deriv, np.outer(weights_line, weights_line).reshape(25))


def order_mask(bucket, orders):
    levels = jnp.zeros(bucket.shape, jnp.int32)
    for position, value in enumerate(bucket_orders):
        levels = levels + jnp.where(bucket == position, value, 0).astype(jnp.int32)
    levels = jnp.repeat(levels, 25)
    cosine_part = orders[None, :] < levels[:, None]
    sine_part = cosine_part & (orders[None, :] >= 1)
    return jnp.stack([cosine_part, sine_part], axis=1).astype(jnp.float32)


def fourier_table(orders, samples, nphi):
    turns = orders[:, None] * samples[None, :] % nphi
    angle = turns.astype(jnp.float32) * (2.0 * math.pi / nphi)
    return jnp.stack([jnp.cos(angle), jnp.sin(angle)]).astype(jnp.bfloat16)


def strains(field, radius, orders, deriv):
    points, parts, count = field.shape
    shaped = field.reshape(points // 25, 5, 5, parts, count)
    along_s = jnp.einsum("aj,ejbcm->eabcm", deriv, shaped, precision=lax.Precision.HIGHEST).reshape(
        field.shape
    )
    along_z = jnp.einsum("bj,eajcm->eabcm", deriv, shaped, precision=lax.Precision.HIGHEST).reshape(
        field.shape
    )
    scale = orders.astype(jnp.float32)[None, :] / radius[:, None]
    beside_all = jnp.stack([scale * field[:, 1], -scale * field[:, 0]], axis=1)
    return jnp.stack([along_s, along_z, beside_all])


def divergence(back, radius, orders, deriv):
    points, parts, count = back.shape[1:]
    first = back[0].reshape(points // 25, 5, 5, parts, count)
    second = back[1].reshape(points // 25, 5, 5, parts, count)
    term_s = jnp.einsum("aj,eabcm->ejbcm", deriv, first, precision=lax.Precision.HIGHEST).reshape(
        points, parts, count
    )
    term_z = jnp.einsum("bj,eabcm->eajcm", deriv, second, precision=lax.Precision.HIGHEST).reshape(
        points, parts, count
    )
    scale = orders.astype(jnp.float32)[None, :] / radius[:, None]
    third = back[2]
    beside_all = jnp.stack([-scale * third[:, 1], scale * third[:, 0]], axis=1)
    return term_s + term_z + beside_all


def local(disp_now, disp_prev, kappa, radius, fwd_strain, order_bucket, shared_nodes, region_map):
    points = disp_now.shape[0]
    order_count = disp_now.shape[2]
    samp_count = kappa.shape[1]
    nphi = 2 * MAXO
    blk_index = lax.axis_index("blk")
    orders = blk_index * order_count + jnp.arange(order_count, dtype=jnp.int32)
    samples = blk_index * samp_count + jnp.arange(samp_count, dtype=jnp.int32)
    all_orders = jnp.arange(MAXO, dtype=jnp.int32)
    synth_table = fourier_table(all_orders, samples, nphi)
    deriv_np, gllw_np = gll_tables()
    deriv = jnp.asarray(deriv_np, jnp.float32)
    mask = order_mask(order_bucket, orders)
    weight_pt = jnp.tile(jnp.asarray(gllw_np, jnp.float32), points // 25) * radius
    quad = weight_pt * (2.0 * math.pi / nphi)
    zero_mode = jnp.stack(
        [(orders == 0).astype(jnp.float32), jnp.zeros((order_count,), jnp.float32)]
    )
    mass = weight_pt[:, None, None] * math.pi * (1.0 + zero_mode)[None]
    left_idx = shared_nodes[0, 0]
    right_idx = shared_nodes[0, 1]
    current = disp_now * mask
    previous = disp_prev * mask
    density = jnp.zeros((points, samp_count), jnp.float32)
    for section in range(STEPS):
        strain = strains(current, radius, orders, deriv).astype(jnp.bfloat16)
        piece = lax.all_gather(strain, "blk", axis=3, tiled=True)
        rows = lax.slice_in_dim(synth_table, 0, piece.shape[3], axis=1)
        phys = jnp.zeros((3, points, samp_count), jnp.float32) + jnp.einsum(
            "ipcm,cmk->ipk", piece, rows, preferred_element_type=jnp.float32
        )
        stress = (phys * kappa.astype(jnp.float32)[None] * quad[None, :, None]).astype(jnp.bfloat16)
        density = (
            density
            + jnp.sum(phys * fwd_strain[section].astype(jnp.float32), axis=0)
            * quad[:, None]
            * kernel_scale
        )
        back = lax.psum_scatter(
            jnp.einsum("cmk,ipk->mcip", synth_table, stress, preferred_element_type=jnp.float32),
            "blk",
            scatter_dimension=0,
            tiled=True,
        ).transpose(2, 3, 1, 0)
        force = divergence(back, radius, orders, deriv)
        from_next = shifted(force[left_idx], "mer", -1)
        from_before = shifted(force[right_idx], "mer", 1)
        assembled = force.at[right_idx].add(from_next).at[left_idx].add(from_before)
        accel = -mask * assembled / mass
        current, previous = (2.0 * current - previous + time_step_sq * accel, current)
    sectors = density.reshape(points, SECT_DEV, samp_count // SECT_DEV).sum(axis=-1)
    region_pt = jnp.repeat(region_map, 25)
    partial_kernel = jax.ops.segment_sum(
        sectors, region_pt, num_segments=REG_DEV * lax.axis_size("mer")
    )
    kernel = lax.psum_scatter(partial_kernel, "mer", scatter_dimension=0, tiled=True)
    return (current, kernel)


def solution(mesh):
    in_specs = (
        P("mer", None, "blk"),
        P("mer", None, "blk"),
        P("mer", "blk"),
        P("mer"),
        P(None, None, "mer", "blk"),
        P("mer"),
        P("mer", None, None),
        P("mer"),
    )
    out_specs = (P("mer", None, "blk"), P("mer", "blk"))
    return jax.shard_map(local, mesh=mesh, in_specs=in_specs, out_specs=out_specs, check_vma=False)
```

profile of v0, /device:TPU:1, one launch (start us, length us, event | category | flops | bytes accessed | tf_op | source)
XLA Modules:
  0.0 435.8 jit_solution(7082877108432063819)
XLA Ops:
  8.2 1.2 copy_select_fusion.1
  9.8 1.6 fusion.17
  11.5 1.7 fusion.16
  13.9 1.0 pad_maximum_fusion
  15.0 0.9 convert_element_type.63
  15.9 3.0 fusion.60
  18.9 34.8 %cosine_convert_fusion = (bf16[1,2048,1024]{2,1,0:T(8,128)(2,1)}, bf16[1,2048,1024]{2,1,0:T(8,128)(2,1)}) fusion(s32[1024]{0:T(1024)S(1)} %iota_add_fusion), kind=kLoop, calls=%fused_computation.17 | loop fusion | flops 33554432 | bytes 8392704 | tf_op jit(solution)/shard_map/convert.14
  53.7 7.2 %all-gather.3.cloned.1.call-done = bf16[3,125,2,2048]{3,1,2,0:T(8,128)(2,1)} async-done(((bf16[3,125,2,512]{3,1,2,0:T(8,128)(2,1)}), bf16[3,125,2,2048]{3,1,2,0:T(8,128)(2,1)}) %all-gather.3.cloned.1.call-update) | async-done | bytes 3072016 | tf_op jit(solution)/shard_map/all_gather | solution.py:116
  61.0 7.9 %fusion.9 = (f32[125,1024]{1,0:T(8,128)}, f32[3,125,1024,1]{2,1,3,0:T(8,128)S(1)}) fusion(bf16[1,3,125,1024]{3,0,2,1:T(2,128)(2,1)S(1)} %copy-done.6, bf16[3,125,2,2048]{3,1,2,0:T(8,128)(2,1)} %all-gather.3.cloned.1.call-done, bf16[1,2048,1024]{2,1,0:T(8,128)(2,1)} %get-tuple-element.25, bf16[1,2048,1024]{2,1,0:T(8,128)(2,1)} %get-tuple-element.24), kind=kOutput, calls=%fused_computation.28 | convolution fusion | flops 3150946304 | bytes 14276608 | tf_op jit(solution)/shard_map/ipcm,cmk->ipk/dot_general | solution.py:118
  68.8 5.4 %convolution_bitcast_fusion.1 = f32[2048,2,3,125]{0,3,1,2:T(8,128)} fusion(f32[3,125,1024,1]{2,1,3,0:T(8,128)S(1)} %get-tuple-element.33, f32[125]{0:T(128)S(1)} %get-tuple-element.29, f32[125,1024]{1,0:T(8,128)S(1)} %copy-done.9, bf16[1,2048,1024]{2,1,0:T(8,128)(2,1)S(1)} %copy-done.4, bf16[1,2048,1024]{2,1,0:T(8,128)(2,1)S(1)} %copy-done.2), kind=kOutput, calls=%fused_computation.22 | convolution fusion | flops 3163657216 | bytes 16581108 | tf_op jit(solution)/shard_map/cmk,ipk->mcip/dot_general | solution.py:129
  75.0 66.3 %reduce-scatter.4.cloned.1.call-done = f32[512,2,3,125]{0,3,1,2:T(8,128)} async-done(((f32[2048,2,3,125]{0,3,1,2:T(8,128)}), f32[512,2,3,125]{0,3,1,2:T(8,128)}) %reduce-scatter.4.cloned.1.call-update) | async-done | bytes 1536016 | tf_op jit(solution)/shard_map/reduce_scatter | solution.py:128
  141.2 1.5 fusion.59
  143.2 0.9 fusion.25
  144.6 1.2 fusion.15
  147.9 2.6 collective-permute-start
  150.5 3.0 collective-permute-start.1
  155.1 1.4 fusion.39
  157.1 0.9 fusion.19
  158.0 0.9 fusion.18
  159.4 1.0 pad_maximum_fusion.1
  160.5 45.4 %all-gather.5.cloned.1.call-done = bf16[3,125,2,2048]{3,1,2,0:T(8,128)(2,1)} async-done(((bf16[3,125,2,512]{3,1,2,0:T(8,128)(2,1)}), bf16[3,125,2,2048]{3,1,2,0:T(8,128)(2,1)}) %all-gather.5.cloned.1.call-update) | async-done | bytes 3072016 | tf_op jit(solution)/shard_map/all_gather | solution.py:116
  205.9 7.9 %fusion.8 = (f32[125,1024]{1,0:T(8,128)}, f32[3,125,1024,1]{2,1,3,0:T(8,128)S(1)}) fusion(bf16[1,3,125,1024]{3,0,2,1:T(2,128)(2,1)S(1)} %get-tuple-element.14, bf16[3,125,2,2048]{3,1,2,0:T(8,128)(2,1)} %all-gather.5.cloned.1.call-done, bf16[1,2048,1024]{2,1,0:T(8,128)(2,1)} %get-tuple-element.25, bf16[1,2048,1024]{2,1,0:T(8,128)(2,1)} %get-tuple-element.24), kind=kOutput, calls=%fused_computation.26 | convolution fusion | flops 3150946304 | bytes 14276608 | tf_op jit(solution)/shard_map/ipcm,cmk->ipk/dot_general | solution.py:118
  213.8 5.4 %convolution_bitcast_fusion = f32[2048,2,3,125]{0,3,1,2:T(8,128)} fusion(f32[3,125,1024,1]{2,1,3,0:T(8,128)S(1)} %get-tuple-element.35, f32[125]{0:T(128)S(1)} %get-tuple-element.29, f32[125,1024]{1,0:T(8,128)S(1)} %copy-done.10, bf16[1,2048,1024]{2,1,0:T(8,128)(2,1)S(1)} %copy-done.5, bf16[1,2048,1024]{2,1,0:T(8,128)(2,1)S(1)} %copy-done.3), kind=kOutput, calls=%fused_computation.21 | convolution fusion | flops 3163657216 | bytes 16581108 | tf_op jit(solution)/shard_map/cmk,ipk->mcip/dot_general | solution.py:129
  221.3 3.7 scatter_custom_fusion.4
  225.0 61.2 %reduce-scatter.6.cloned.1.call-done = f32[512,2,3,125]{0,3,1,2:T(8,128)} async-done(((f32[2048,2,3,125]{0,3,1,2:T(8,128)}), f32[512,2,3,125]{0,3,1,2:T(8,128)}) %reduce-scatter.6.cloned.1.call-update) | async-done | bytes 1536016 | tf_op jit(solution)/shard_map/reduce_scatter | solution.py:128
  286.2 1.5 fusion.58
  288.5 1.0 fusion.20
  289.5 1.2 fusion.14
  292.3 2.5 collective-permute-start.2
  295.4 3.0 collective-permute-start.3
  300.4 1.2 copy.126
  301.6 127.6 %reduce-scatter.8.cloned.1.call-done = f32[64,256]{1,0:T(8,128)} async-done(((f32[4096,256]{1,0:T(8,128)}), f32[64,256]{1,0:T(8,128)}) %reduce-scatter.8.cloned.1.call-update) | async-done | bytes 65552 | tf_op jit(solution)/shard_map/reduce_scatter | solution.py:145
  (104 shorter events, 15.5 us)
Async XLA Ops:
  7.2 6.5 %copy-start.13 = (f32[125]{0:T(128)S(1)}, f32[125]{0:T(128)}, u32[]{:S(2)}) copy-start(f32[125]{0:T(128)} %param.13) | copy-start | bytes 1504
  7.2 53.8 %all-gather.3.cloned.1.call-start = ((), (), s32[]{:S(2)}) async-start(), calls=%async_computation.3 | async-start | bytes 3932160 | tf_op jit(solution)/shard_map/all_gather | solution.py:116
  9.8 5.1 %copy-start.16 = (f32[25]{0:T(128)S(1)}, f32[25]{0:T(128)}, u32[]{:S(2)}) copy-start(f32[25]{0:T(128)} %constant.67.clone) | copy-start | bytes 304
  9.8 5.2 %copy-start.12 = (bf16[125,1024]{1,0:T(8,128)(2,1)S(1)}, bf16[125,1024]{1,0:T(8,128)(2,1)}, u32[]{:S(2)}) copy-start(bf16[125,1024]{1,0:T(8,128)(2,1)} %param.12) | copy-start | bytes 768004
  11.5 4.5 %copy-start = (bf16[2,3,125,1024]{3,0,2,1:T(2,128)(2,1)S(1)}, bf16[2,3,125,1024]{3,0,2,1:T(2,128)(2,1)}, u32[]{:S(2)}) copy-start(bf16[2,3,125,1024]{3,0,2,1:T(2,128)(2,1)} %param.14) | copy-start | bytes 4608004
  14.9 126.4 %reduce-scatter.4.cloned.1.call-start = ((), (), s32[]{:S(2)}) async-start(), calls=%async_computation.4 | async-start | bytes 7864320 | tf_op jit(solution)/shard_map/reduce_scatter | solution.py:128
  18.9 42.0 %copy-start.6 = (bf16[1,3,125,1024]{3,0,2,1:T(2,128)(2,1)S(1)}, bf16[1,3,125,1024]{3,0,2,1:T(2,128)(2,1)}, u32[]{:S(2)}) copy-start(bf16[1,3,125,1024]{3,0,2,1:T(2,128)(2,1)} %get-tuple-element.15) | copy-start | bytes 2304004
  61.0 7.9 %copy-start.2 = (bf16[1,2048,1024]{2,1,0:T(8,128)(2,1)S(1)}, bf16[1,2048,1024]{2,1,0:T(8,128)(2,1)}, u32[]{:S(2)}) copy-start(bf16[1,2048,1024]{2,1,0:T(8,128)(2,1)} %get-tuple-element.24) | copy-start | bytes 12582916
  61.0 7.9 %copy-start.4 = (bf16[1,2048,1024]{2,1,0:T(8,128)(2,1)S(1)}, bf16[1,2048,1024]{2,1,0:T(8,128)(2,1)}, u32[]{:S(2)}) copy-start(bf16[1,2048,1024]{2,1,0:T(8,128)(2,1)} %get-tuple-element.25) | copy-start | bytes 12582916
  61.0 7.9 %copy-start.9 = (f32[125,1024]{1,0:T(8,128)S(1)}, f32[125,1024]{1,0:T(8,128)}, u32[]{:S(2)}) copy-start(f32[125,1024]{1,0:T(8,128)} %convert_element_type.63) | copy-start | bytes 1536004
  74.3 0.7 copy-start.14
  74.3 68.9 %copy-start.11 = (f32[5,5,1,1,1]{1,0,4,3,2:T(8,128)S(1)}, f32[5,5,1,1,1]{1,0,4,3,2:T(8,128)}, u32[]{:S(2)}) copy-start(f32[5,5,1,1,1]{1,0,4,3,2:T(8,128)} %constant.78) | copy-start | bytes 304
  74.3 131.6 %all-gather.5.cloned.1.call-start = ((), (), s32[]{:S(2)}) async-start(), calls=%async_computation.5 | async-start | bytes 3932160 | tf_op jit(solution)/shard_map/all_gather | solution.py:116
  144.2 10.9 %copy-start.1 = (f32[125,2,512]{2,1,0:T(2,128)S(1)}, f32[125,2,512]{2,1,0:T(2,128)}, u32[]{:S(2)}) copy-start(f32[125,2,512]{2,1,0:T(2,128)} %param.10) | copy-start | bytes 1536004
  147.9 5.6 %collective-permute-start = (f32[5,2,512]{2,1,0:T(2,128)S(1)}, f32[5,2,512]{2,1,0:T(2,128)S(1)}, u32[]{:S(2)}, u32[]{:S(2)}) collective-permute-start(f32[5,2,512]{2,1,0:T(2,128)S(1)} %gather_fusion), channel_id=1, source_target_pairs={{4,0},{8,4},{12,8},{16,12},{20,16},{24,20},{28,24},{32,28},{36,32}... | collective-permute-start | bytes 61448 | tf_op jit(solution)/shard_map/ppermute | solution.py:23
  150.5 3.9 collective-permute-start.1
  160.4 125.8 %reduce-scatter.6.cloned.1.call-start = ((), (), s32[]{:S(2)}) async-start(), calls=%async_computation.6 | async-start | bytes 7864320 | tf_op jit(solution)/shard_map/reduce_scatter | solution.py:128
  205.9 7.9 %copy-start.3 = (bf16[1,2048,1024]{2,1,0:T(8,128)(2,1)S(1)}, bf16[1,2048,1024]{2,1,0:T(8,128)(2,1)}, u32[]{:S(2)}) copy-start(bf16[1,2048,1024]{2,1,0:T(8,128)(2,1)} %get-tuple-element.24) | copy-start | bytes 12582916
  205.9 7.9 %copy-start.5 = (bf16[1,2048,1024]{2,1,0:T(8,128)(2,1)S(1)}, bf16[1,2048,1024]{2,1,0:T(8,128)(2,1)}, u32[]{:S(2)}) copy-start(bf16[1,2048,1024]{2,1,0:T(8,128)(2,1)} %get-tuple-element.25) | copy-start | bytes 12582916
  205.9 7.9 %copy-start.10 = (f32[125,1024]{1,0:T(8,128)S(1)}, f32[125,1024]{1,0:T(8,128)}, u32[]{:S(2)}) copy-start(f32[125,1024]{1,0:T(8,128)} %convert_element_type.63) | copy-start | bytes 1536004
  219.2 0.7 copy-start.15
  219.2 1.1 copy-start.7
  219.2 1.2 copy-start.8
  219.3 210.0 %reduce-scatter.8.cloned.1.call-start = ((), (), s32[]{:S(2)}) async-start(), calls=%async_computation.7 | async-start | bytes 4259840 | tf_op jit(solution)/shard_map/reduce_scatter | solution.py:145
  292.3 6.2 %collective-permute-start.2 = (f32[5,2,512]{2,1,0:T(2,128)S(1)}, f32[5,2,512]{2,1,0:T(2,128)S(1)}, u32[]{:S(2)}, u32[]{:S(2)}) collective-permute-start(f32[5,2,512]{2,1,0:T(2,128)S(1)} %gather_fusion.2), channel_id=1, source_target_pairs={{4,0},{8,4},{12,8},{16,12},{20,16},{24,20},{28,24},{32,28},{36,32}... | collective-permute-start | bytes 61448 | tf_op jit(solution)/shard_map/ppermute | solution.py:23
  295.4 3.9 collective-permute-start.3
Sparse Core Ops, SparseCore 0:
  15.0 45.9 all-gather.2
  74.4 66.7 reduce-scatter.3
  160.5 45.3 all-gather.4
  219.4 66.8 reduce-scatter.5
  290.8 138.4 reduce-scatter.7
where the time goes:
time: 440 us; the launch traced here: 436 us
  waiting for transfers between devices  308 us (70%)
  other arithmetic  49.3 us (11%)
  matrix products  35.9 us (8%)
  local copies, waits for them, and re-layouts  16.3 us (4%)
  between operations  14.3 us (3%)
  starting transfers between devices  11.7 us (3%)
    reduce_scatter x1, waiting for transfers between devices, local(): lax.psum_scatter(partial_kernel, 'mer', scatter_dimension=0, tiled=True)  128 us
    reduce_scatter x2, waiting for transfers between devices, local(): lax.psum_scatter(jnp.einsum('cmk,ipk->mcip', synth_table, stress, preferr...  127 us
    all_gather x2, waiting for transfers between devices, local(): piece = lax.all_gather(strain, 'blk', axis=3, tiled=True)  52.7 us
    another operation x3, other arithmetic  35 us
    dot_general x2, matrix products, local(): jnp.einsum('ipcm,cmk->ipk', piece, rows, preferred_element_type=jnp.float32)  15.8 us
    ppermute x4, starting transfers between devices, shifted(): return lax.ppermute(x, axis, pairs)  11.1 us
    dot_general x2, matrix products, local(): jnp.einsum('cmk,ipk->mcip', synth_table, stress, preferred_element_type=j...  10.9 us
  transfers between devices with their start and end apart: 9, of which 7 were waited for; matrix products, arithmetic and copies ran while one was open for 12% of the time, Pallas kernels for 0%

commit v1 on v0

v1 whole, which is shorter than its diff:
```python
import functools
import math

import jax
import jax.numpy as jnp
import numpy as np
from jax import lax
from jax.experimental import pallas as pl
from jax.experimental.pallas import tpu as pltpu
from jax.sharding import PartitionSpec as P

MAXO = 2048
STEPS = 2
PTS = 128
ELEM_ROWS = 8
TABLE_STRIDE = 64

time_step_sq = 0.0004
kernel_scale = 0.0001
bucket_orders = (8, 64, 512, 2048)

f32 = jnp.float32
bf16 = jnp.bfloat16


def gll_tables():
    nodes = np.array([-1.0, -math.sqrt(3.0 / 7.0), 0.0, math.sqrt(3.0 / 7.0), 1.0])
    weights_line = np.array([0.1, 49.0 / 90.0, 32.0 / 45.0, 49.0 / 90.0, 0.1])
    legendre = (35.0 * nodes**4 - 30.0 * nodes**2 + 3.0) / 8.0
    deriv = np.zeros((5, 5))
    for row_index in range(5):
        for col_index in range(5):
            if row_index != col_index:
                deriv[row_index, col_index] = (
                    legendre[row_index]
                    / legendre[col_index]
                    / (nodes[row_index] - nodes[col_index])
                )
    deriv[0, 0] = -5.0
    deriv[4, 4] = 5.0
    return (deriv, np.outer(weights_line, weights_line).reshape(25))


def split_const(x):
    high = np.asarray(x, np.float32).astype(bf16)
    low = (np.asarray(x, np.float32) - high.astype(np.float32)).astype(bf16)
    return high, low


def derivative_matrices(elements):
    deriv, _ = gll_tables()
    along_s = np.zeros((PTS, PTS))
    along_z = np.zeros((PTS, PTS))
    for e in range(elements):
        base = slice(25 * e, 25 * e + 25)
        along_s[base, base] = np.kron(deriv, np.eye(5))
        along_z[base, base] = np.kron(np.eye(5), deriv)
    both = np.concatenate([along_s, along_z])
    high, low = split_const(both)
    forward = np.concatenate([high, high, low], axis=1)
    high_t, low_t = split_const(both.T)
    return forward, np.concatenate([high_t, low_t], axis=1)


def small_tables(samples, nphi):
    coarse = TABLE_STRIDE * jnp.arange(MAXO // TABLE_STRIDE, dtype=jnp.int32)
    fine = jnp.arange(TABLE_STRIDE, dtype=jnp.int32)
    every = jnp.concatenate([coarse, fine])
    angle = (every[:, None] * samples[None, :] % nphi).astype(f32) * (2.0 * math.pi / nphi)
    both = jnp.stack([jnp.cos(angle), jnp.sin(angle)])
    return both[:, : coarse.shape[0]], both[:, coarse.shape[0] :]


def table_kernel(coarse_ref, fine_ref, out_ref):
    per_step = out_ref.shape[1] // TABLE_STRIDE
    fine_cos, fine_sin = fine_ref[0], fine_ref[1]
    for i in range(per_step):
        a = pl.program_id(0) * per_step + i
        big_cos = coarse_ref[0, pl.ds(a, 1), :]
        big_sin = coarse_ref[1, pl.ds(a, 1), :]
        rows = slice(i * TABLE_STRIDE, (i + 1) * TABLE_STRIDE)
        out_ref[0, rows, :] = (big_cos * fine_cos - big_sin * fine_sin).astype(bf16)
        out_ref[1, rows, :] = (big_sin * fine_cos + big_cos * fine_sin).astype(bf16)


def fourier_table(coarse, fine):
    count = coarse.shape[2]
    block = 4 * TABLE_STRIDE
    return pl.pallas_call(
        table_kernel,
        grid=(MAXO // block,),
        in_specs=[
            pl.BlockSpec(coarse.shape, lambda i: (0, 0, 0)),
            pl.BlockSpec(fine.shape, lambda i: (0, 0, 0)),
        ],
        out_specs=pl.BlockSpec((2, block, count), lambda i: (0, i, 0)),
        out_shape=jax.ShapeDtypeStruct((2, MAXO, count), bf16),
        name="table",
        cost_estimate=pl.CostEstimate(
            flops=6 * MAXO * count, bytes_accessed=4 * MAXO * count, transcendentals=0
        ),
    )(coarse, fine)


def dot(a, b):
    return jnp.dot(a, b, preferred_element_type=f32)


def dot_t(a, b):
    return lax.dot_general(a, b, (((1,), (1,)), ((), ())), preferred_element_type=f32)


def exact_dot(a, b):
    return jnp.dot(a, b, preferred_element_type=f32, precision=lax.Precision.HIGHEST)


def step_kernel(
    place_ref,
    u0_ref,
    u1_ref,
    u2_ref,
    u3_ref,
    kappa_ref,
    fwd_ref,
    table_ref,
    forward_ref,
    backward_ref,
    column_ref,
    sum_rows_ref,
    sum_cols_ref,
    before_ref,
    o0_ref,
    o1_ref,
    o2_ref,
    o3_ref,
    density_ref,
    coeff_ref,
    stress_ref,
):
    count = u0_ref.shape[2]
    samples = kappa_ref.shape[1]
    lane = lax.broadcasted_iota(jnp.int32, (1, count), 1)
    inv_radius = column_ref[:, 0:1]
    quad = column_ref[:, 1:2]
    for shift, u_ref in enumerate((u0_ref, u1_ref, u2_ref, u3_ref)):
        start = pl.multiple_of(place_ref[0, shift], count)
        order = (lane + start).astype(f32)
        u0, u1 = u_ref[0], u_ref[1]
        coeff_ref[:PTS, pl.ds(start, count)] = u0
        coeff_ref[:PTS, pl.ds(MAXO + start, count)] = u1
        coeff_ref[PTS:, pl.ds(start, count)] = (order * u1.astype(f32)).astype(bf16)
        coeff_ref[PTS:, pl.ds(MAXO + start, count)] = (-order * u0.astype(f32)).astype(bf16)
    forward, backward = forward_ref[...], backward_ref[...]
    width = 256
    density = before_ref[...]
    for n in range(samples // width):
        cols = slice(n * width, (n + 1) * width)
        phys = dot(coeff_ref[:, :MAXO], table_ref[0, :, cols]) + dot(
            coeff_ref[:, MAXO:], table_ref[1, :, cols]
        )
        field, around = phys[:PTS], phys[PTS:] * inv_radius
        high = field.astype(bf16)
        low = (field - high.astype(f32)).astype(bf16)
        along = dot(forward, jnp.concatenate([high, low, high]))
        along_s, along_z = along[:PTS], along[PTS:]
        modulus = kappa_ref[:, cols].astype(f32) * quad
        stress = jnp.concatenate([along_s * modulus, along_z * modulus]).astype(bf16)
        stress_ref[:PTS, cols] = dot(backward, jnp.concatenate([stress, stress])).astype(bf16)
        stress_ref[PTS:, cols] = (around * modulus * inv_radius).astype(bf16)
        dens = (
            along_s * fwd_ref[0, :, cols].astype(f32)
            + along_z * fwd_ref[1, :, cols].astype(f32)
            + around * fwd_ref[2, :, cols].astype(f32)
        ) * (quad * kernel_scale)
        by_element = exact_dot(sum_rows_ref[...], dens)
        density = density + exact_dot(by_element, sum_cols_ref[cols, :])
    density_ref[...] = density
    for shift, o_ref in enumerate((o0_ref, o1_ref, o2_ref, o3_ref)):
        start = pl.multiple_of(place_ref[1, shift], count)
        order = (lane + start).astype(f32)
        cosine = dot_t(stress_ref[...], table_ref[0, pl.ds(start, count), :])
        sine = dot_t(stress_ref[...], table_ref[1, pl.ds(start, count), :])
        o_ref[0] = (cosine[:PTS] - order * sine[PTS:]).astype(bf16)
        o_ref[1] = (sine[:PTS] + order * cosine[PTS:]).astype(bf16)


def step_call(place, blocks, kappa, fwd, table, consts, columns, before):
    count = blocks[0].shape[2]
    samples = kappa.shape[1]
    vmem = pl.BlockSpec(memory_space=pltpu.VMEM)
    smem = pl.BlockSpec(memory_space=pltpu.SMEM)
    out_block = jax.ShapeDtypeStruct((2, PTS, count), bf16)
    flops = 2 * 2 * 2 * PTS * 2 * MAXO * samples
    return pl.pallas_call(
        step_kernel,
        in_specs=[smem] + [vmem] * 13,
        out_specs=[vmem] * 5,
        out_shape=[out_block] * 4 + [jax.ShapeDtypeStruct(before.shape, f32)],
        scratch_shapes=[
            pltpu.VMEM((2 * PTS, 2 * MAXO), bf16),
            pltpu.VMEM((2 * PTS, samples), bf16),
        ],
        name="step",
        compiler_params=pltpu.CompilerParams(vmem_limit_bytes=40 * 1024 * 1024),
        cost_estimate=pl.CostEstimate(
            flops=flops, bytes_accessed=4 * MAXO * samples, transcendentals=0
        ),
    )(place, *blocks, kappa, fwd, table, consts[0], consts[1], columns, consts[2], consts[3], before)


def gather_rows_kernel(nodes_ref, a_ref, b_ref, c_ref, d_ref, force_ref, left_ref, right_ref):
    force_ref[...] = (
        a_ref[...].astype(f32) + b_ref[...].astype(f32) + c_ref[...].astype(f32) + d_ref[...].astype(f32)
    )
    for side, o_ref in enumerate((left_ref, right_ref)):
        for k in range(nodes_ref.shape[1]):
            row = nodes_ref[side, k]
            for c in range(2):
                o_ref[c, k : k + 1, :] = force_ref[c, pl.ds(row, 1), :]


def gather_rows(nodes, parts):
    vmem = pl.BlockSpec(memory_space=pltpu.VMEM)
    smem = pl.BlockSpec(memory_space=pltpu.SMEM)
    count = parts[0].shape[2]
    rows = jax.ShapeDtypeStruct((2, nodes.shape[1], count), f32)
    return pl.pallas_call(
        gather_rows_kernel,
        in_specs=[smem] + [vmem] * 4,
        out_specs=[vmem] * 3,
        out_shape=[jax.ShapeDtypeStruct((2, PTS, count), f32), rows, rows],
        name="rows",
    )(nodes, *parts)


def update_kernel(
    nodes_ref, place_ref, force_ref, before_ref, after_ref, now_ref, prev_ref, column_ref, next_ref, send_ref, total_ref
):
    total_ref[...] = force_ref[...]
    for side, r_ref in enumerate((before_ref, after_ref)):
        for k in range(nodes_ref.shape[1]):
            row = nodes_ref[side, k]
            for c in range(2):
                total_ref[c, pl.ds(row, 1), :] += r_ref[c, k : k + 1, :]
    shape = total_ref.shape[1:]
    order = lax.broadcasted_iota(jnp.int32, shape, 1) + place_ref[0, 0]
    level = column_ref[:, 2:3]
    scale = column_ref[:, 3:4]
    inside = order.astype(f32) < level
    first = order == 0
    for c in range(2):
        gain = jnp.where(first, scale * (0.5 if c == 0 else 0.0), scale)
        gain = jnp.where(inside, gain, 0.0)
        value = 2.0 * now_ref[c] - prev_ref[c] - gain * total_ref[c]
        next_ref[c] = value
        send_ref[c] = value.astype(bf16)


def update(nodes, place, force, before, after, now, prev, columns):
    vmem = pl.BlockSpec(memory_space=pltpu.VMEM)
    smem = pl.BlockSpec(memory_space=pltpu.SMEM)
    return pl.pallas_call(
        update_kernel,
        in_specs=[smem, smem] + [vmem] * 6,
        out_specs=[vmem] * 2,
        out_shape=[jax.ShapeDtypeStruct(force.shape, f32), jax.ShapeDtypeStruct(force.shape, bf16)],
        scratch_shapes=[pltpu.VMEM(force.shape, f32)],
        name="update",
    )(nodes, place, force, before, after, now, prev, columns)


def owners_kernel(first_ref, rows_ref, out_ref):
    regions, sectors = out_ref.shape
    ids = rows_ref[:, sectors : sectors + 1]
    mine = lax.broadcasted_iota(jnp.int32, (rows_ref.shape[0], regions), 1) + first_ref[0, 0]
    chosen = jnp.where(ids == mine.astype(f32), 1.0, 0.0)
    out_ref[...] = lax.dot_general(
        chosen,
        rows_ref[:, :sectors],
        (((0,), (0,)), ((), ())),
        preferred_element_type=f32,
        precision=lax.Precision.HIGHEST,
    )


def owners(first, rows, regions, sectors):
    return pl.pallas_call(
        owners_kernel,
        in_specs=[pl.BlockSpec(memory_space=pltpu.SMEM), pl.BlockSpec(memory_space=pltpu.VMEM)],
        out_specs=pl.BlockSpec(memory_space=pltpu.VMEM),
        out_shape=jax.ShapeDtypeStruct((regions, sectors), f32),
        name="owners",
    )(first, rows)


def turned(x, by):
    devices = lax.axis_size("blk")
    return lax.ppermute(x, "blk", [(i, (i + by) % devices) for i in range(devices)])


def shifted(x, by):
    devices = lax.axis_size("mer")
    pairs = [(i, i + by) for i in range(devices) if 0 <= i + by < devices]
    return lax.ppermute(x, "mer", pairs)


def everyone(x):
    devices = lax.axis_size("mer")
    x_bits = [8, 16, 32, 2, 4, 1]
    assert devices == 64
    for bit in x_bits:
        other = lax.ppermute(x, "mer", [(i, i ^ bit) for i in range(devices)])
        x = jnp.concatenate([x, other])
    return x


def local(disp_now, disp_prev, kappa, radius, fwd_strain, order_bucket, shared_nodes, region_map):
    points, _, count = disp_now.shape
    elements = order_bucket.shape[0]
    samp_count = kappa.shape[1]
    nphi = 2 * MAXO
    sectors = samp_count // 4
    regions = 4096 // lax.axis_size("mer")
    blk = lax.axis_index("blk")
    mer = lax.axis_index("mer")
    pad = PTS - points

    levels = jnp.zeros(order_bucket.shape, jnp.int32)
    for position, value in enumerate(bucket_orders):
        levels = levels + jnp.where(order_bucket == position, value, 0).astype(jnp.int32)
    levels = jnp.repeat(levels, 25)
    orders = blk * count + jnp.arange(count, dtype=jnp.int32)
    cosine_part = orders[None, :] < levels[:, None]
    mask = jnp.stack([cosine_part, cosine_part & (orders[None, :] >= 1)])

    def arranged(disp):
        return jnp.pad(jnp.where(mask, disp.transpose(1, 0, 2), 0.0), ((0, 0), (0, pad), (0, 0)))

    current = arranged(disp_now)
    previous = arranged(disp_prev)
    send = current.astype(bf16)

    _, gllw = gll_tables()
    weight = jnp.tile(jnp.asarray(gllw, f32), elements) * radius
    columns = jnp.stack(
        [
            1.0 / radius,
            weight * (2.0 * math.pi / nphi),
            levels.astype(f32),
            time_step_sq / (weight * math.pi),
        ],
        axis=1,
    )
    columns = jnp.pad(columns, ((0, pad), (0, 0)))
    table = fourier_table(*small_tables(blk * samp_count + jnp.arange(samp_count, dtype=jnp.int32), nphi))
    kappa = jnp.pad(kappa, ((0, pad), (0, 0)))
    fwd = jnp.pad(fwd_strain, ((0, 0), (0, 0), (0, pad), (0, 0)))
    forward, backward = derivative_matrices(elements)
    sum_rows = np.zeros((ELEM_ROWS, PTS), np.float32)
    for e in range(elements):
        sum_rows[e, 25 * e : 25 * e + 25] = 1.0
    sum_cols = np.kron(np.eye(sectors), np.ones((4, 1))).astype(np.float32)
    consts = tuple(jnp.asarray(x) for x in (forward, backward, sum_rows, sum_cols))
    shifts = (0, 1, 3, 2)
    nblk = lax.axis_size("blk")
    place = jnp.stack(
        [
            jnp.stack([(blk - s) % nblk * count for s in shifts]),
            jnp.stack([(blk + s) % nblk * count for s in shifts]),
        ]
    ).astype(jnp.int32)
    nodes = shared_nodes[0]
    density = jnp.zeros((ELEM_ROWS, sectors), f32)
    for section in range(STEPS):
        blocks = [send] + [turned(send, s) for s in shifts[1:]]
        *forces, density = step_call(place, blocks, kappa, fwd[section], table, consts, columns, density)
        parts = [forces[0]] + [turned(x, s) for x, s in zip(forces[1:], shifts[1:])]
        force, left, right = gather_rows(nodes, parts)
        from_next = shifted(left, -1)
        from_before = shifted(right, 1)
        following, send = update(nodes, place, force, from_before, from_next, current, previous, columns)
        current, previous = following, current
    ids = jnp.pad(region_map.astype(f32), (0, ELEM_ROWS - elements), constant_values=-1.0)
    rows = jnp.concatenate([density, jnp.broadcast_to(ids[:, None], (ELEM_ROWS, 128))], axis=1)
    first = (mer * regions).astype(jnp.int32).reshape(1, 1)
    kernel = owners(first, everyone(rows), regions, sectors)
    displacement = current[:, :points].transpose(1, 0, 2)
    return (displacement, kernel)


def solution(mesh):
    in_specs = (
        P("mer", None, "blk"),
        P("mer", None, "blk"),
        P("mer", "blk"),
        P("mer"),
        P(None, None, "mer", "blk"),
        P("mer"),
        P("mer", None, None),
        P("mer"),
    )
    out_specs = (P("mer", None, "blk"), P("mer", "blk"))
    return jax.shard_map(local, mesh=mesh, in_specs=in_specs, out_specs=out_specs, check_vma=False)
```

time: 440 us -> 162 us (0.37)
  the two profiles are of different devices: /device:TPU:1 before, /device:TPU:103 now
where the time goes in v1:
time: 162 us
  starting transfers between devices  48.6 us (30%)
  waiting for transfers between devices  43.8 us (27%)
  Pallas kernels  40 us (25%)
  local copies, waits for them, and re-layouts  21.8 us (13%)
  other arithmetic  6.46 us (4%)
    ppermute x4, starting transfers between devices, shifted(): return lax.ppermute(x, 'mer', pairs)  24.3 us
    pallas_call x2, Pallas kernels, step_call(): pl.pallas_call(step_kernel, in_specs=[smem] + [vmem] * 13, out_specs=[vme...  21.6 us
    ppermute x12, waiting for transfers between devices, turned(): lax.ppermute(x, 'blk', [(i, (i + by) % devices) for i in range(devices)])  17 us
    ppermute x6, waiting for transfers between devices, everyone(): other = lax.ppermute(x, 'mer', [(i, i ^ bit) for i in range(devices)])  15.9 us
    unnamed x68, local copies, waits for them, and re-layouts  15.7 us
    ppermute x12, starting transfers between devices, turned(): lax.ppermute(x, 'blk', [(i, (i + by) % devices) for i in range(devices)])  14.7 us
    ppermute x4, waiting for transfers between devices, shifted(): return lax.ppermute(x, 'mer', pairs)  10.9 us
    ppermute x6, starting transfers between devices, everyone(): other = lax.ppermute(x, 'mer', [(i, i ^ bit) for i in range(devices)])  9.65 us
  transfers between devices with their start and end apart: 22, of which 12 were waited for; matrix products, arithmetic and copies ran while one was open for 7% of the time, Pallas kernels for 7%

profile of v1, /device:TPU:103, one launch (start us, length us, event | category | flops | bytes accessed | tf_op | source)
XLA Modules:
  0.0 161.8 jit_solution(10139825831507590426)
XLA Ops:
  1.6 2.3 %bitcast_select_fusion = (f32[2,125,512]{2,1,0:T(8,128)}, f32[2,125,512]{2,1,0:T(8,128)S(1)}) fusion(f32[125,2,512]{2,1,0:T(2,128)} %param.14, pred[1,125,512]{2,1,0:T(8,128)(4,1)S(1)} %get-tuple-element.71, pred[1,125,512]{2,1,0:T(8,128)(4,1)S(1)} %get-tuple-element.70, f32[125,2,512]{2,1,0:T(2,128)} %param.13), kind=kLoop, calls=%fused_computation.10 | loop fusion | flops 384000 | bytes 2176000 | tf_op jit(solution)/shard_map/jit(_where)/select_n | solution.py:337
  5.3 2.1 %collective-permute-start.1 = (bf16[2,128,512]{2,1,0:T(8,128)(2,1)S(1)}, bf16[2,128,512]{2,1,0:T(8,128)(2,1)S(1)}, u32[]{:S(2)}, u32[]{:S(2)}) collective-permute-start(bf16[2,128,512]{2,1,0:T(8,128)(2,1)S(1)} %pad.136.u0_ref), channel_id=1, source_target_pairs={{0,3},{1,0},{2,1},{3,2},{4,7},{5,4},{6,5},{7,6},{8,11},{9,8},{10,9... | collective-permute-start | bytes 786440 | tf_op jit(solution)/shard_map/ppermute | solution.py:298
  13.7 6.6 %table.1.table_ref = bf16[2,2048,1024]{2,1,0:T(8,128)(2,1)} custom-call(f32[2,32,1024]{2,1,0:T(8,128)} %pad_maximum_fusion.1.coarse_ref, f32[2,64,1024]{2,1,0:T(8,128)} %pad_maximum_fusion.fine_ref), custom_call_target="tpu_custom_call" | custom-call | flops 12582912 | bytes 8388608 | tf_op jit(solution)/shard_map/table/pallas_call | solution.py:89
  20.5 1.6 %fusion.1 = (bf16[3,128,1024]{2,1,0:T(8,128)(2,1)S(1)}, bf16[3,128,1024]{2,1,0:T(8,128)(2,1)S(1)}) fusion(bf16[2,3,125,1024]{3,2,1,0:T(8,128)(2,1)} %copy.24), kind=kLoop, calls=%fused_computation.3 | loop fusion | bytes 3108864 | tf_op jit(solution)/shard_map/squeeze | solution.py:376
  22.2 3.4 %copy-done = bf16[2,2048,1024]{2,1,0:T(8,128)(2,1)S(1)} copy-done((bf16[2,2048,1024]{2,1,0:T(8,128)(2,1)S(1)}, bf16[2,2048,1024]{2,1,0:T(8,128)(2,1)}, u32[]{:S(2)}) %copy-start) | copy-done | bytes 8388632
  25.6 10.8 %step.2 = (bf16[2,128,512]{2,1,0:T(8,128)(2,1)S(1)}, bf16[2,128,512]{2,1,0:T(8,128)(2,1)S(1)}, bf16[2,128,512]{2,1,0:T(8,128)(2,1)S(1)}, bf16[2,128,512]{2,1,0:T(8,128)(2,1)S(1)}, f32[8,256]{1,0:T(8,128)S(1)}) custom-call(s32[2,4]{1,0:T(2,128)S(1)} %pad_add_fusion.1.place_ref, bf16[2,128,512]{2,1,0:T(8,128)(2,1)S(1)} %pad.136.u0_ref, ...), custom_call_target="tpu_custom_call" | custom-call | flops 4294967296 | bytes 8388608 | tf_op jit(solution)/shard_map/step/pallas_call | solution.py:194
  37.5 2.3 %collective-permute-start.4 = (bf16[2,128,512]{2,1,0:T(8,128)(2,1)S(1)}, bf16[2,128,512]{2,1,0:T(8,128)(2,1)S(1)}, u32[]{:S(2)}, u32[]{:S(2)}) collective-permute-start(bf16[2,128,512]{2,1,0:T(8,128)(2,1)S(1)} %get-tuple-element.23), channel_id=1, source_target_pairs={{0,3},{1,0},{2,1},{3,2},{4,7},{5,4},{6,5},{7,6},{8,11},{9,8},{10,9... | collective-permute-start | bytes 786440 | tf_op jit(solution)/shard_map/ppermute | solution.py:298
  40.6 4.6 %collective-permute-done.3.b_ref = bf16[2,128,512]{2,1,0:T(8,128)(2,1)S(1)} collective-permute-done((bf16[2,128,512]{2,1,0:T(8,128)(2,1)S(1)}, bf16[2,128,512]{2,1,0:T(8,128)(2,1)S(1)}, u32[]{:S(2)}, u32[]{:S(2)}) %collective-permute-start.3) | collective-permute-done | bytes 262176 | tf_op jit(solution)/shard_map/ppermute | solution.py:298
  45.2 4.6 %collective-permute-done.5.d_ref = bf16[2,128,512]{2,1,0:T(8,128)(2,1)S(1)} collective-permute-done((bf16[2,128,512]{2,1,0:T(8,128)(2,1)S(1)}, bf16[2,128,512]{2,1,0:T(8,128)(2,1)S(1)}, u32[]{:S(2)}, u32[]{:S(2)}) %collective-permute-start.5) | collective-permute-done | bytes 262176 | tf_op jit(solution)/shard_map/ppermute | solution.py:298
  50.4 2.3 %rows.2 = (f32[2,128,512]{2,1,0:T(8,128)}, f32[2,5,512]{2,1,0:T(8,128)}, f32[2,5,512]{2,1,0:T(8,128)}) custom-call(s32[2,5]{1,0:T(2,128)} %bitcast.29, bf16[2,128,512]{2,1,0:T(8,128)(2,1)} %copy-done.5, bf16[2,128,512]{2,1,0:T(8,128)(2,1)} %copy-done.20, bf16[2,128,512]{2,1,0:T(8,128)(2,1)} %copy-done.21, bf16[2,128,512]{2,1,0:T(8,128)(2,1)} %copy-done.22), custom_call_target="tpu_custom_call" | custom-call | tf_op jit(solution)/shard_map/rows/pallas_call | solution.py:227
  52.7 8.2 %collective-permute-start.6 = (f32[2,5,512]{2,1,0:T(8,128)}, f32[2,5,512]{2,1,0:T(8,128)S(1)}, u32[]{:S(2)}, u32[]{:S(2)}) collective-permute-start(f32[2,5,512]{2,1,0:T(8,128)} %get-tuple-element.26), channel_id=1, source_target_pairs={{0,4},{4,8},{8,12},{12,16},{16,20},{20,24},{24,28},{28,32},{32,36}... | collective-permute-start | bytes 61448 | tf_op jit(solution)/shard_map/ppermute | solution.py:304
  60.9 1.9 %collective-permute-start.7 = (f32[2,5,512]{2,1,0:T(8,128)}, f32[2,5,512]{2,1,0:T(8,128)S(1)}, u32[]{:S(2)}, u32[]{:S(2)}) collective-permute-start(f32[2,5,512]{2,1,0:T(8,128)} %get-tuple-element.27), channel_id=1, source_target_pairs={{4,0},{8,4},{12,8},{16,12},{20,16},{24,20},{28,24},{32,28},{36,32}... | collective-permute-start | bytes 61448 | tf_op jit(solution)/shard_map/ppermute | solution.py:304
  62.8 1.9 %pad.23.now_ref.prev_ref = f32[2,128,512]{2,1,0:T(8,128)} pad(f32[2,125,512]{2,1,0:T(8,128)} %copy-done.13, f32[]{:T(128)} %constant.105.clone.1), padding=0_0x0_3x0_0 | pad | bytes 1036292 | tf_op jit(solution)/shard_map/jit(_pad)/pad | solution.py:337
  65.6 4.1 %collective-permute-done.7.after_ref = f32[2,5,512]{2,1,0:T(8,128)S(1)} collective-permute-done((f32[2,5,512]{2,1,0:T(8,128)}, f32[2,5,512]{2,1,0:T(8,128)S(1)}, u32[]{:S(2)}, u32[]{:S(2)}) %collective-permute-start.7) | collective-permute-done | bytes 20512 | tf_op jit(solution)/shard_map/ppermute | solution.py:304
  70.3 2.5 %update.2 = (f32[2,128,512]{2,1,0:T(8,128)}, bf16[2,128,512]{2,1,0:T(8,128)(2,1)}) custom-call(s32[2,5]{1,0:T(2,128)} %bitcast.30, s32[2,4]{1,0:T(2,128)} %copy-done.6, f32[2,128,512]{2,1,0:T(8,128)} %get-tuple-element.25.force_ref, f32[2,5,512]{2,1,0:T(8,128)} %copy-done.26, f32[2,5,512]{2,1,0:T(8,128)} %copy-done.27, f32[2,128,512]{2,1,0:T(8,128)} %pad.23.now_ref.prev_ref, ...), custom_call_target="tpu_custom_call" | custom-call | tf_op jit(solution)/shard_map/update/pallas_call | solution.py:262
  72.8 2.7 %collective-permute-start.9 = (bf16[2,128,512]{2,1,0:T(8,128)(2,1)}, bf16[2,128,512]{2,1,0:T(8,128)(2,1)S(1)}, u32[]{:S(2)}, u32[]{:S(2)}) collective-permute-start(bf16[2,128,512]{2,1,0:T(8,128)(2,1)} %get-tuple-element.28.u0_ref), channel_id=1, source_target_pairs={{0,3},{1,0},{2,1},{3,2},{4,7},{5,4},{6,5},{7,6},{8,11},{9,8},{10,9... | collective-permute-start | bytes 786440 | tf_op jit(solution)/shard_map/ppermute | solution.py:298
  76.6 5.0 %collective-permute-done.8.u1_ref = bf16[2,128,512]{2,1,0:T(8,128)(2,1)S(1)} collective-permute-done((bf16[2,128,512]{2,1,0:T(8,128)(2,1)}, bf16[2,128,512]{2,1,0:T(8,128)(2,1)S(1)}, u32[]{:S(2)}, u32[]{:S(2)}) %collective-permute-start.8) | collective-permute-done | bytes 262176 | tf_op jit(solution)/shard_map/ppermute | solution.py:298
  84.5 3.4 %copy-done.1 = bf16[2,2048,1024]{2,1,0:T(8,128)(2,1)S(1)} copy-done((bf16[2,2048,1024]{2,1,0:T(8,128)(2,1)S(1)}, bf16[2,2048,1024]{2,1,0:T(8,128)(2,1)}, u32[]{:S(2)}) %copy-start.1) | copy-done | bytes 8388632
  88.8 10.8 %step.3 = (bf16[2,128,512]{2,1,0:T(8,128)(2,1)S(1)}, bf16[2,128,512]{2,1,0:T(8,128)(2,1)S(1)}, bf16[2,128,512]{2,1,0:T(8,128)(2,1)S(1)}, bf16[2,128,512]{2,1,0:T(8,128)(2,1)S(1)}, f32[8,256]{1,0:T(8,128)S(1)}) custom-call(s32[2,4]{1,0:T(2,128)S(1)} %copy-done.7, bf16[2,128,512]{2,1,0:T(8,128)(2,1)S(1)} %copy-done.8, ...), custom_call_target="tpu_custom_call" | custom-call | flops 4294967296 | bytes 8388608 | tf_op jit(solution)/shard_map/step/pallas_call | solution.py:194
  100.4 2.5 %collective-permute-done.16 = f32[8,384]{1,0:T(8,128)S(1)} collective-permute-done((f32[8,384]{1,0:T(8,128)S(1)}, f32[8,384]{1,0:T(8,128)S(1)}, u32[]{:S(2)}, u32[]{:S(2)}) %collective-permute-start.16) | collective-permute-done | bytes 12320 | tf_op jit(solution)/shard_map/ppermute | solution.py:312
  102.9 3.7 %collective-permute-done.17 = f32[16,384]{1,0:T(8,128)S(1)} collective-permute-done((f32[16,384]{1,0:T(8,128)S(1)}, f32[16,384]{1,0:T(8,128)S(1)}, u32[]{:S(2)}, u32[]{:S(2)}) %collective-permute-start.17) | collective-permute-done | bytes 24608 | tf_op jit(solution)/shard_map/ppermute | solution.py:312
  106.7 3.3 %collective-permute-start.18 = (f32[32,384]{1,0:T(8,128)S(1)}, f32[32,384]{1,0:T(8,128)S(1)}, u32[]{:S(2)}, u32[]{:S(2)}) collective-permute-start(f32[32,384]{1,0:T(8,128)S(1)} %pad_maximum_fusion.3), channel_id=1, source_target_pairs={{0,128},{4,132},{8,136},{12,140},{16,144},{20,148},{24,152},{28,15... | collective-permute-start | bytes 147464 | tf_op jit(solution)/shard_map/ppermute | solution.py:312
  110.0 3.8 %collective-permute-done.18 = f32[32,384]{1,0:T(8,128)S(1)} collective-permute-done((f32[32,384]{1,0:T(8,128)S(1)}, f32[32,384]{1,0:T(8,128)S(1)}, u32[]{:S(2)}, u32[]{:S(2)}) %collective-permute-start.18) | collective-permute-done | bytes 49184 | tf_op jit(solution)/shard_map/ppermute | solution.py:312
  113.9 3.4 %collective-permute-done.19 = f32[64,384]{1,0:T(8,128)S(1)} collective-permute-done((f32[64,384]{1,0:T(8,128)S(1)}, f32[64,384]{1,0:T(8,128)S(1)}, u32[]{:S(2)}, u32[]{:S(2)}) %collective-permute-start.19) | collective-permute-done | bytes 98336 | tf_op jit(solution)/shard_map/ppermute | solution.py:312
  121.3 2.4 %collective-permute-done.20 = f32[128,384]{1,0:T(8,128)S(1)} collective-permute-done((f32[128,384]{1,0:T(8,128)S(1)}, f32[128,384]{1,0:T(8,128)S(1)}, u32[]{:S(2)}, u32[]{:S(2)}) %collective-permute-start.20) | collective-permute-done | bytes 196640 | tf_op jit(solution)/shard_map/ppermute | solution.py:312
  123.8 5.3 %collective-permute-start.21 = (f32[256,384]{1,0:T(8,128)S(1)}, f32[256,384]{1,0:T(8,128)S(1)}, u32[]{:S(2)}, u32[]{:S(2)}) collective-permute-start(f32[256,384]{1,0:T(8,128)S(1)} %get-tuple-element.48), channel_id=1, source_target_pairs={{0,4},{4,0},{8,12},{12,8},{16,20},{20,16},{24,28},{28,24},{32,36},... | collective-permute-start | bytes 1179656 | tf_op jit(solution)/shard_map/ppermute | solution.py:312
  129.9 2.2 %rows.3 = (f32[2,128,512]{2,1,0:T(8,128)}, f32[2,5,512]{2,1,0:T(8,128)}, f32[2,5,512]{2,1,0:T(8,128)}) custom-call(s32[2,5]{1,0:T(2,128)} %bitcast.31, bf16[2,128,512]{2,1,0:T(8,128)(2,1)} %copy-done.4, bf16[2,128,512]{2,1,0:T(8,128)(2,1)} %copy-done.17, bf16[2,128,512]{2,1,0:T(8,128)(2,1)} %copy-done.18, bf16[2,128,512]{2,1,0:T(8,128)(2,1)} %copy-done.19), custom_call_target="tpu_custom_call" | custom-call | tf_op jit(solution)/shard_map/rows/pallas_call | solution.py:227
  132.2 12.2 %collective-permute-start.14 = (f32[2,5,512]{2,1,0:T(8,128)}, f32[2,5,512]{2,1,0:T(8,128)S(1)}, u32[]{:S(2)}, u32[]{:S(2)}) collective-permute-start(f32[2,5,512]{2,1,0:T(8,128)} %get-tuple-element.35), channel_id=1, source_target_pairs={{0,4},{4,8},{8,12},{12,16},{16,20},{20,24},{24,28},{28,32},{32,36}... | collective-permute-start | bytes 61448 | tf_op jit(solution)/shard_map/ppermute | solution.py:304
  144.4 1.9 %collective-permute-start.15 = (f32[2,5,512]{2,1,0:T(8,128)}, f32[2,5,512]{2,1,0:T(8,128)S(1)}, u32[]{:S(2)}, u32[]{:S(2)}) collective-permute-start(f32[2,5,512]{2,1,0:T(8,128)} %get-tuple-element.36), channel_id=1, source_target_pairs={{4,0},{8,4},{12,8},{16,12},{20,16},{24,20},{28,24},{32,28},{36,32}... | collective-permute-start | bytes 61448 | tf_op jit(solution)/shard_map/ppermute | solution.py:304
  146.3 6.8 %collective-permute-done.15.after_ref = f32[2,5,512]{2,1,0:T(8,128)S(1)} collective-permute-done((f32[2,5,512]{2,1,0:T(8,128)}, f32[2,5,512]{2,1,0:T(8,128)S(1)}, u32[]{:S(2)}, u32[]{:S(2)}) %collective-permute-start.15) | collective-permute-done | bytes 20512 | tf_op jit(solution)/shard_map/ppermute | solution.py:304
  153.8 2.5 %update.3 = (f32[2,128,512]{2,1,0:T(8,128)}, bf16[2,128,512]{2,1,0:T(8,128)(2,1)}) custom-call(s32[2,5]{1,0:T(2,128)} %bitcast.32, s32[2,4]{1,0:T(2,128)} %copy-done.6, f32[2,128,512]{2,1,0:T(8,128)} %get-tuple-element.34.force_ref, f32[2,5,512]{2,1,0:T(8,128)} %copy-done.24, f32[2,5,512]{2,1,0:T(8,128)} %copy-done.25, ...), custom_call_target="tpu_custom_call" | custom-call | tf_op jit(solution)/shard_map/update/pallas_call | solution.py:262
  159.5 2.3 %owners.1 = f32[64,256]{1,0:T(8,128)} custom-call(s32[1,1]{1,0:T(1,128)} %bitcast.18.first_ref, f32[512,384]{1,0:T(8,128)} %copy-done.16), custom_call_target="tpu_custom_call" | custom-call | tf_op jit(solution)/shard_map/owners/pallas_call | solution.py:287
  (128 shorter events, 27.3 us)
Async XLA Ops:
  3.9 18.2 %collective-permute-start = (bf16[2,128,512]{2,1,0:T(8,128)(2,1)S(1)}, bf16[2,128,512]{2,1,0:T(8,128)(2,1)S(1)}, u32[]{:S(2)}, u32[]{:S(2)}) collective-permute-start(bf16[2,128,512]{2,1,0:T(8,128)(2,1)S(1)} %pad.136.u0_ref), channel_id=1, source_target_pairs={{0,1},{1,2},{2,3},{3,0},{4,5},{5,6},{6,7},{7,4},{8,9},{9,10},{10,1... | collective-permute-start | bytes 786440 | tf_op jit(solution)/shard_map/ppermute | solution.py:298
  5.3 16.8 %collective-permute-start.1 = (bf16[2,128,512]{2,1,0:T(8,128)(2,1)S(1)}, bf16[2,128,512]{2,1,0:T(8,128)(2,1)S(1)}, u32[]{:S(2)}, u32[]{:S(2)}) collective-permute-start(bf16[2,128,512]{2,1,0:T(8,128)(2,1)S(1)} %pad.136.u0_ref), channel_id=1, source_target_pairs={{0,3},{1,0},{2,1},{3,2},{4,7},{5,4},{6,5},{7,6},{8,11},{9,8},{10,9... | collective-permute-start | bytes 786440 | tf_op jit(solution)/shard_map/ppermute | solution.py:298
  7.4 14.8 %collective-permute-start.2 = (bf16[2,128,512]{2,1,0:T(8,128)(2,1)S(1)}, bf16[2,128,512]{2,1,0:T(8,128)(2,1)S(1)}, u32[]{:S(2)}, u32[]{:S(2)}) collective-permute-start(bf16[2,128,512]{2,1,0:T(8,128)(2,1)S(1)} %pad.136.u0_ref), channel_id=1, source_target_pairs={{0,2},{1,3},{2,0},{3,1},{4,6},{5,7},{6,4},{7,5},{8,10},{9,11},{10,... | collective-permute-start | bytes 786440 | tf_op jit(solution)/shard_map/ppermute | solution.py:298
  13.7 8.5 %copy-start.2 = (f32[128,4]{1,0:T(8,128)}, f32[128,4]{1,0:T(8,128)S(1)}, u32[]{:S(2)}) copy-start(f32[128,4]{1,0:T(8,128)S(1)} %pad.26.column_ref) | copy-start | bytes 6148
  37.1 27.6 %copy-start.14 = (f32[2,125,512]{2,1,0:T(8,128)S(1)}, f32[2,125,512]{2,1,0:T(8,128)}, u32[]{:S(2)}) copy-start(f32[2,125,512]{2,1,0:T(8,128)} %get-tuple-element.50) | copy-start | bytes 1536004
  37.1 8.0 %collective-permute-start.3 = (bf16[2,128,512]{2,1,0:T(8,128)(2,1)S(1)}, bf16[2,128,512]{2,1,0:T(8,128)(2,1)S(1)}, u32[]{:S(2)}, u32[]{:S(2)}) collective-permute-start(bf16[2,128,512]{2,1,0:T(8,128)(2,1)S(1)} %get-tuple-element.22), channel_id=1, source_target_pairs={{0,1},{1,2},{2,3},{3,0},{4,5},{5,6},{6,7},{7,4},{8,9},{9,10},{10,1... | collective-permute-start | bytes 786440 | tf_op jit(solution)/shard_map/ppermute | solution.py:298
  37.5 7.6 %collective-permute-start.4 = (bf16[2,128,512]{2,1,0:T(8,128)(2,1)S(1)}, bf16[2,128,512]{2,1,0:T(8,128)(2,1)S(1)}, u32[]{:S(2)}, u32[]{:S(2)}) collective-permute-start(bf16[2,128,512]{2,1,0:T(8,128)(2,1)S(1)} %get-tuple-element.23), channel_id=1, source_target_pairs={{0,3},{1,0},{2,1},{3,2},{4,7},{5,4},{6,5},{7,6},{8,11},{9,8},{10,9... | collective-permute-start | bytes 786440 | tf_op jit(solution)/shard_map/ppermute | solution.py:298
  39.8 9.9 %collective-permute-start.5 = (bf16[2,128,512]{2,1,0:T(8,128)(2,1)S(1)}, bf16[2,128,512]{2,1,0:T(8,128)(2,1)S(1)}, u32[]{:S(2)}, u32[]{:S(2)}) collective-permute-start(bf16[2,128,512]{2,1,0:T(8,128)(2,1)S(1)} %get-tuple-element.24), channel_id=1, source_target_pairs={{0,2},{1,3},{2,0},{3,1},{4,6},{5,7},{6,4},{7,5},{8,10},{9,11},{10,... | collective-permute-start | bytes 786440 | tf_op jit(solution)/shard_map/ppermute | solution.py:298
  45.1 5.3 %copy-start.20 = (bf16[2,128,512]{2,1,0:T(8,128)(2,1)}, bf16[2,128,512]{2,1,0:T(8,128)(2,1)S(1)}, u32[]{:S(2)}) copy-start(bf16[2,128,512]{2,1,0:T(8,128)(2,1)S(1)} %collective-permute-done.3.b_ref) | copy-start | bytes 786436
  45.2 4.6 %copy-start.21 = (bf16[2,128,512]{2,1,0:T(8,128)(2,1)}, bf16[2,128,512]{2,1,0:T(8,128)(2,1)S(1)}, u32[]{:S(2)}) copy-start(bf16[2,128,512]{2,1,0:T(8,128)(2,1)S(1)} %collective-permute-done.4.c_ref) | copy-start | bytes 786436
  52.7 12.9 %collective-permute-start.6 = (f32[2,5,512]{2,1,0:T(8,128)}, f32[2,5,512]{2,1,0:T(8,128)S(1)}, u32[]{:S(2)}, u32[]{:S(2)}) collective-permute-start(f32[2,5,512]{2,1,0:T(8,128)} %get-tuple-element.26), channel_id=1, source_target_pairs={{0,4},{4,8},{8,12},{12,16},{16,20},{20,24},{24,28},{28,32},{32,36}... | collective-permute-start | bytes 61448 | tf_op jit(solution)/shard_map/ppermute | solution.py:304
  60.9 8.8 %collective-permute-start.7 = (f32[2,5,512]{2,1,0:T(8,128)}, f32[2,5,512]{2,1,0:T(8,128)S(1)}, u32[]{:S(2)}, u32[]{:S(2)}) collective-permute-start(f32[2,5,512]{2,1,0:T(8,128)} %get-tuple-element.27), channel_id=1, source_target_pairs={{4,0},{8,4},{12,8},{16,12},{20,16},{24,20},{28,24},{32,28},{36,32}... | collective-permute-start | bytes 61448 | tf_op jit(solution)/shard_map/ppermute | solution.py:304
  64.7 11.9 %copy-start.30 = (s32[5]{0:T(128)S(1)}, s32[5]{0:T(128)}, u32[]{:S(2)}) copy-start(s32[5]{0:T(128)} %param.20) | copy-start | bytes 64
  64.7 19.7 %copy-start.3 = (f32[128,4]{1,0:T(8,128)S(1)}, f32[128,4]{1,0:T(8,128)}, u32[]{:S(2)}) copy-start(f32[128,4]{1,0:T(8,128)} %copy-done.2) | copy-start | bytes 6148
  64.7 19.7 %copy-start.7 = (s32[2,4]{1,0:T(2,128)S(1)}, s32[2,4]{1,0:T(2,128)}, u32[]{:S(2)}) copy-start(s32[2,4]{1,0:T(2,128)} %copy-done.6) | copy-start | bytes 100
  65.6 4.1 %copy-start.26 = (f32[2,5,512]{2,1,0:T(8,128)}, f32[2,5,512]{2,1,0:T(8,128)S(1)}, u32[]{:S(2)}) copy-start(f32[2,5,512]{2,1,0:T(8,128)S(1)} %collective-permute-done.6.before_ref) | copy-start | bytes 61444
  72.8 8.9 %collective-permute-start.8 = (bf16[2,128,512]{2,1,0:T(8,128)(2,1)}, bf16[2,128,512]{2,1,0:T(8,128)(2,1)S(1)}, u32[]{:S(2)}, u32[]{:S(2)}) collective-permute-start(bf16[2,128,512]{2,1,0:T(8,128)(2,1)} %get-tuple-element.28.u0_ref), channel_id=1, source_target_pairs={{0,1},{1,2},{2,3},{3,0},{4,5},{5,6},{6,7},{7,4},{8,9},{9,10},{10,1... | collective-permute-start | bytes 786440 | tf_op jit(solution)/shard_map/ppermute | solution.py:298
  72.8 10.5 %collective-permute-start.9 = (bf16[2,128,512]{2,1,0:T(8,128)(2,1)}, bf16[2,128,512]{2,1,0:T(8,128)(2,1)S(1)}, u32[]{:S(2)}, u32[]{:S(2)}) collective-permute-start(bf16[2,128,512]{2,1,0:T(8,128)(2,1)} %get-tuple-element.28.u0_ref), channel_id=1, source_target_pairs={{0,3},{1,0},{2,1},{3,2},{4,7},{5,4},{6,5},{7,6},{8,11},{9,8},{10,9... | collective-permute-start | bytes 786440 | tf_op jit(solution)/shard_map/ppermute | solution.py:298
  75.4 9.0 %collective-permute-start.10 = (bf16[2,128,512]{2,1,0:T(8,128)(2,1)}, bf16[2,128,512]{2,1,0:T(8,128)(2,1)S(1)}, u32[]{:S(2)}, u32[]{:S(2)}) collective-permute-start(bf16[2,128,512]{2,1,0:T(8,128)(2,1)} %get-tuple-element.28.u0_ref), channel_id=1, source_target_pairs={{0,2},{1,3},{2,0},{3,1},{4,6},{5,7},{6,4},{7,5},{8,10},{9,11},{10,... | collective-permute-start | bytes 786440 | tf_op jit(solution)/shard_map/ppermute | solution.py:298
  84.4 3.4 %copy-start.1 = (bf16[2,2048,1024]{2,1,0:T(8,128)(2,1)S(1)}, bf16[2,2048,1024]{2,1,0:T(8,128)(2,1)}, u32[]{:S(2)}) copy-start(bf16[2,2048,1024]{2,1,0:T(8,128)(2,1)} %table.1.table_ref) | copy-start | bytes 25165828
  100.3 2.6 %collective-permute-start.16 = (f32[8,384]{1,0:T(8,128)S(1)}, f32[8,384]{1,0:T(8,128)S(1)}, u32[]{:S(2)}, u32[]{:S(2)}) collective-permute-start(f32[8,384]{1,0:T(8,128)S(1)} %get-tuple-element.67), channel_id=1, source_target_pairs={{0,32},{4,36},{8,40},{12,44},{16,48},{20,52},{24,56},{28,60},{32,0... | collective-permute-start | bytes 36872 | tf_op jit(solution)/shard_map/ppermute | solution.py:312
  102.9 3.8 %collective-permute-start.17 = (f32[16,384]{1,0:T(8,128)S(1)}, f32[16,384]{1,0:T(8,128)S(1)}, u32[]{:S(2)}, u32[]{:S(2)}) collective-permute-start(f32[16,384]{1,0:T(8,128)S(1)} %pad_maximum_fusion.4), channel_id=1, source_target_pairs={{0,64},{4,68},{8,72},{12,76},{16,80},{20,84},{24,88},{28,92},{32,9... | collective-permute-start | bytes 73736 | tf_op jit(solution)/shard_map/ppermute | solution.py:312
  106.7 7.1 %collective-permute-start.18 = (f32[32,384]{1,0:T(8,128)S(1)}, f32[32,384]{1,0:T(8,128)S(1)}, u32[]{:S(2)}, u32[]{:S(2)}) collective-permute-start(f32[32,384]{1,0:T(8,128)S(1)} %pad_maximum_fusion.3), channel_id=1, source_target_pairs={{0,128},{4,132},{8,136},{12,140},{16,144},{20,148},{24,152},{28,15... | collective-permute-start | bytes 147464 | tf_op jit(solution)/shard_map/ppermute | solution.py:312
  113.8 3.6 %collective-permute-start.19 = (f32[64,384]{1,0:T(8,128)S(1)}, f32[64,384]{1,0:T(8,128)S(1)}, u32[]{:S(2)}, u32[]{:S(2)}) collective-permute-start(f32[64,384]{1,0:T(8,128)S(1)} %pad_maximum_fusion.2), channel_id=1, source_target_pairs={{0,8},{4,12},{8,0},{12,4},{16,24},{20,28},{24,16},{28,20},{32,40},... | collective-permute-start | bytes 294920 | tf_op jit(solution)/shard_map/ppermute | solution.py:312
  117.4 6.4 %collective-permute-start.20 = (f32[128,384]{1,0:T(8,128)S(1)}, f32[128,384]{1,0:T(8,128)S(1)}, u32[]{:S(2)}, u32[]{:S(2)}) collective-permute-start(f32[128,384]{1,0:T(8,128)S(1)} %get-tuple-element.54), channel_id=1, source_target_pairs={{0,16},{4,20},{8,24},{12,28},{16,0},{20,4},{24,8},{28,12},{32,48},... | collective-permute-start | bytes 589832 | tf_op jit(solution)/shard_map/ppermute | solution.py:312
  118.3 10.7 %collective-permute-start.11 = (bf16[2,128,512]{2,1,0:T(8,128)(2,1)S(1)}, bf16[2,128,512]{2,1,0:T(8,128)(2,1)S(1)}, u32[]{:S(2)}, u32[]{:S(2)}) collective-permute-start(bf16[2,128,512]{2,1,0:T(8,128)(2,1)S(1)} %get-tuple-element.31), channel_id=1, source_target_pairs={{0,1},{1,2},{2,3},{3,0},{4,5},{5,6},{6,7},{7,4},{8,9},{9,10},{10,1... | collective-permute-start | bytes 786440 | tf_op jit(solution)/shard_map/ppermute | solution.py:298
  119.4 9.6 %collective-permute-start.12 = (bf16[2,128,512]{2,1,0:T(8,128)(2,1)S(1)}, bf16[2,128,512]{2,1,0:T(8,128)(2,1)S(1)}, u32[]{:S(2)}, u32[]{:S(2)}) collective-permute-start(bf16[2,128,512]{2,1,0:T(8,128)(2,1)S(1)} %get-tuple-element.32), channel_id=1, source_target_pairs={{0,3},{1,0},{2,1},{3,2},{4,7},{5,4},{6,5},{7,6},{8,11},{9,8},{10,9... | collective-permute-start | bytes 786440 | tf_op jit(solution)/shard_map/ppermute | solution.py:298
  121.0 8.1 %collective-permute-start.13 = (bf16[2,128,512]{2,1,0:T(8,128)(2,1)S(1)}, bf16[2,128,512]{2,1,0:T(8,128)(2,1)S(1)}, u32[]{:S(2)}, u32[]{:S(2)}) collective-permute-start(bf16[2,128,512]{2,1,0:T(8,128)(2,1)S(1)} %get-tuple-element.33), channel_id=1, source_target_pairs={{0,2},{1,3},{2,0},{3,1},{4,6},{5,7},{6,4},{7,5},{8,10},{9,11},{10,... | collective-permute-start | bytes 786440 | tf_op jit(solution)/shard_map/ppermute | solution.py:298
  123.8 34.7 %collective-permute-start.21 = (f32[256,384]{1,0:T(8,128)S(1)}, f32[256,384]{1,0:T(8,128)S(1)}, u32[]{:S(2)}, u32[]{:S(2)}) collective-permute-start(f32[256,384]{1,0:T(8,128)S(1)} %get-tuple-element.48), channel_id=1, source_target_pairs={{0,4},{4,0},{8,12},{12,8},{16,20},{20,16},{24,28},{28,24},{32,36},... | collective-permute-start | bytes 1179656 | tf_op jit(solution)/shard_map/ppermute | solution.py:312
  132.2 14.1 %collective-permute-start.14 = (f32[2,5,512]{2,1,0:T(8,128)}, f32[2,5,512]{2,1,0:T(8,128)S(1)}, u32[]{:S(2)}, u32[]{:S(2)}) collective-permute-start(f32[2,5,512]{2,1,0:T(8,128)} %get-tuple-element.35), channel_id=1, source_target_pairs={{0,4},{4,8},{8,12},{12,16},{16,20},{20,24},{24,28},{28,32},{32,36}... | collective-permute-start | bytes 61448 | tf_op jit(solution)/shard_map/ppermute | solution.py:304
  144.4 8.8 %collective-permute-start.15 = (f32[2,5,512]{2,1,0:T(8,128)}, f32[2,5,512]{2,1,0:T(8,128)S(1)}, u32[]{:S(2)}, u32[]{:S(2)}) collective-permute-start(f32[2,5,512]{2,1,0:T(8,128)} %get-tuple-element.36), channel_id=1, source_target_pairs={{4,0},{8,4},{12,8},{16,12},{20,16},{24,20},{28,24},{32,28},{36,32}... | collective-permute-start | bytes 61448 | tf_op jit(solution)/shard_map/ppermute | solution.py:304
  146.3 6.8 %copy-start.24 = (f32[2,5,512]{2,1,0:T(8,128)}, f32[2,5,512]{2,1,0:T(8,128)S(1)}, u32[]{:S(2)}) copy-start(f32[2,5,512]{2,1,0:T(8,128)S(1)} %collective-permute-done.14.before_ref) | copy-start | bytes 61444
  (21 other events, 29.8 us)

commit v2 on v0

v2 whole, which is shorter than its diff:
```python
import functools
import math

import jax
import jax.numpy as jnp
import numpy as np
from jax import lax
from jax.experimental import pallas as pl
from jax.experimental.pallas import tpu as pltpu
from jax.sharding import PartitionSpec as P

MAXO = 2048
STEPS = 2
PTS = 128
ELEM_ROWS = 8
ID_ROW = 5
TABLE_STRIDE = 64
PARTNERS = (0, 2, 1, 3)

time_step_sq = 0.0004
kernel_scale = 0.0001
bucket_orders = (8, 64, 512, 2048)

f32 = jnp.float32
bf16 = jnp.bfloat16


def gll_tables():
    nodes = np.array([-1.0, -math.sqrt(3.0 / 7.0), 0.0, math.sqrt(3.0 / 7.0), 1.0])
    weights_line = np.array([0.1, 49.0 / 90.0, 32.0 / 45.0, 49.0 / 90.0, 0.1])
    legendre = (35.0 * nodes**4 - 30.0 * nodes**2 + 3.0) / 8.0
    deriv = np.zeros((5, 5))
    for row_index in range(5):
        for col_index in range(5):
            if row_index != col_index:
                deriv[row_index, col_index] = (
                    legendre[row_index]
                    / legendre[col_index]
                    / (nodes[row_index] - nodes[col_index])
                )
    deriv[0, 0] = -5.0
    deriv[4, 4] = 5.0
    return (deriv, np.outer(weights_line, weights_line).reshape(25))


def split_const(x):
    high = np.asarray(x, np.float32).astype(bf16)
    low = (np.asarray(x, np.float32) - high.astype(np.float32)).astype(bf16)
    return high, low


def derivative_matrices(elements):
    deriv, _ = gll_tables()
    along_s = np.zeros((PTS, PTS))
    along_z = np.zeros((PTS, PTS))
    for e in range(elements):
        base = slice(25 * e, 25 * e + 25)
        along_s[base, base] = np.kron(deriv, np.eye(5))
        along_z[base, base] = np.kron(np.eye(5), deriv)
    both = np.concatenate([along_s, along_z])
    high, low = split_const(both)
    forward = np.concatenate([high, high, low], axis=1)
    high_t, low_t = split_const(both.T)
    return forward, np.concatenate([high_t, low_t], axis=1)


def small_tables(nphi):
    coarse = TABLE_STRIDE * np.arange(MAXO // TABLE_STRIDE)
    every = np.concatenate([coarse, np.arange(TABLE_STRIDE)])
    angle = (every[:, None] * np.arange(nphi)[None, :] % nphi) * (2.0 * math.pi / nphi)
    return np.stack([np.cos(angle), np.sin(angle)]).astype(np.float32)


def table_kernel(small_ref, out_ref):
    coarse = MAXO // TABLE_STRIDE

    def one(a, carry):
        big_cos = small_ref[0, pl.ds(a, 1), :]
        big_sin = small_ref[1, pl.ds(a, 1), :]
        start = pl.multiple_of(a * TABLE_STRIDE, TABLE_STRIDE)
        for part in range(0, TABLE_STRIDE, 16):
            fine_cos = small_ref[0, coarse + part : coarse + part + 16, :]
            fine_sin = small_ref[1, coarse + part : coarse + part + 16, :]
            rows = pl.ds(pl.multiple_of(start + part, 16), 16)
            out_ref[0, rows, :] = (big_cos * fine_cos - big_sin * fine_sin).astype(bf16)
            out_ref[1, rows, :] = (big_sin * fine_cos + big_cos * fine_sin).astype(bf16)
        return carry

    lax.fori_loop(0, coarse, one, 0)


VMEM = pl.BlockSpec(memory_space=pltpu.VMEM)
SMEM = pl.BlockSpec(memory_space=pltpu.SMEM)


def call(kernel, name, out_shape, operands, scalars=0, scratch=(), mib=16):
    single = not isinstance(out_shape, (list, tuple))
    return pl.pallas_call(
        kernel,
        in_specs=[SMEM] * scalars + [VMEM] * (len(operands) - scalars),
        out_specs=VMEM if single else [VMEM] * len(out_shape),
        out_shape=out_shape,
        scratch_shapes=list(scratch),
        name=name,
        compiler_params=pltpu.CompilerParams(vmem_limit_bytes=mib * 1024 * 1024),
    )(*operands)


def block_start(blk_ref, bits, count):
    blk = blk_ref[0, 0]
    partner = (blk, blk + 1 - 2 * lax.rem(blk, 2), lax.rem(blk + 2, 4), 3 - blk)[bits]
    return pl.multiple_of(partner * count, count)


def fourier_table(small):
    count = small.shape[2]
    shape = jax.ShapeDtypeStruct((2, MAXO, count), bf16)
    return call(table_kernel, "table", shape, [small])


def dot(a, b):
    return jnp.dot(a, b, preferred_element_type=f32)


def dot_t(a, b):
    return lax.dot_general(a, b, (((1,), (1,)), ((), ())), preferred_element_type=f32)


def exact_dot(a, b):
    return jnp.dot(a, b, preferred_element_type=f32, precision=lax.Precision.HIGHEST)


def levels_of(bucket_ref, points):
    point = lax.broadcasted_iota(jnp.int32, (points, 1), 0)
    level = jnp.zeros((points, 1), jnp.int32)
    for e in range(bucket_ref.shape[1]):
        value = jnp.int32(0)
        for position, orders in enumerate(bucket_orders):
            value = jnp.where(bucket_ref[0, e] == position, orders, value)
        level = jnp.where((point >= 25 * e) & (point < 25 * e + 25), value, level)
    return level


def arrange_kernel(bucket_ref, blk_ref, disp_ref, now_ref, *send_ref):
    points, _, count = disp_ref.shape
    order = lax.broadcasted_iota(jnp.int32, (points, count), 1) + blk_ref[0, 0] * count
    inside = order < levels_of(bucket_ref, points)
    now_ref[:, points:, :] = jnp.zeros((2, now_ref.shape[1] - points, count), f32)
    for c in range(2):
        kept = inside if c == 0 else inside & (order >= 1)
        now_ref[c, :points, :] = jnp.where(kept, disp_ref[:, c, :], 0.0)
    for s_ref in send_ref:
        s_ref[...] = now_ref[...].astype(bf16)


def arrange(buckets, blk, disp, with_send):
    shape = (2, PTS, disp.shape[2])
    outs = [jax.ShapeDtypeStruct(shape, f32)] + [jax.ShapeDtypeStruct(shape, bf16)] * with_send
    return call(arrange_kernel, "arrange", outs, [buckets, blk, disp], 2)


def setup_kernel(bucket_ref, region_ref, radius_ref, weight_ref, kappa_ref, fwd_ref, column_ref, kap_ref, first_ref, second_ref, density_ref):
    points = radius_ref.shape[1]
    square = (points, points)
    diagonal = lax.broadcasted_iota(jnp.int32, square, 0) == lax.broadcasted_iota(jnp.int32, square, 1)
    radius = jnp.sum(jnp.where(diagonal, radius_ref[...], 0.0), axis=1, keepdims=True)
    weight = weight_ref[...] * radius
    column_ref[...] = jnp.zeros(column_ref.shape, f32)
    column_ref[:points, 0:1] = 1.0 / radius
    column_ref[:points, 1:2] = weight * (2.0 * math.pi / (2 * MAXO))
    column_ref[:points, 2:3] = levels_of(bucket_ref, points).astype(f32)
    column_ref[:points, 3:4] = time_step_sq / (weight * math.pi)
    tail = PTS - 16
    kap_ref[tail:, :] = jnp.zeros((16, kap_ref.shape[1]), bf16)
    kap_ref[:points, :] = kappa_ref[...]
    for s, o_ref in enumerate((first_ref, second_ref)):
        for i in range(3):
            o_ref[i, tail:, :] = jnp.zeros((16, kap_ref.shape[1]), bf16)
            o_ref[i, :points, :] = fwd_ref[s, i]
    shape = density_ref.shape
    row, lane = lax.broadcasted_iota(jnp.int32, shape, 0), lax.broadcasted_iota(jnp.int32, shape, 1)
    density = jnp.zeros(shape, f32)
    for e in range(region_ref.shape[1]):
        name = region_ref[0, e].astype(f32)
        density = jnp.where((row == ID_ROW) & (lane == e), name, density)
    density_ref[...] = density


def setup(buckets, regions, radius, weight, kappa, fwd):
    samples = kappa.shape[1]
    outs = [
        jax.ShapeDtypeStruct((PTS, 4), f32),
        jax.ShapeDtypeStruct((PTS, samples), bf16),
        jax.ShapeDtypeStruct((3, PTS, samples), bf16),
        jax.ShapeDtypeStruct((3, PTS, samples), bf16),
        jax.ShapeDtypeStruct((ELEM_ROWS, samples // 4), f32),
    ]
    return call(setup_kernel, "setup", outs, [buckets, regions, radius, weight, kappa, fwd], 2)


def sides(mer_ref):
    here = 1 - lax.rem(mer_ref[0, 0], 2)
    return here, 1 - here


def synthesis_kernel(
    blk_ref,
    mer_ref,
    nodes_ref,
    u0_ref,
    u1_ref,
    u2_ref,
    u3_ref,
    kappa_ref,
    fwd_ref,
    table_ref,
    forward_ref,
    backward_ref,
    column_ref,
    sum_rows_ref,
    sum_cols_ref,
    before_ref,
    stress_ref,
    core_ref,
    chip_ref,
    density_ref,
    coeff_ref,
    dens_ref,
):
    count = u0_ref.shape[2]
    samples = kappa_ref.shape[1]
    lane = lax.broadcasted_iota(jnp.int32, (1, count), 1)
    inv_radius = column_ref[:, 0:1]
    quad = column_ref[:, 1:2]
    for bits, u_ref in zip(PARTNERS, (u0_ref, u1_ref, u2_ref, u3_ref)):
        start = block_start(blk_ref, bits, count)
        order = (lane + start).astype(f32)
        u0, u1 = u_ref[0], u_ref[1]
        coeff_ref[:PTS, pl.ds(start, count)] = u0
        coeff_ref[:PTS, pl.ds(MAXO + start, count)] = u1
        coeff_ref[PTS:, pl.ds(start, count)] = (order * u1.astype(f32)).astype(bf16)
        coeff_ref[PTS:, pl.ds(MAXO + start, count)] = (-order * u0.astype(f32)).astype(bf16)
    width = 1024
    for n in range(samples // width):
        cols = slice(n * width, (n + 1) * width)
        phys = dot(coeff_ref[:, :MAXO], table_ref[0, :, cols]) + dot(
            coeff_ref[:, MAXO:], table_ref[1, :, cols]
        )
        field, around = phys[:PTS], phys[PTS:] * inv_radius
        high = field.astype(bf16)
        low = (field - high.astype(f32)).astype(bf16)
        along = dot(forward_ref[...], jnp.concatenate([high, low, high]))
        along_s, along_z = along[:PTS], along[PTS:]
        modulus = kappa_ref[:, cols].astype(f32) * quad
        stress = jnp.concatenate([along_s * modulus, along_z * modulus]).astype(bf16)
        stress_ref[:PTS, cols] = dot(backward_ref[...], jnp.concatenate([stress, stress]))
        stress_ref[PTS:, cols] = around * modulus * inv_radius
        dens = (
            along_s * fwd_ref[0, :, cols].astype(f32)
            + along_z * fwd_ref[1, :, cols].astype(f32)
            + around * fwd_ref[2, :, cols].astype(f32)
        ) * (quad * kernel_scale)
        dens_high = dens.astype(bf16)
        dens_ref[:PTS, cols] = dens_high
        dens_ref[PTS:, cols] = (dens - dens_high.astype(f32)).astype(bf16)
    spare = jnp.zeros((8 - nodes_ref.shape[1], samples), f32)
    for o_ref, side in zip((core_ref, chip_ref), sides(mer_ref)):
        rows = []
        for part in range(2):
            for k in range(nodes_ref.shape[1]):
                rows.append(stress_ref[pl.ds(PTS * part + nodes_ref[side, k], 1), :])
            rows.append(spare)
        o_ref[...] = jnp.concatenate(rows).astype(bf16)
    by_sector = dot(dens_ref[...], sum_cols_ref[...])
    density_ref[...] = before_ref[...] + exact_dot(sum_rows_ref[...], by_sector[:PTS] + by_sector[PTS:])


def synthesis(blk, mer, nodes, blocks, kappa, fwd, table, consts, columns, before):
    forward, backward, sum_rows, sum_cols = consts
    samples = kappa.shape[1]
    rows = jax.ShapeDtypeStruct((16, samples), bf16)
    outs = [jax.ShapeDtypeStruct((2 * PTS, samples), f32), rows, rows, jax.ShapeDtypeStruct(before.shape, f32)]
    scratch = [pltpu.VMEM((2 * PTS, 2 * MAXO), bf16), pltpu.VMEM((2 * PTS, samples), bf16)]
    operands = [blk, mer, nodes, *blocks, kappa, fwd, table, forward, backward, columns, sum_rows, sum_cols, before]
    return call(synthesis_kernel, "synthesis", outs, operands, 3, scratch)


def merge_kernel(mer_ref, nodes_ref, stress_ref, core_ref, chip_ref, out_ref, total_ref):
    total_ref[...] = stress_ref[...]
    for r_ref, side in zip((core_ref, chip_ref), sides(mer_ref)):
        rows = r_ref[...].astype(f32)
        for part in range(2):
            for k in range(nodes_ref.shape[1]):
                at = 8 * part + k
                total_ref[pl.ds(PTS * part + nodes_ref[side, k], 1), :] += rows[at : at + 1]
    out_ref[...] = total_ref[...].astype(bf16)


def merge(mer, nodes, stress, core, chip):
    shape = jax.ShapeDtypeStruct(stress.shape, bf16)
    scratch = [pltpu.VMEM(stress.shape, f32)]
    return call(merge_kernel, "merge", shape, [mer, nodes, stress, core, chip], 2, scratch)


def analysis_kernel(shift, blk_ref, stress_ref, table_ref, o_ref):
    count = o_ref.shape[2]
    start = block_start(blk_ref, shift, count)
    order = (lax.broadcasted_iota(jnp.int32, (1, count), 1) + start).astype(f32)
    cosine = dot_t(stress_ref[...], table_ref[0, pl.ds(start, count), :])
    sine = dot_t(stress_ref[...], table_ref[1, pl.ds(start, count), :])
    o_ref[0] = (cosine[:PTS] - order * sine[PTS:]).astype(bf16)
    o_ref[1] = (sine[:PTS] + order * cosine[PTS:]).astype(bf16)


def analysis(shift, blk, stress, table, count):
    shape = jax.ShapeDtypeStruct((2, PTS, count), bf16)
    kernel = functools.partial(analysis_kernel, shift)
    return call(kernel, "analysis", shape, [blk, stress, table], 1)


def update_kernel(blk_ref, *refs):
    parts = refs[:4]
    now_ref, prev_ref, column_ref = refs[4:7]
    outs = refs[7:]
    shape = now_ref.shape[1:]
    order = lax.broadcasted_iota(jnp.int32, shape, 1) + blk_ref[0, 0] * shape[1]
    level = column_ref[:, 2:3]
    scale = column_ref[:, 3:4]
    inside = order.astype(f32) < level
    first = order == 0
    for c in range(2):
        gain = jnp.where(first, scale * (0.5 if c == 0 else 0.0), scale)
        gain = jnp.where(inside, gain, 0.0)
        force = sum(p[c].astype(f32) for p in parts)
        value = 2.0 * now_ref[c] - prev_ref[c] - gain * force
        if len(outs) == 2:
            outs[0][c] = value
            outs[1][c] = value.astype(bf16)
        else:
            points = outs[0].shape[0]
            outs[0][:, c, :] = value[:points]


def update(blk, parts, now, prev, columns, points):
    if points:
        outs = [jax.ShapeDtypeStruct((points, 2, now.shape[2]), f32)]
    else:
        outs = [jax.ShapeDtypeStruct(now.shape, f32), jax.ShapeDtypeStruct(now.shape, bf16)]
    return call(update_kernel, "update", outs, [blk, *parts, now, prev, columns], 1)


def join_kernel(*refs):
    rows = refs[0].shape[0]
    for i, ref in enumerate(refs[:-1]):
        refs[-1][i * rows : (i + 1) * rows] = ref[...]


def joined(x, axis, *bits):
    pieces = [x] + [swapped(x, axis, b) for b in bits]
    shape = jax.ShapeDtypeStruct((len(pieces) * x.shape[0], x.shape[1]), x.dtype)
    return call(join_kernel, "join", shape, pieces)


def owners_kernel(first_ref, rows_ref, out_ref):
    regions, sectors = out_ref.shape
    count = rows_ref.shape[0]
    rows = rows_ref[...]
    names = rows[:, :128].reshape(count // ELEM_ROWS, ELEM_ROWS, 128)
    names = jnp.broadcast_to(names[:, ID_ROW : ID_ROW + 1], names.shape)
    element = lax.broadcasted_iota(jnp.int32, names.shape, 1)
    lane = lax.broadcasted_iota(jnp.int32, names.shape, 2)
    ids = jnp.sum(jnp.where((lane == element) & (element < ID_ROW), names, 0.0), axis=2, keepdims=True)
    ids = jnp.where(element[:, :, :1] < ID_ROW, ids, -1.0).reshape(count, 1)
    mine = (lax.broadcasted_iota(jnp.int32, (count, regions), 1) + first_ref[0, 0]).astype(f32)
    out_ref[...] = lax.dot_general(
        jnp.where(ids == mine, 1.0, 0.0),
        rows,
        (((0,), (0,)), ((), ())),
        preferred_element_type=f32,
        precision=lax.Precision.HIGHEST,
    )


def owners(first, rows, regions):
    shape = jax.ShapeDtypeStruct((regions, rows.shape[1]), f32)
    return call(owners_kernel, "owners", shape, [first, rows], 1)


def swapped(x, axis, bits):
    return lax.ppermute(x, axis, [(i, i ^ bits) for i in range(lax.axis_size(axis))])


def across_chips(x):
    ends = range(1, lax.axis_size("mer") - 1)
    return lax.ppermute(x, "mer", [(i, i + 1 if i % 2 else i - 1) for i in ends])


def tied(x, other):
    return lax.optimization_barrier((x, other))[0]


def local(disp_now, disp_prev, kappa, radius, fwd_strain, order_bucket, shared_nodes, region_map):
    points, _, count = disp_now.shape
    elements = order_bucket.shape[0]
    samp_count = kappa.shape[1]
    nphi = 2 * MAXO
    sectors = samp_count // 4
    regions = 4096 // lax.axis_size("mer")
    blk_index = lax.axis_index("blk").astype(jnp.int32)
    blk = blk_index.reshape(1, 1)
    mer = lax.axis_index("mer").astype(jnp.int32).reshape(1, 1)
    first = (lax.axis_index("mer").astype(jnp.int32) * regions).reshape(1, 1)
    buckets = order_bucket.reshape(1, -1)
    nodes = shared_nodes[0]
    current, send = arrange(buckets, blk, disp_now, 1)
    (previous,) = arrange(buckets, blk, disp_prev, 0)
    _, gllw = gll_tables()
    weight = jnp.asarray(np.tile(gllw, elements).reshape(-1, 1), f32)
    columns, kappa, *fwd, density = setup(
        buckets, region_map.reshape(1, -1), radius.reshape(1, -1), weight, kappa, fwd_strain
    )
    forward, backward = derivative_matrices(elements)
    sum_rows = np.zeros((ELEM_ROWS, PTS), np.float32)
    for e in range(elements):
        sum_rows[e, 25 * e : 25 * e + 25] = 1.0
    sum_cols = np.kron(np.eye(sectors), np.ones((4, 1))).astype(bf16)
    consts = tuple(jnp.asarray(x) for x in (forward, backward, sum_rows, sum_cols))
    small = lax.dynamic_slice_in_dim(jnp.asarray(small_tables(nphi)), blk_index * samp_count, samp_count, 2)
    small, columns, kappa, fwd, density, previous, first, consts = lax.optimization_barrier(
        (small, columns, kappa, fwd, density, previous, first, consts)
    )
    table = fourier_table(small)
    for section in range(STEPS):
        last = section == STEPS - 1
        blocks = [send] + [swapped(send, "blk", bits) for bits in PARTNERS[1:]]
        stress, core, chip, density = synthesis(
            blk, mer, nodes, blocks, kappa, fwd[section], table, consts, columns, density
        )
        if last:
            gathered = joined(density, "mer", 8, 16, 24)
            stress = tied(stress, gathered)
        chip, core = across_chips(chip), swapped(core, "mer", 1)
        stress = merge(mer, nodes, stress, core, chip)
        forces = {bits: analysis(bits, blk, stress, table, count) for bits in (2, 1)}
        if last:
            gathered = joined(tied(gathered, stress), "mer", 32)
            stress = tied(stress, gathered)
        forces |= {bits: analysis(bits, blk, stress, table, count) for bits in (3, 0)}
        parts = [forces[0]] + [swapped(forces[bits], "blk", bits) for bits in PARTNERS[1:]]
        if last:
            gathered = joined(tied(gathered, [parts[1], forces[1], forces[3], forces[0]]), "mer", 2, 4, 6)
            gathered = joined(gathered, "mer", 1)
        outs = update(blk, parts, current, previous, columns, points if last else 0)
        if not last:
            current, previous, send = outs[0], current, outs[1]
    return (outs[0], owners(first, gathered, regions))


def solution(mesh):
    in_specs = (
        P("mer", None, "blk"),
        P("mer", None, "blk"),
        P("mer", "blk"),
        P("mer"),
        P(None, None, "mer", "blk"),
        P("mer"),
        P("mer", None, None),
        P("mer"),
    )
    out_specs = (P("mer", None, "blk"), P("mer", "blk"))
    return jax.shard_map(local, mesh=mesh, in_specs=in_specs, out_specs=out_specs, check_vma=False)
```

time: 440 us -> 111 us (0.25)
  the two profiles are of different devices: /device:TPU:1 before, /device:TPU:192 now
where the time goes in v2:
time: 111 us
  waiting for transfers between devices  41.1 us (37%)
  starting transfers between devices  37.4 us (34%)
  Pallas kernels  24 us (22%)
  local copies, waits for them, and re-layouts  7.43 us (7%)
    ppermute x22, waiting for transfers between devices, swapped(): lax.ppermute(x, axis, [(i, i ^ bits) for i in range(lax.axis_size(axis))])  39 us
    ppermute x22, starting transfers between devices, swapped(): lax.ppermute(x, axis, [(i, i ^ bits) for i in range(lax.axis_size(axis))])  26.3 us
    pallas_call x23, Pallas kernels, call(): pl.pallas_call(kernel, in_specs=[SMEM] * scalars + [VMEM] * (len(operands...  24 us
    ppermute x2, starting transfers between devices, across_chips(): lax.ppermute(x, 'mer', [(i, i + 1 if i % 2 else i - 1) for i in ends])  11.1 us
    unnamed x29, local copies, waits for them, and re-layouts  6.23 us
  transfers between devices with their start and end apart: 24, of which 14 were waited for; matrix products, arithmetic and copies ran while one was open for 3% of the time, Pallas kernels for 8%

profile of v2, /device:TPU:192, one launch (start us, length us, event | category | flops | bytes accessed | tf_op | source)
XLA Modules:
  0.0 110.9 jit_solution(773296486554577912)
XLA Ops:
  3.1 3.1 %collective-permute-start.2 = (bf16[2,128,512]{2,1,0:T(8,128)(2,1)S(1)}, bf16[2,128,512]{2,1,0:T(8,128)(2,1)S(1)}, u32[]{:S(2)}, u32[]{:S(2)}) collective-permute-start(bf16[2,128,512]{2,1,0:T(8,128)(2,1)S(1)} %get-tuple-element.35.u0_ref), channel_id=1, source_target_pairs={{0,3},{1,2},{2,1},{3,0},{4,7},{5,6},{6,5},{7,4},{8,11},{9,10},{10,... | collective-permute-start | bytes 786440 | tf_op jit(solution)/shard_map/ppermute | solution.py:390
  6.3 1.5 %collective-permute-start = (bf16[2,128,512]{2,1,0:T(8,128)(2,1)S(1)}, bf16[2,128,512]{2,1,0:T(8,128)(2,1)}, u32[]{:S(2)}, u32[]{:S(2)}) collective-permute-start(bf16[2,128,512]{2,1,0:T(8,128)(2,1)S(1)} %get-tuple-element.35.u0_ref), channel_id=1, source_target_pairs={{0,2},{1,3},{2,0},{3,1},{4,6},{5,7},{6,4},{7,5},{8,10},{9,11},{10,... | collective-permute-start | bytes 786440 | tf_op jit(solution)/shard_map/ppermute | solution.py:390
  10.2 1.8 %copy.16.fwd_ref = bf16[2,3,125,1024]{3,2,1,0:T(8,128)(2,1)S(1)} copy(bf16[2,3,125,1024]{3,0,2,1:T(2,128)(2,1)} %param.18) | data formatting | bytes 3072000 | tf_op args[4]
  13.9 1.2 %constant_dynamic-slice_fusion.small_ref = f32[2,96,1024]{2,1,0:T(8,128)S(1)} fusion(f32[2,96,4096]{2,1,0:T(8,128)} %constant.34.clone, s32[]{:T(128)S(6)} %select_n.3), kind=kLoop, calls=%fused_computation | loop fusion | bytes 1572868 | tf_op jit(solution)/shard_map/dynamic_slice | solution.py:428
  15.1 2.8 %table.1.table_ref = bf16[2,2048,1024]{2,1,0:T(8,128)(2,1)S(1)} custom-call(f32[2,96,1024]{2,1,0:T(8,128)S(1)} %constant_dynamic-slice_fusion.small_ref), custom_call_target="tpu_custom_call" | custom-call | tf_op jit(solution)/shard_map/table/pallas_call | solution.py:98
  17.9 1.6 %collective-permute-done.u1_ref = bf16[2,128,512]{2,1,0:T(8,128)(2,1)} collective-permute-done((bf16[2,128,512]{2,1,0:T(8,128)(2,1)S(1)}, bf16[2,128,512]{2,1,0:T(8,128)(2,1)}, u32[]{:S(2)}, u32[]{:S(2)}) %collective-permute-start) | collective-permute-done | bytes 262176 | tf_op jit(solution)/shard_map/ppermute | solution.py:390
  19.5 4.6 %synthesis.2 = (f32[256,1024]{1,0:T(8,128)S(1)}, bf16[16,1024]{1,0:T(8,128)(2,1)S(1)}, bf16[16,1024]{1,0:T(8,128)(2,1)S(1)}, f32[8,256]{1,0:T(8,128)S(1)}) custom-call(s32[1,1]{1,0:T(1,128)} %bitcast.blk_ref, s32[1,1]{1,0:T(1,128)} %bitcast.1.mer_ref, s32[2,5]{1,0:T(2,128)S(1)} %bitcast.7, bf16[2,128,512]{2,1,0:T(8,128)(2,1)S(1)} %get-tuple-element.35.u0_ref, ...), custom_call_target="tpu_custom_call" | custom-call | tf_op jit(solution)/shard_map/synthesis/pallas_call | solution.py:98
  24.1 5.2 %collective-permute-start.4 = (bf16[16,1024]{1,0:T(8,128)(2,1)S(1)}, bf16[16,1024]{1,0:T(8,128)(2,1)S(1)}, u32[]{:S(2)}, u32[]{:S(2)}) collective-permute-start(bf16[16,1024]{1,0:T(8,128)(2,1)S(1)} %get-tuple-element.52), channel_id=1, source_target_pairs={{4,8},{8,4},{12,16},{16,12},{20,24},{24,20},{28,32},{32,28},{36,40... | collective-permute-start | bytes 98312 | tf_op jit(solution)/shard_map/ppermute | solution.py:395
  29.4 2.1 %collective-permute-done.4.chip_ref = bf16[16,1024]{1,0:T(8,128)(2,1)S(1)} collective-permute-done((bf16[16,1024]{1,0:T(8,128)(2,1)S(1)}, bf16[16,1024]{1,0:T(8,128)(2,1)S(1)}, u32[]{:S(2)}, u32[]{:S(2)}) %collective-permute-start.4) | collective-permute-done | bytes 32800 | tf_op jit(solution)/shard_map/ppermute | solution.py:395
  34.5 2.0 %collective-permute-start.5 = (bf16[2,128,512]{2,1,0:T(8,128)(2,1)S(1)}, bf16[2,128,512]{2,1,0:T(8,128)(2,1)S(1)}, u32[]{:S(2)}, u32[]{:S(2)}) collective-permute-start(bf16[2,128,512]{2,1,0:T(8,128)(2,1)S(1)} %analysis.9), channel_id=1, source_target_pairs={{0,2},{1,3},{2,0},{3,1},{4,6},{5,7},{6,4},{7,5},{8,10},{9,11},{10,... | collective-permute-start | bytes 786440 | tf_op jit(solution)/shard_map/ppermute | solution.py:390
  36.6 1.7 %collective-permute-start.6 = (bf16[2,128,512]{2,1,0:T(8,128)(2,1)S(1)}, bf16[2,128,512]{2,1,0:T(8,128)(2,1)S(1)}, u32[]{:S(2)}, u32[]{:S(2)}) collective-permute-start(bf16[2,128,512]{2,1,0:T(8,128)(2,1)S(1)} %analysis.10), channel_id=1, source_target_pairs={{0,1},{1,0},{2,3},{3,2},{4,5},{5,4},{6,7},{7,6},{8,9},{9,8},{10,11... | collective-permute-start | bytes 786440 | tf_op jit(solution)/shard_map/ppermute | solution.py:390
  39.4 5.9 %collective-permute-done.5.refs_1_ = bf16[2,128,512]{2,1,0:T(8,128)(2,1)S(1)} collective-permute-done((bf16[2,128,512]{2,1,0:T(8,128)(2,1)S(1)}, bf16[2,128,512]{2,1,0:T(8,128)(2,1)S(1)}, u32[]{:S(2)}, u32[]{:S(2)}) %collective-permute-start.5) | collective-permute-done | bytes 262176 | tf_op jit(solution)/shard_map/ppermute | solution.py:390
  45.3 3.2 %collective-permute-done.6.refs_2_ = bf16[2,128,512]{2,1,0:T(8,128)(2,1)S(1)} collective-permute-done((bf16[2,128,512]{2,1,0:T(8,128)(2,1)S(1)}, bf16[2,128,512]{2,1,0:T(8,128)(2,1)S(1)}, u32[]{:S(2)}, u32[]{:S(2)}) %collective-permute-start.6) | collective-permute-done | bytes 262176 | tf_op jit(solution)/shard_map/ppermute | solution.py:390
  48.9 2.7 %collective-permute-start.10 = (bf16[2,128,512]{2,1,0:T(8,128)(2,1)S(1)}, bf16[2,128,512]{2,1,0:T(8,128)(2,1)S(1)}, u32[]{:S(2)}, u32[]{:S(2)}) collective-permute-start(bf16[2,128,512]{2,1,0:T(8,128)(2,1)S(1)} %get-tuple-element.55.u0_ref), channel_id=1, source_target_pairs={{0,3},{1,2},{2,1},{3,0},{4,7},{5,6},{6,5},{7,4},{8,11},{9,10},{10,... | collective-permute-start | bytes 786440 | tf_op jit(solution)/shard_map/ppermute | solution.py:390
  51.6 2.1 %collective-permute-start.8 = (bf16[2,128,512]{2,1,0:T(8,128)(2,1)S(1)}, bf16[2,128,512]{2,1,0:T(8,128)(2,1)S(1)}, u32[]{:S(2)}, u32[]{:S(2)}) collective-permute-start(bf16[2,128,512]{2,1,0:T(8,128)(2,1)S(1)} %get-tuple-element.55.u0_ref), channel_id=1, source_target_pairs={{0,2},{1,3},{2,0},{3,1},{4,6},{5,7},{6,4},{7,5},{8,10},{9,11},{10,... | collective-permute-start | bytes 786440 | tf_op jit(solution)/shard_map/ppermute | solution.py:390
  53.6 4.3 %collective-permute-done.10.u3_ref = bf16[2,128,512]{2,1,0:T(8,128)(2,1)S(1)} collective-permute-done((bf16[2,128,512]{2,1,0:T(8,128)(2,1)S(1)}, bf16[2,128,512]{2,1,0:T(8,128)(2,1)S(1)}, u32[]{:S(2)}, u32[]{:S(2)}) %collective-permute-start.10) | collective-permute-done | bytes 262176 | tf_op jit(solution)/shard_map/ppermute | solution.py:390
  57.9 2.9 %collective-permute-done.9.u2_ref = bf16[2,128,512]{2,1,0:T(8,128)(2,1)S(1)} collective-permute-done((bf16[2,128,512]{2,1,0:T(8,128)(2,1)S(1)}, bf16[2,128,512]{2,1,0:T(8,128)(2,1)S(1)}, u32[]{:S(2)}, u32[]{:S(2)}) %collective-permute-start.9) | collective-permute-done | bytes 262176 | tf_op jit(solution)/shard_map/ppermute | solution.py:390
  60.8 4.2 %collective-permute-done.8.u1_ref = bf16[2,128,512]{2,1,0:T(8,128)(2,1)S(1)} collective-permute-done((bf16[2,128,512]{2,1,0:T(8,128)(2,1)S(1)}, bf16[2,128,512]{2,1,0:T(8,128)(2,1)S(1)}, u32[]{:S(2)}, u32[]{:S(2)}) %collective-permute-start.8) | collective-permute-done | bytes 262176 | tf_op jit(solution)/shard_map/ppermute | solution.py:390
  65.0 4.2 %synthesis.3 = (f32[256,1024]{1,0:T(8,128)S(1)}, bf16[16,1024]{1,0:T(8,128)(2,1)S(1)}, bf16[16,1024]{1,0:T(8,128)(2,1)S(1)}, f32[8,256]{1,0:T(8,128)S(1)}) custom-call(s32[1,1]{1,0:T(1,128)} %bitcast.blk_ref, s32[1,1]{1,0:T(1,128)} %bitcast.1.mer_ref, s32[2,5]{1,0:T(2,128)S(1)} %bitcast.9, bf16[2,128,512]{2,1,0:T(8,128)(2,1)S(1)} %get-tuple-element.55.u0_ref, ...), custom_call_target="tpu_custom_call" | custom-call | tf_op jit(solution)/shard_map/synthesis/pallas_call | solution.py:98
  69.1 5.8 %collective-permute-start.15 = (bf16[16,1024]{1,0:T(8,128)(2,1)S(1)}, bf16[16,1024]{1,0:T(8,128)(2,1)S(1)}, u32[]{:S(2)}, u32[]{:S(2)}) collective-permute-start(bf16[16,1024]{1,0:T(8,128)(2,1)S(1)} %get-tuple-element.62), channel_id=1, source_target_pairs={{4,8},{8,4},{12,16},{16,12},{20,24},{24,20},{28,32},{32,28},{36,40... | collective-permute-start | bytes 98312 | tf_op jit(solution)/shard_map/ppermute | solution.py:395
  75.0 1.1 collective-permute-start.13
  76.1 2.4 %collective-permute-start.12 = (f32[8,256]{1,0:T(8,128)S(1)}, f32[8,256]{1,0:T(8,128)S(1)}, u32[]{:S(2)}, u32[]{:S(2)}) collective-permute-start(f32[8,256]{1,0:T(8,128)S(1)} %get-tuple-element.59.refs_0_), channel_id=1, source_target_pairs={{0,64},{4,68},{8,72},{12,76},{16,80},{20,84},{24,88},{28,92},{32,9... | collective-permute-start | bytes 24584 | tf_op jit(solution)/shard_map/ppermute | solution.py:390
  78.7 1.9 %collective-permute-done.12.refs_2_ = f32[8,256]{1,0:T(8,128)S(1)} collective-permute-done((f32[8,256]{1,0:T(8,128)S(1)}, f32[8,256]{1,0:T(8,128)S(1)}, u32[]{:S(2)}, u32[]{:S(2)}) %collective-permute-start.12) | collective-permute-done | bytes 8224 | tf_op jit(solution)/shard_map/ppermute | solution.py:390
  80.6 1.5 %collective-permute-done.11.refs_1_ = f32[8,256]{1,0:T(8,128)S(1)} collective-permute-done((f32[8,256]{1,0:T(8,128)S(1)}, f32[8,256]{1,0:T(8,128)S(1)}, u32[]{:S(2)}, u32[]{:S(2)}) %collective-permute-start.11) | collective-permute-done | bytes 8224 | tf_op jit(solution)/shard_map/ppermute | solution.py:390
  83.7 1.9 %collective-permute-start.17 = (bf16[2,128,512]{2,1,0:T(8,128)(2,1)S(1)}, bf16[2,128,512]{2,1,0:T(8,128)(2,1)S(1)}, u32[]{:S(2)}, u32[]{:S(2)}) collective-permute-start(bf16[2,128,512]{2,1,0:T(8,128)(2,1)S(1)} %analysis.13), channel_id=1, source_target_pairs={{0,2},{1,3},{2,0},{3,1},{4,6},{5,7},{6,4},{7,5},{8,10},{9,11},{10,... | collective-permute-start | bytes 786440 | tf_op jit(solution)/shard_map/ppermute | solution.py:390
  86.9 6.5 %collective-permute-done.16.refs_1_ = f32[32,256]{1,0:T(8,128)S(1)} collective-permute-done((f32[32,256]{1,0:T(8,128)S(1)}, f32[32,256]{1,0:T(8,128)S(1)}, u32[]{:S(2)}, u32[]{:S(2)}) %collective-permute-start.16) | collective-permute-done | bytes 32800 | tf_op jit(solution)/shard_map/ppermute | solution.py:390
  95.3 3.9 %collective-permute-start.20 = (f32[64,256]{1,0:T(8,128)S(1)}, f32[64,256]{1,0:T(8,128)S(1)}, u32[]{:S(2)}, u32[]{:S(2)}) collective-permute-start(f32[64,256]{1,0:T(8,128)S(1)} %join.5.refs_0_), channel_id=1, source_target_pairs={{0,8},{4,12},{8,0},{12,4},{16,24},{20,28},{24,16},{28,20},{32,40},... | collective-permute-start | bytes 196616 | tf_op jit(solution)/shard_map/ppermute | solution.py:390
  99.1 1.7 %collective-permute-start.18 = (bf16[2,128,512]{2,1,0:T(8,128)(2,1)S(1)}, bf16[2,128,512]{2,1,0:T(8,128)(2,1)S(1)}, u32[]{:S(2)}, u32[]{:S(2)}) collective-permute-start(bf16[2,128,512]{2,1,0:T(8,128)(2,1)S(1)} %analysis.14), channel_id=1, source_target_pairs={{0,1},{1,0},{2,3},{3,2},{4,5},{5,4},{6,7},{7,6},{8,9},{9,8},{10,11... | collective-permute-start | bytes 786440 | tf_op jit(solution)/shard_map/ppermute | solution.py:390
  102.2 3.3 %collective-permute-done.18.refs_2_ = bf16[2,128,512]{2,1,0:T(8,128)(2,1)S(1)} collective-permute-done((bf16[2,128,512]{2,1,0:T(8,128)(2,1)S(1)}, bf16[2,128,512]{2,1,0:T(8,128)(2,1)S(1)}, u32[]{:S(2)}, u32[]{:S(2)}) %collective-permute-start.18) | collective-permute-done | bytes 262176 | tf_op jit(solution)/shard_map/ppermute | solution.py:390
  105.5 2.9 %collective-permute-done.19.refs_3_ = bf16[2,128,512]{2,1,0:T(8,128)(2,1)S(1)} collective-permute-done((bf16[2,128,512]{2,1,0:T(8,128)(2,1)S(1)}, bf16[2,128,512]{2,1,0:T(8,128)(2,1)S(1)}, u32[]{:S(2)}, u32[]{:S(2)}) %collective-permute-start.19) | collective-permute-done | bytes 262176 | tf_op jit(solution)/shard_map/ppermute | solution.py:390
  108.4 1.2 %update.3 = f32[125,2,512]{2,1,0:T(2,128)} custom-call(s32[1,1]{1,0:T(1,128)} %bitcast.blk_ref, bf16[2,128,512]{2,1,0:T(8,128)(2,1)S(1)} %analysis.12.refs_0_, bf16[2,128,512]{2,1,0:T(8,128)(2,1)S(1)} %collective-permute-done.17.refs_1_, bf16[2,128,512]{2,1,0:T(8,128)(2,1)S(1)} %collective-permute-done.18.refs_2_, ...), custom_call_target="tpu_custom_call" | custom-call | tf_op jit(solution)/shard_map/update/pallas_call | solution.py:98
  109.6 1.2 %owners.1 = f32[64,256]{1,0:T(8,128)} custom-call(s32[1,1]{1,0:T(1,128)} %bitcast.6.first_ref, f32[512,256]{1,0:T(8,128)S(1)} %join.7.rows_ref), custom_call_target="tpu_custom_call" | custom-call | tf_op jit(solution)/shard_map/owners/pallas_call | solution.py:98
  (69 shorter events, 17.5 us)
Async XLA Ops:
  0.6 11.5 %copy-start.11 = (s32[5]{0:T(128)S(1)}, s32[5]{0:T(128)}, u32[]{:S(2)}) copy-start(s32[5]{0:T(128)} %param.19) | copy-start | bytes 64
  0.6 11.5 %copy-start.12 = (s32[5]{0:T(128)S(1)}, s32[5]{0:T(128)}, u32[]{:S(2)}) copy-start(s32[5]{0:T(128)} %param.21) | copy-start | bytes 64
  0.7 11.5 %copy-start.13 = (f32[125]{0:T(128)S(1)}, f32[125]{0:T(128)}, u32[]{:S(2)}) copy-start(f32[125]{0:T(128)} %param.17) | copy-start | bytes 1504
  2.4 9.8 %copy-start.6 = (f32[125,1]{1,0:T(8,128)S(1)}, f32[125,1]{1,0:T(8,128)}, u32[]{:S(2)}) copy-start(f32[125,1]{1,0:T(8,128)} %constant.29.clone.weight_ref) | copy-start | bytes 1504
  3.1 14.8 %collective-permute-start.2 = (bf16[2,128,512]{2,1,0:T(8,128)(2,1)S(1)}, bf16[2,128,512]{2,1,0:T(8,128)(2,1)S(1)}, u32[]{:S(2)}, u32[]{:S(2)}) collective-permute-start(bf16[2,128,512]{2,1,0:T(8,128)(2,1)S(1)} %get-tuple-element.35.u0_ref), channel_id=1, source_target_pairs={{0,3},{1,2},{2,1},{3,0},{4,7},{5,6},{6,5},{7,4},{8,11},{9,10},{10,... | collective-permute-start | bytes 786440 | tf_op jit(solution)/shard_map/ppermute | solution.py:390
  6.2 11.7 %collective-permute-start.1 = (bf16[2,128,512]{2,1,0:T(8,128)(2,1)S(1)}, bf16[2,128,512]{2,1,0:T(8,128)(2,1)S(1)}, u32[]{:S(2)}, u32[]{:S(2)}) collective-permute-start(bf16[2,128,512]{2,1,0:T(8,128)(2,1)S(1)} %get-tuple-element.35.u0_ref), channel_id=1, source_target_pairs={{0,1},{1,0},{2,3},{3,2},{4,5},{5,4},{6,7},{7,6},{8,9},{9,8},{10,11... | collective-permute-start | bytes 786440 | tf_op jit(solution)/shard_map/ppermute | solution.py:390
  6.3 13.2 %collective-permute-start = (bf16[2,128,512]{2,1,0:T(8,128)(2,1)S(1)}, bf16[2,128,512]{2,1,0:T(8,128)(2,1)}, u32[]{:S(2)}, u32[]{:S(2)}) collective-permute-start(bf16[2,128,512]{2,1,0:T(8,128)(2,1)S(1)} %get-tuple-element.35.u0_ref), channel_id=1, source_target_pairs={{0,2},{1,3},{2,0},{3,1},{4,6},{5,7},{6,4},{7,5},{8,10},{9,11},{10,... | collective-permute-start | bytes 786440 | tf_op jit(solution)/shard_map/ppermute | solution.py:390
  15.1 4.4 %copy-start = (bf16[1024,256]{1,0:T(8,128)(2,1)S(1)}, bf16[1024,256]{1,0:T(8,128)(2,1)}, u32[]{:S(2)}) copy-start(bf16[1024,256]{1,0:T(8,128)(2,1)} %constant.33.clone.sum_cols_ref) | copy-start | bytes 1572868
  15.1 4.4 %copy-start.1 = (bf16[256,384]{1,0:T(8,128)(2,1)S(1)}, bf16[256,384]{1,0:T(8,128)(2,1)}, u32[]{:S(2)}) copy-start(bf16[256,384]{1,0:T(8,128)(2,1)} %constant.30.clone.forward_ref) | copy-start | bytes 589828
  15.1 4.4 %copy-start.2 = (bf16[128,512]{1,0:T(8,128)(2,1)S(1)}, bf16[128,512]{1,0:T(8,128)(2,1)}, u32[]{:S(2)}) copy-start(bf16[128,512]{1,0:T(8,128)(2,1)} %constant.31.clone.backward_ref) | copy-start | bytes 393220
  15.1 4.4 %copy-start.7 = (f32[8,128]{1,0:T(8,128)S(1)}, f32[8,128]{1,0:T(8,128)}, u32[]{:S(2)}) copy-start(f32[8,128]{1,0:T(8,128)} %constant.32.clone.sum_rows_ref) | copy-start | bytes 12292
  24.1 5.2 %collective-permute-start.3 = (bf16[16,1024]{1,0:T(8,128)(2,1)S(1)}, bf16[16,1024]{1,0:T(8,128)(2,1)S(1)}, u32[]{:S(2)}, u32[]{:S(2)}) collective-permute-start(bf16[16,1024]{1,0:T(8,128)(2,1)S(1)} %get-tuple-element.51), channel_id=1, source_target_pairs={{0,4},{4,0},{8,12},{12,8},{16,20},{20,16},{24,28},{28,24},{32,36},... | collective-permute-start | bytes 98312 | tf_op jit(solution)/shard_map/ppermute | solution.py:390
  24.1 7.3 %collective-permute-start.4 = (bf16[16,1024]{1,0:T(8,128)(2,1)S(1)}, bf16[16,1024]{1,0:T(8,128)(2,1)S(1)}, u32[]{:S(2)}, u32[]{:S(2)}) collective-permute-start(bf16[16,1024]{1,0:T(8,128)(2,1)S(1)} %get-tuple-element.52), channel_id=1, source_target_pairs={{4,8},{8,4},{12,16},{16,12},{20,24},{24,20},{28,32},{32,28},{36,40... | collective-permute-start | bytes 98312 | tf_op jit(solution)/shard_map/ppermute | solution.py:395
  34.5 10.8 %collective-permute-start.5 = (bf16[2,128,512]{2,1,0:T(8,128)(2,1)S(1)}, bf16[2,128,512]{2,1,0:T(8,128)(2,1)S(1)}, u32[]{:S(2)}, u32[]{:S(2)}) collective-permute-start(bf16[2,128,512]{2,1,0:T(8,128)(2,1)S(1)} %analysis.9), channel_id=1, source_target_pairs={{0,2},{1,3},{2,0},{3,1},{4,6},{5,7},{6,4},{7,5},{8,10},{9,11},{10,... | collective-permute-start | bytes 786440 | tf_op jit(solution)/shard_map/ppermute | solution.py:390
  36.6 12.0 %collective-permute-start.6 = (bf16[2,128,512]{2,1,0:T(8,128)(2,1)S(1)}, bf16[2,128,512]{2,1,0:T(8,128)(2,1)S(1)}, u32[]{:S(2)}, u32[]{:S(2)}) collective-permute-start(bf16[2,128,512]{2,1,0:T(8,128)(2,1)S(1)} %analysis.10), channel_id=1, source_target_pairs={{0,1},{1,0},{2,3},{3,2},{4,5},{5,4},{6,7},{7,6},{8,9},{9,8},{10,11... | collective-permute-start | bytes 786440 | tf_op jit(solution)/shard_map/ppermute | solution.py:390
  38.3 10.2 %collective-permute-start.7 = (bf16[2,128,512]{2,1,0:T(8,128)(2,1)S(1)}, bf16[2,128,512]{2,1,0:T(8,128)(2,1)S(1)}, u32[]{:S(2)}, u32[]{:S(2)}) collective-permute-start(bf16[2,128,512]{2,1,0:T(8,128)(2,1)S(1)} %analysis.11), channel_id=1, source_target_pairs={{0,3},{1,2},{2,1},{3,0},{4,7},{5,6},{6,5},{7,4},{8,11},{9,10},{10,... | collective-permute-start | bytes 786440 | tf_op jit(solution)/shard_map/ppermute | solution.py:390
  48.9 9.1 %collective-permute-start.10 = (bf16[2,128,512]{2,1,0:T(8,128)(2,1)S(1)}, bf16[2,128,512]{2,1,0:T(8,128)(2,1)S(1)}, u32[]{:S(2)}, u32[]{:S(2)}) collective-permute-start(bf16[2,128,512]{2,1,0:T(8,128)(2,1)S(1)} %get-tuple-element.55.u0_ref), channel_id=1, source_target_pairs={{0,3},{1,2},{2,1},{3,0},{4,7},{5,6},{6,5},{7,4},{8,11},{9,10},{10,... | collective-permute-start | bytes 786440 | tf_op jit(solution)/shard_map/ppermute | solution.py:390
  51.6 9.2 %collective-permute-start.9 = (bf16[2,128,512]{2,1,0:T(8,128)(2,1)S(1)}, bf16[2,128,512]{2,1,0:T(8,128)(2,1)S(1)}, u32[]{:S(2)}, u32[]{:S(2)}) collective-permute-start(bf16[2,128,512]{2,1,0:T(8,128)(2,1)S(1)} %get-tuple-element.55.u0_ref), channel_id=1, source_target_pairs={{0,1},{1,0},{2,3},{3,2},{4,5},{5,4},{6,7},{7,6},{8,9},{9,8},{10,11... | collective-permute-start | bytes 786440 | tf_op jit(solution)/shard_map/ppermute | solution.py:390
  51.6 13.4 %collective-permute-start.8 = (bf16[2,128,512]{2,1,0:T(8,128)(2,1)S(1)}, bf16[2,128,512]{2,1,0:T(8,128)(2,1)S(1)}, u32[]{:S(2)}, u32[]{:S(2)}) collective-permute-start(bf16[2,128,512]{2,1,0:T(8,128)(2,1)S(1)} %get-tuple-element.55.u0_ref), channel_id=1, source_target_pairs={{0,2},{1,3},{2,0},{3,1},{4,6},{5,7},{6,4},{7,5},{8,10},{9,11},{10,... | collective-permute-start | bytes 786440 | tf_op jit(solution)/shard_map/ppermute | solution.py:390
  69.1 13.0 %collective-permute-start.14 = (bf16[16,1024]{1,0:T(8,128)(2,1)S(1)}, bf16[16,1024]{1,0:T(8,128)(2,1)S(1)}, u32[]{:S(2)}, u32[]{:S(2)}) collective-permute-start(bf16[16,1024]{1,0:T(8,128)(2,1)S(1)} %get-tuple-element.61), channel_id=1, source_target_pairs={{0,4},{4,0},{8,12},{12,8},{16,20},{20,16},{24,28},{28,24},{32,36},... | collective-permute-start | bytes 98312 | tf_op jit(solution)/shard_map/ppermute | solution.py:390
  69.1 13.0 %collective-permute-start.15 = (bf16[16,1024]{1,0:T(8,128)(2,1)S(1)}, bf16[16,1024]{1,0:T(8,128)(2,1)S(1)}, u32[]{:S(2)}, u32[]{:S(2)}) collective-permute-start(bf16[16,1024]{1,0:T(8,128)(2,1)S(1)} %get-tuple-element.62), channel_id=1, source_target_pairs={{4,8},{8,4},{12,16},{16,12},{20,24},{24,20},{28,32},{32,28},{36,40... | collective-permute-start | bytes 98312 | tf_op jit(solution)/shard_map/ppermute | solution.py:395
  75.0 3.7 %collective-permute-start.13 = (f32[8,256]{1,0:T(8,128)S(1)}, f32[8,256]{1,0:T(8,128)S(1)}, u32[]{:S(2)}, u32[]{:S(2)}) collective-permute-start(f32[8,256]{1,0:T(8,128)S(1)} %get-tuple-element.59.refs_0_), channel_id=1, source_target_pairs={{0,96},{4,100},{8,104},{12,108},{16,112},{20,116},{24,120},{28,124... | collective-permute-start | bytes 24584 | tf_op jit(solution)/shard_map/ppermute | solution.py:390
  76.1 4.5 %collective-permute-start.12 = (f32[8,256]{1,0:T(8,128)S(1)}, f32[8,256]{1,0:T(8,128)S(1)}, u32[]{:S(2)}, u32[]{:S(2)}) collective-permute-start(f32[8,256]{1,0:T(8,128)S(1)} %get-tuple-element.59.refs_0_), channel_id=1, source_target_pairs={{0,64},{4,68},{8,72},{12,76},{16,80},{20,84},{24,88},{28,92},{32,9... | collective-permute-start | bytes 24584 | tf_op jit(solution)/shard_map/ppermute | solution.py:390
  78.5 3.7 %collective-permute-start.11 = (f32[8,256]{1,0:T(8,128)S(1)}, f32[8,256]{1,0:T(8,128)S(1)}, u32[]{:S(2)}, u32[]{:S(2)}) collective-permute-start(f32[8,256]{1,0:T(8,128)S(1)} %get-tuple-element.59.refs_0_), channel_id=1, source_target_pairs={{0,32},{4,36},{8,40},{12,44},{16,48},{20,52},{24,56},{28,60},{32,0... | collective-permute-start | bytes 24584 | tf_op jit(solution)/shard_map/ppermute | solution.py:390
  83.7 11.3 %collective-permute-start.17 = (bf16[2,128,512]{2,1,0:T(8,128)(2,1)S(1)}, bf16[2,128,512]{2,1,0:T(8,128)(2,1)S(1)}, u32[]{:S(2)}, u32[]{:S(2)}) collective-permute-start(bf16[2,128,512]{2,1,0:T(8,128)(2,1)S(1)} %analysis.13), channel_id=1, source_target_pairs={{0,2},{1,3},{2,0},{3,1},{4,6},{5,7},{6,4},{7,5},{8,10},{9,11},{10,... | collective-permute-start | bytes 786440 | tf_op jit(solution)/shard_map/ppermute | solution.py:390
  85.5 7.8 %collective-permute-start.16 = (f32[32,256]{1,0:T(8,128)S(1)}, f32[32,256]{1,0:T(8,128)S(1)}, u32[]{:S(2)}, u32[]{:S(2)}) collective-permute-start(f32[32,256]{1,0:T(8,128)S(1)} %join.4.refs_0_), channel_id=1, source_target_pairs={{0,128},{4,132},{8,136},{12,140},{16,144},{20,148},{24,152},{28,15... | collective-permute-start | bytes 98312 | tf_op jit(solution)/shard_map/ppermute | solution.py:390
  94.9 6.5 %collective-permute-start.22 = (f32[64,256]{1,0:T(8,128)S(1)}, f32[64,256]{1,0:T(8,128)S(1)}, u32[]{:S(2)}, u32[]{:S(2)}) collective-permute-start(f32[64,256]{1,0:T(8,128)S(1)} %join.5.refs_0_), channel_id=1, source_target_pairs={{0,24},{4,28},{8,16},{12,20},{16,8},{20,12},{24,0},{28,4},{32,56},... | collective-permute-start | bytes 196616 | tf_op jit(solution)/shard_map/ppermute | solution.py:390
  95.0 6.4 %collective-permute-start.21 = (f32[64,256]{1,0:T(8,128)S(1)}, f32[64,256]{1,0:T(8,128)S(1)}, u32[]{:S(2)}, u32[]{:S(2)}) collective-permute-start(f32[64,256]{1,0:T(8,128)S(1)} %join.5.refs_0_), channel_id=1, source_target_pairs={{0,16},{4,20},{8,24},{12,28},{16,0},{20,4},{24,8},{28,12},{32,48},... | collective-permute-start | bytes 196616 | tf_op jit(solution)/shard_map/ppermute | solution.py:390
  95.3 6.8 %collective-permute-start.20 = (f32[64,256]{1,0:T(8,128)S(1)}, f32[64,256]{1,0:T(8,128)S(1)}, u32[]{:S(2)}, u32[]{:S(2)}) collective-permute-start(f32[64,256]{1,0:T(8,128)S(1)} %join.5.refs_0_), channel_id=1, source_target_pairs={{0,8},{4,12},{8,0},{12,4},{16,24},{20,28},{24,16},{28,20},{32,40},... | collective-permute-start | bytes 196616 | tf_op jit(solution)/shard_map/ppermute | solution.py:390
  99.1 6.4 %collective-permute-start.18 = (bf16[2,128,512]{2,1,0:T(8,128)(2,1)S(1)}, bf16[2,128,512]{2,1,0:T(8,128)(2,1)S(1)}, u32[]{:S(2)}, u32[]{:S(2)}) collective-permute-start(bf16[2,128,512]{2,1,0:T(8,128)(2,1)S(1)} %analysis.14), channel_id=1, source_target_pairs={{0,1},{1,0},{2,3},{3,2},{4,5},{5,4},{6,7},{7,6},{8,9},{9,8},{10,11... | collective-permute-start | bytes 786440 | tf_op jit(solution)/shard_map/ppermute | solution.py:390
  100.9 7.6 %collective-permute-start.19 = (bf16[2,128,512]{2,1,0:T(8,128)(2,1)S(1)}, bf16[2,128,512]{2,1,0:T(8,128)(2,1)S(1)}, u32[]{:S(2)}, u32[]{:S(2)}) collective-permute-start(bf16[2,128,512]{2,1,0:T(8,128)(2,1)S(1)} %analysis.15), channel_id=1, source_target_pairs={{0,3},{1,2},{2,1},{3,0},{4,7},{5,6},{6,5},{7,4},{8,11},{9,10},{10,... | collective-permute-start | bytes 786440 | tf_op jit(solution)/shard_map/ppermute | solution.py:390
  102.1 7.5 %collective-permute-start.23 = (f32[256,256]{1,0:T(8,128)S(1)}, f32[256,256]{1,0:T(8,128)S(1)}, u32[]{:S(2)}, u32[]{:S(2)}) collective-permute-start(f32[256,256]{1,0:T(8,128)S(1)} %join.6.refs_0_), channel_id=1, source_target_pairs={{0,4},{4,0},{8,12},{12,8},{16,20},{20,16},{24,28},{28,24},{32,36},... | collective-permute-start | bytes 786440 | tf_op jit(solution)/shard_map/ppermute | solution.py:390
  (6 other events, 8.7 us)

commit v3 on v2

v3 whole, which is shorter than its diff:
```python
import functools
import math

import jax
import jax.numpy as jnp
import numpy as np
from jax import lax
from jax.experimental import pallas as pl
from jax.experimental.pallas import tpu as pltpu
from jax.sharding import PartitionSpec as P

MAXO = 2048
STEPS = 2
PIECES = 2
PTS = 128
ELEM_ROWS = 8
ID_ROW = 5
TABLE_STRIDE = 64
FLOPS_US = 1150000000
PARTNERS = (0, 2, 1, 3)

time_step_sq = 0.0004
kernel_scale = 0.0001
bucket_orders = (8, 64, 512, 2048)

f32 = jnp.float32
bf16 = jnp.bfloat16


def gll_tables():
    nodes = np.array([-1.0, -math.sqrt(3.0 / 7.0), 0.0, math.sqrt(3.0 / 7.0), 1.0])
    weights_line = np.array([0.1, 49.0 / 90.0, 32.0 / 45.0, 49.0 / 90.0, 0.1])
    legendre = (35.0 * nodes**4 - 30.0 * nodes**2 + 3.0) / 8.0
    deriv = np.zeros((5, 5))
    for row_index in range(5):
        for col_index in range(5):
            if row_index != col_index:
                deriv[row_index, col_index] = (
                    legendre[row_index]
                    / legendre[col_index]
                    / (nodes[row_index] - nodes[col_index])
                )
    deriv[0, 0] = -5.0
    deriv[4, 4] = 5.0
    return (deriv, np.outer(weights_line, weights_line).reshape(25))


def split_const(x):
    high = np.asarray(x, np.float32).astype(bf16)
    low = (np.asarray(x, np.float32) - high.astype(np.float32)).astype(bf16)
    return high, low


def derivative_matrices(elements):
    deriv, _ = gll_tables()
    along_s = np.zeros((PTS, PTS))
    along_z = np.zeros((PTS, PTS))
    for e in range(elements):
        base = slice(25 * e, 25 * e + 25)
        along_s[base, base] = np.kron(deriv, np.eye(5))
        along_z[base, base] = np.kron(np.eye(5), deriv)
    both = np.concatenate([along_s, along_z])
    high, low = split_const(both)
    forward = np.concatenate([high, high, low], axis=1)
    high_t, low_t = split_const(both.T)
    return forward, np.concatenate([high_t, low_t], axis=1)


def small_tables(samples):
    coarse = TABLE_STRIDE * np.arange(MAXO // TABLE_STRIDE)
    every = np.concatenate([coarse, np.arange(TABLE_STRIDE)])
    angle = (every[:, None] * np.arange(samples)[None, :] % (2 * MAXO)) * (math.pi / MAXO)
    return np.stack([np.cos(angle), np.sin(angle)]).astype(np.float32)


def table_kernel(blk_ref, small_ref, out_ref, fine_ref):
    coarse = MAXO // TABLE_STRIDE
    quarters = lax.broadcasted_iota(jnp.int32, (TABLE_STRIDE, 1), 0) * blk_ref[0, 0]
    quarters = jnp.bitwise_and(quarters, 3)
    by_cos = jnp.where(quarters == 0, 1.0, jnp.where(quarters == 2, -1.0, 0.0))
    by_sin = jnp.where(quarters == 1, 1.0, jnp.where(quarters == 3, -1.0, 0.0))
    fine_cos, fine_sin = small_ref[0, coarse:, :], small_ref[1, coarse:, :]
    fine_ref[0] = fine_cos * by_cos - fine_sin * by_sin
    fine_ref[1] = fine_sin * by_cos + fine_cos * by_sin

    def one(a, carry):
        big_cos = small_ref[0, pl.ds(a, 1), :]
        big_sin = small_ref[1, pl.ds(a, 1), :]
        start = pl.multiple_of(a * TABLE_STRIDE, TABLE_STRIDE)
        for part in range(0, TABLE_STRIDE, 16):
            fine_cos = fine_ref[0, part : part + 16, :]
            fine_sin = fine_ref[1, part : part + 16, :]
            rows = pl.ds(pl.multiple_of(start + part, 16), 16)
            out_ref[0, rows, :] = (big_cos * fine_cos - big_sin * fine_sin).astype(bf16)
            out_ref[1, rows, :] = (big_sin * fine_cos + big_cos * fine_sin).astype(bf16)
        return carry

    lax.fori_loop(0, coarse, one, 0)


VMEM = pl.BlockSpec(memory_space=pltpu.VMEM)
SMEM = pl.BlockSpec(memory_space=pltpu.SMEM)


def call(kernel, name, out_shape, operands, scalars=0, scratch=(), us=1.0):
    single = not isinstance(out_shape, (list, tuple))
    return pl.pallas_call(
        kernel,
        in_specs=[SMEM] * scalars + [VMEM] * (len(operands) - scalars),
        out_specs=VMEM if single else [VMEM] * len(out_shape),
        out_shape=out_shape,
        scratch_shapes=list(scratch),
        name=name,
        compiler_params=pltpu.CompilerParams(vmem_limit_bytes=16 * 1024 * 1024),
        cost_estimate=pl.CostEstimate(flops=int(us * FLOPS_US), bytes_accessed=0, transcendentals=0),
    )(*operands)


def block_start(blk_ref, bits, count):
    blk = blk_ref[0, 0]
    partner = (blk, blk + 1 - 2 * lax.rem(blk, 2), lax.rem(blk + 2, 4), 3 - blk)[bits]
    return pl.multiple_of(partner * count, count)


def fourier_table(blk, samples):
    shape = jax.ShapeDtypeStruct((2, MAXO, samples), bf16)
    small = jnp.asarray(small_tables(samples))
    return call(table_kernel, "table", shape, [blk, small], 1, [pltpu.VMEM((2, TABLE_STRIDE, samples), f32)])


def dot(a, b):
    return jnp.dot(a, b, preferred_element_type=f32)


def dot_t(a, b):
    return lax.dot_general(a, b, (((1,), (1,)), ((), ())), preferred_element_type=f32)


def exact_dot(a, b):
    return jnp.dot(a, b, preferred_element_type=f32, precision=lax.Precision.HIGHEST)


def levels_of(bucket_ref, points):
    point = lax.broadcasted_iota(jnp.int32, (points, 1), 0)
    level = jnp.zeros((points, 1), jnp.int32)
    for e in range(bucket_ref.shape[1]):
        value = jnp.int32(0)
        for position, orders in enumerate(bucket_orders):
            value = jnp.where(bucket_ref[0, e] == position, orders, value)
        level = jnp.where((point >= 25 * e) & (point < 25 * e + 25), value, level)
    return level


def arrange_kernel(blk_ref, bucket_hbm, disp_hbm, now_ref, *rest):
    *send_ref, disp_ref, bucket_ref, sems = rest
    points, _, count = disp_ref.shape
    buckets = pltpu.make_async_copy(bucket_hbm, bucket_ref, sems.at[0])
    field = pltpu.make_async_copy(disp_hbm, disp_ref, sems.at[1])
    buckets.start()
    field.start()
    now_ref[:, points:, :] = jnp.zeros((2, now_ref.shape[1] - points, count), f32)
    buckets.wait()
    order = lax.broadcasted_iota(jnp.int32, (points, count), 1) + blk_ref[0, 0] * count
    inside = order < levels_of(bucket_ref, points)
    field.wait()
    for c in range(2):
        kept = inside if c == 0 else inside & (order >= 1)
        now_ref[c, :points, :] = jnp.where(kept, disp_ref[:, c, :], 0.0)
    for i, s_ref in enumerate(send_ref):
        width = s_ref.shape[2]
        s_ref[...] = now_ref[:, :, i * width : (i + 1) * width].astype(bf16)


def arrange(blk, buckets, disp, pieces):
    shape = (2, PTS, disp.shape[2])
    sent = [jax.ShapeDtypeStruct((2, PTS, disp.shape[2] // pieces), bf16)] * pieces if pieces else []
    hbm = pl.BlockSpec(memory_space=pltpu.HBM)
    return pl.pallas_call(
        arrange_kernel,
        in_specs=[SMEM, hbm, hbm],
        out_specs=[VMEM] * (1 + pieces),
        out_shape=[jax.ShapeDtypeStruct(shape, f32), *sent],
        scratch_shapes=[
            pltpu.VMEM(disp.shape, f32),
            pltpu.SMEM(buckets.shape, jnp.int32),
            pltpu.SemaphoreType.DMA((2,)),
        ],
        name="arrange",
        compiler_params=pltpu.CompilerParams(vmem_limit_bytes=16 * 1024 * 1024),
    )(blk, buckets, disp)


def setup_kernel(bucket_ref, region_ref, radius_ref, weight_ref, column_ref, density_ref):
    points = radius_ref.shape[1]
    square = (points, points)
    diagonal = lax.broadcasted_iota(jnp.int32, square, 0) == lax.broadcasted_iota(jnp.int32, square, 1)
    radius = jnp.sum(jnp.where(diagonal, radius_ref[...], 0.0), axis=1, keepdims=True)
    weight = weight_ref[...] * radius
    column_ref[...] = jnp.zeros(column_ref.shape, f32)
    column_ref[:points, 0:1] = 1.0 / radius
    column_ref[:points, 1:2] = weight * (2.0 * math.pi / (2 * MAXO))
    column_ref[:points, 2:3] = levels_of(bucket_ref, points).astype(f32)
    column_ref[:points, 3:4] = time_step_sq / (weight * math.pi)
    shape = density_ref.shape
    row, lane = lax.broadcasted_iota(jnp.int32, shape, 0), lax.broadcasted_iota(jnp.int32, shape, 1)
    density = jnp.zeros(shape, f32)
    for e in range(region_ref.shape[1]):
        name = region_ref[0, e].astype(f32)
        density = jnp.where((row == ID_ROW) & (lane == e), name, density)
    density_ref[...] = density


def setup(buckets, regions, radius, weight, sectors):
    outs = [jax.ShapeDtypeStruct((PTS, 4), f32), jax.ShapeDtypeStruct((ELEM_ROWS, sectors), f32)]
    return call(setup_kernel, "setup", outs, [buckets, regions, radius, weight], 2)


def sides(mer_ref):
    here = 1 - lax.rem(mer_ref[0, 0], 2)
    return here, 1 - here


def coefficients_times_table(blk_ref, places, block_refs, table_ref):
    total = 0.0
    for (bits, piece), u_ref in zip(places, block_refs, strict=True):
        count = u_ref.shape[2]
        start = block_start(blk_ref, bits, MAXO // len(PARTNERS))
        start = pl.multiple_of(start + piece * count, count)
        order = (lax.broadcasted_iota(jnp.int32, (1, count), 1) + start).astype(f32)
        u0, u1 = u_ref[0], u_ref[1]
        cosine = jnp.concatenate([u0, (order * u1.astype(f32)).astype(bf16)])
        sine = jnp.concatenate([u1, (-order * u0.astype(f32)).astype(bf16)])
        total += dot(cosine, table_ref[0, pl.ds(start, count), :])
        total += dot(sine, table_ref[1, pl.ds(start, count), :])
    return total


def early_kernel(places, blk_ref, *refs):
    *block_refs, table_ref, phys_ref = refs
    phys_ref[...] = coefficients_times_table(blk_ref, places, block_refs, table_ref)


def early(blk, blocks, table):
    shape = jax.ShapeDtypeStruct((2 * PTS, table.shape[2]), f32)
    kernel = functools.partial(early_kernel, tuple(blocks))
    return call(kernel, "early", shape, [blk, *blocks.values(), table], 1, us=1.3)


def synthesis_kernel(section, places, blk_ref, mer_ref, nodes_ref, *refs):
    (
        *block_refs,
        phys_ref,
        kappa_ref,
        fwd_ref,
        table_ref,
        forward_ref,
        backward_ref,
        column_ref,
        sum_rows_ref,
        sum_cols_ref,
        before_ref,
        stress_ref,
        core_ref,
        chip_ref,
        density_ref,
        dens_ref,
        padded_ref,
    ) = refs
    points, samples = kappa_ref.shape
    inv_radius = column_ref[:, 0:1]
    quad = column_ref[:, 1:2]
    for i in range(4):
        padded_ref[i, PTS - 16 :, :] = jnp.zeros((16, samples), bf16)
        padded_ref[i, :points, :] = fwd_ref[section, i] if i < 3 else kappa_ref[...]
    phys = phys_ref[...] + coefficients_times_table(blk_ref, places, block_refs, table_ref)
    field, around = phys[:PTS], phys[PTS:] * inv_radius
    high = field.astype(bf16)
    low = (field - high.astype(f32)).astype(bf16)
    along = dot(forward_ref[...], jnp.concatenate([high, low, high]))
    along_s, along_z = along[:PTS], along[PTS:]
    modulus = padded_ref[3].astype(f32) * quad
    stress = jnp.concatenate([along_s * modulus, along_z * modulus]).astype(bf16)
    stress_ref[:PTS] = dot(backward_ref[...], jnp.concatenate([stress, stress]))
    stress_ref[PTS:] = around * modulus * inv_radius
    dens = (
        along_s * padded_ref[0].astype(f32)
        + along_z * padded_ref[1].astype(f32)
        + around * padded_ref[2].astype(f32)
    ) * (quad * kernel_scale)
    dens_high = dens.astype(bf16)
    dens_ref[:PTS] = dens_high
    dens_ref[PTS:] = (dens - dens_high.astype(f32)).astype(bf16)
    by_sector = dot(dens_ref[...], sum_cols_ref[...])
    density = before_ref[...] + exact_dot(sum_rows_ref[...], by_sector[:PTS] + by_sector[PTS:])
    density_ref[...] = density
    spare = jnp.zeros((8 - nodes_ref.shape[1], samples), f32)
    for o_ref, side in zip((core_ref, chip_ref), sides(mer_ref)):
        for part in range(2):
            rows = [stress_ref[pl.ds(PTS * part + nodes_ref[side, k], 1), :] for k in range(nodes_ref.shape[1])]
            o_ref[8 * part : 8 * part + 8, :] = jnp.concatenate([*rows, spare])


def synthesis(section, blk, mer, nodes, blocks, phys, kappa, fwd, table, consts, columns, before):
    forward, backward, sum_rows, sum_cols = consts
    samples = kappa.shape[1]
    outs = [
        jax.ShapeDtypeStruct((2 * PTS, samples), f32),
        jax.ShapeDtypeStruct((16, samples), f32),
        jax.ShapeDtypeStruct((16, samples), f32),
        jax.ShapeDtypeStruct(before.shape, f32),
    ]
    scratch = [
        pltpu.VMEM((2 * PTS, samples), bf16),
        pltpu.VMEM((4, PTS, samples), bf16),
    ]
    operands = [blk, mer, nodes, *blocks.values(), phys, kappa, fwd, table, forward, backward, columns, sum_rows, sum_cols, before]
    return call(functools.partial(synthesis_kernel, section, tuple(blocks)), "synthesis", outs, operands, 3, scratch, us=3.0)


def merge_kernel(mer_ref, nodes_ref, stress_ref, core_ref, chip_ref, out_ref, total_ref):
    total_ref[...] = stress_ref[...]
    for r_ref, side in zip((core_ref, chip_ref), sides(mer_ref)):
        rows = r_ref[...]
        for part in range(2):
            for k in range(nodes_ref.shape[1]):
                at = 8 * part + k
                total_ref[pl.ds(PTS * part + nodes_ref[side, k], 1), :] += rows[at : at + 1]
    out_ref[...] = total_ref[...].astype(bf16)


def merge(mer, nodes, stress, core, chip):
    shape = jax.ShapeDtypeStruct(stress.shape, bf16)
    scratch = [pltpu.VMEM(stress.shape, f32)]
    return call(merge_kernel, "merge", shape, [mer, nodes, stress, core, chip], 2, scratch, us=0.8)


def analysis_kernel(bits, piece, blk_ref, stress_ref, table_ref, o_ref):
    count = o_ref.shape[2]
    start = block_start(blk_ref, bits, MAXO // len(PARTNERS))
    start = pl.multiple_of(start + piece * count, count)
    order = (lax.broadcasted_iota(jnp.int32, (1, count), 1) + start).astype(f32)
    cosine = dot_t(stress_ref[...], table_ref[0, pl.ds(start, count), :])
    sine = dot_t(stress_ref[...], table_ref[1, pl.ds(start, count), :])
    o_ref[0] = (cosine[:PTS] - order * sine[PTS:]).astype(bf16)
    o_ref[1] = (sine[:PTS] + order * cosine[PTS:]).astype(bf16)


def analysis(bits, piece, blk, stress, table, count, us=0.75):
    shape = jax.ShapeDtypeStruct((2, PTS, count), bf16)
    kernel = functools.partial(analysis_kernel, bits, piece)
    return call(kernel, "analysis", shape, [blk, stress, table], 1, us=us)


def next_values(c, cols, total, parts, now, prev, column_ref, first_order):
    order = lax.broadcasted_iota(jnp.int32, now.shape, 1) + (first_order + cols.start)
    level = column_ref[:, 2:3]
    scale = column_ref[:, 3:4]
    gain = jnp.where(order == 0, scale * (0.5 if c == 0 else 0.0), scale)
    gain = jnp.where(order.astype(f32) < level, gain, 0.0)
    force = sum(p.astype(f32) for p in parts)
    return 2.0 * now - prev - gain * force


def update_kernel(piece, blk_ref, a_ref, b_ref, c_ref, d_ref, now_ref, prev_ref, column_ref, next_ref, send_ref):
    total, width = now_ref.shape[2], next_ref.shape[2]
    cols = slice(piece * width, (piece + 1) * width)
    for c in range(2):
        parts = [p[c] for p in (a_ref, b_ref, c_ref, d_ref)]
        now, prev = now_ref[c, :, cols], prev_ref[c, :, cols]
        value = next_values(c, cols, total, parts, now, prev, column_ref, blk_ref[0, 0] * total)
        next_ref[c] = value
        send_ref[c] = value.astype(bf16)


def update(piece, blk, parts, now, prev, columns):
    outs = [jax.ShapeDtypeStruct(parts[0].shape, f32), jax.ShapeDtypeStruct(parts[0].shape, bf16)]
    kernel = functools.partial(update_kernel, piece)
    return call(kernel, "update", outs, [blk, *parts, now, prev, columns], 1, us=0.3)


def finish_kernel(blk_ref, a_ref, b_ref, c_ref, d_ref, *refs):
    *now_refs, prev_ref, column_ref, out_ref = refs
    points, _, total = out_ref.shape
    width = now_refs[0].shape[2]
    for i, now_ref in enumerate(now_refs):
        cols = slice(i * width, (i + 1) * width)
        for c in range(2):
            parts = [p[c, :, cols] for p in (a_ref, b_ref, c_ref, d_ref)]
            prev = prev_ref[c, :, cols]
            value = next_values(c, cols, total, parts, now_ref[c], prev, column_ref, blk_ref[0, 0] * total)
            out_ref[:, c, cols] = value[:points]


def finish(blk, parts, now, prev, columns, points):
    shape = jax.ShapeDtypeStruct((points, 2, parts[0].shape[2]), f32)
    return call(finish_kernel, "finish", shape, [blk, *parts, *now, prev, columns], 1, us=1.2)


def join_kernel(*refs):
    rows = refs[0].shape[0]
    for i, ref in enumerate(refs[:-1]):
        refs[-1][i * rows : (i + 1) * rows] = ref[...]


def everywhere(x, piece):
    return {(bits, piece): swapped(x, "blk", bits) if bits else x for bits in PARTNERS}


def join(*pieces):
    shape = jax.ShapeDtypeStruct((len(pieces) * pieces[0].shape[0], pieces[0].shape[1]), f32)
    return call(join_kernel, "join", shape, pieces, us=0.35)


def joined(x, *bits):
    return join(x, *[swapped(x, "mer", b) for b in bits])


def owners_kernel(first_ref, *refs):
    *row_refs, out_ref = refs
    regions = out_ref.shape[0]
    total = jnp.zeros(out_ref.shape, f32)
    for rows_ref in row_refs:
        rows = rows_ref[...]
        count = rows.shape[0]
        names = rows[:, :128].reshape(count // ELEM_ROWS, ELEM_ROWS, 128)
        names = jnp.broadcast_to(names[:, ID_ROW : ID_ROW + 1], names.shape)
        element = lax.broadcasted_iota(jnp.int32, names.shape, 1)
        lane = lax.broadcasted_iota(jnp.int32, names.shape, 2)
        ids = jnp.sum(jnp.where((lane == element) & (element < ID_ROW), names, 0.0), axis=2, keepdims=True)
        ids = jnp.where(element[:, :, :1] < ID_ROW, ids, -1.0).reshape(count, 1)
        mine = (lax.broadcasted_iota(jnp.int32, (count, regions), 1) + first_ref[0, 0]).astype(f32)
        total = total + lax.dot_general(
            jnp.where(ids == mine, 1.0, 0.0),
            rows,
            (((0,), (0,)), ((), ())),
            preferred_element_type=f32,
            precision=lax.Precision.HIGHEST,
        )
    out_ref[...] = total


def owners(first, halves, regions):
    shape = jax.ShapeDtypeStruct((regions, halves[0].shape[1]), f32)
    return call(owners_kernel, "owners", shape, [first, *halves], 1, us=1.2)


def swapped(x, axis, bits):
    return lax.ppermute(x, axis, [(i, i ^ bits) for i in range(lax.axis_size(axis))])


def across_chips(x):
    ends = range(1, lax.axis_size("mer") - 1)
    return lax.ppermute(x, "mer", [(i, i + 1 if i % 2 else i - 1) for i in ends])


def tied(x, other):
    return lax.optimization_barrier((x, other))[0]


def local(disp_now, disp_prev, kappa, radius, fwd_strain, order_bucket, shared_nodes, region_map):
    points, _, count = disp_now.shape
    elements = order_bucket.shape[0]
    samp_count = kappa.shape[1]
    nphi = 2 * MAXO
    sectors = samp_count // 4
    regions = 4096 // lax.axis_size("mer")
    blk_index = lax.axis_index("blk").astype(jnp.int32)
    blk = blk_index.reshape(1, 1)
    mer = lax.axis_index("mer").astype(jnp.int32).reshape(1, 1)
    first = (lax.axis_index("mer").astype(jnp.int32) * regions).reshape(1, 1)
    buckets = order_bucket.reshape(1, -1)
    nodes = shared_nodes[0]
    in_hbm = lambda x: pltpu.with_memory_space_constraint(x, pltpu.HBM)
    buckets, disp_now, disp_prev = in_hbm(buckets), in_hbm(disp_now), in_hbm(disp_prev)
    current, send = arrange(blk, buckets, disp_now, 1)
    (previous,) = arrange(blk, buckets, disp_prev, 0)
    _, gllw = gll_tables()
    weight = jnp.asarray(np.tile(gllw, elements).reshape(-1, 1), f32)
    columns, density = setup(
        buckets, in_hbm(region_map.reshape(1, -1)), in_hbm(radius.reshape(1, -1)), in_hbm(weight), sectors
    )
    forward, backward = derivative_matrices(elements)
    sum_rows = np.zeros((ELEM_ROWS, PTS), np.float32)
    for e in range(elements):
        sum_rows[e, 25 * e : 25 * e + 25] = 1.0
    sum_cols = np.kron(np.eye(sectors), np.ones((4, 1))).astype(bf16)
    consts = tuple(jnp.asarray(x) for x in (forward, backward, sum_rows, sum_cols))
    blocks = everywhere(send, 0)
    fwd, columns, density, table_blk = lax.optimization_barrier((fwd_strain, columns, density, blk))
    table = fourier_table(table_blk, samp_count)

    late = {place: blocks.pop(place) for place in ((1, 0), (3, 0))}
    phys = early(blk, blocks, table)
    stress, core, chip, density = synthesis(
        0, blk, mer, nodes, late, phys, kappa, fwd, table, consts, columns, density
    )
    chip, core = across_chips(chip), swapped(core, "mer", 1)
    stress = merge(mer, nodes, stress, core, chip)
    pieces = range(PIECES)
    forces = [
        {bits: analysis(bits, h, blk, stress, table, count // len(pieces), us=0.05) for bits in (2, 1, 3, 0)}
        for h in pieces
    ]
    middle, blocks = [], []
    for h in pieces:
        parts = [forces[h][0]] + [swapped(forces[h][bits], "blk", bits) for bits in PARTNERS[1:]]
        following, send = update(h, blk, parts, current, previous, columns)
        middle.append(following)
        blocks.append(everywhere(send, h))

    stress, core, chip, density = synthesis(
        1, blk, mer, nodes, blocks[1], early(blk, blocks[0], table), kappa, fwd, table, consts, columns, density
    )
    chip, core = across_chips(chip), swapped(core, "mer", 1)
    gathered = swapped(density, "mer", 8)
    stress = merge(mer, nodes, stress, core, chip)
    forces = {2: analysis(2, 0, blk, stress, table, count)}
    gathered = join(tied(density, forces[2]), gathered)
    forces[1] = analysis(1, 0, blk, tied(stress, gathered), table, count)
    gathered = joined(gathered, 32)
    forces[3] = analysis(3, 0, blk, stress, table, count)
    gathered = tied(gathered, forces[3])
    forces[0] = analysis(0, 0, blk, tied(stress, gathered), table, count)
    gathered = joined(gathered, 16)
    parts = [forces[0]] + [swapped(forces[bits], "blk", bits) for bits in PARTNERS[1:]]
    gathered = joined(tied(gathered, [parts[1], parts[2], forces[0]]), 2, 4, 6)
    gathered = tied(gathered, parts[3])
    displacement = finish(blk, parts, middle, current, columns, points)
    return (displacement, owners(first, [gathered, swapped(gathered, "mer", 1)], regions))


def solution(mesh):
    in_specs = (
        P("mer", None, "blk"),
        P("mer", None, "blk"),
        P("mer", "blk"),
        P("mer"),
        P(None, None, "mer", "blk"),
        P("mer"),
        P("mer", None, None),
        P("mer"),
    )
    out_specs = (P("mer", None, "blk"), P("mer", "blk"))
    return jax.shard_map(local, mesh=mesh, in_specs=in_specs, out_specs=out_specs, check_vma=False)
```

time: 111 us -> 104 us (0.937)
  the two profiles are of different devices: /device:TPU:192 before, /device:TPU:1 now
where the time goes in v3:
time: 104 us; the launch traced here: 103 us
  starting transfers between devices  54 us (52%)
  Pallas kernels  26.2 us (25%)
  waiting for transfers between devices  21 us (20%)
  local copies, waits for them, and re-layouts  1.23 us (1%)
    ppermute x27, starting transfers between devices, swapped(): lax.ppermute(x, axis, [(i, i ^ bits) for i in range(lax.axis_size(axis))])  45.7 us
    pallas_call x28, Pallas kernels, call(): pl.pallas_call(kernel, in_specs=[SMEM] * scalars + [VMEM] * (len(operands...  23.8 us
    ppermute x27, waiting for transfers between devices, swapped(): lax.ppermute(x, axis, [(i, i ^ bits) for i in range(lax.axis_size(axis))])  18.3 us
    ppermute x2, starting transfers between devices, across_chips(): lax.ppermute(x, 'mer', [(i, i + 1 if i % 2 else i - 1) for i in ends])  8.3 us
    ppermute x2, waiting for transfers between devices, across_chips(): lax.ppermute(x, 'mer', [(i, i + 1 if i % 2 else i - 1) for i in ends])  2.72 us
    pallas_call x2, Pallas kernels, arrange(): pl.pallas_call(arrange_kernel, in_specs=[SMEM, hbm, hbm], out_specs=[VMEM...  2.4 us
  transfers between devices with their start and end apart: 29, of which 9 were waited for; matrix products, arithmetic and copies ran while one was open for 0% of the time, Pallas kernels for 15%

profile of v3, /device:TPU:1, one launch (start us, length us, event | category | flops | bytes accessed | tf_op | source)
XLA Modules:
  0.0 103.4 jit_solution(12560897776491882497)
XLA Ops:
  0.6 1.2 %arrange.2 = (f32[2,128,512]{2,1,0:T(8,128)S(1)}, bf16[2,128,512]{2,1,0:T(8,128)(2,1)S(1)}) custom-call(s32[1,1]{1,0:T(1,128)} %bitcast.blk_ref, s32[1,5]{1,0:T(1,128)} %bitcast.11, f32[125,2,512]{2,1,0:T(2,128)} %disp_hbm.2), custom_call_target="tpu_custom_call" | custom-call | tf_op jit(solution)/shard_map/arrange/pallas_call | solution.py:178
  1.9 3.8 %collective-permute-start.2 = (bf16[2,128,512]{2,1,0:T(8,128)(2,1)S(1)}, bf16[2,128,512]{2,1,0:T(8,128)(2,1)S(1)}, u32[]{:S(2)}, u32[]{:S(2)}) collective-permute-start(bf16[2,128,512]{2,1,0:T(8,128)(2,1)S(1)} %get-tuple-element.28.refs_0_), channel_id=1, source_target_pairs={{0,2},{1,3},{2,0},{3,1},{4,6},{5,7},{6,4},{7,5},{8,10},{9,11},{10,... | collective-permute-start | bytes 786440 | tf_op jit(solution)/shard_map/ppermute | solution.py:448
  8.8 2.7 %table.1.refs_2_.refs_5_.table_ref.refs_4_.refs_7_ = bf16[2,2048,1024]{2,1,0:T(8,128)(2,1)S(1)} custom-call(s32[1,1]{1,0:T(1,128)} %bitcast.blk_ref, f32[2,96,1024]{2,1,0:T(8,128)S(1)} %copy-done), custom_call_target="tpu_custom_call" | custom-call | flops 1150000000 | tf_op jit(solution)/shard_map/table/pallas_call | solution.py:107
  11.6 1.2 %early.2.refs_2_ = f32[256,1024]{1,0:T(8,128)S(1)} custom-call(s32[1,1]{1,0:T(1,128)} %bitcast.blk_ref, bf16[2,128,512]{2,1,0:T(8,128)(2,1)S(1)} %get-tuple-element.28.refs_0_, bf16[2,128,512]{2,1,0:T(8,128)(2,1)S(1)} %collective-permute-done.2.refs_1_, bf16[2,2048,1024]{2,1,0:T(8,128)(2,1)S(1)} %table.1.refs_2_.refs_5_.table_ref.refs_4_.refs_7_), custom_call_target="tpu_custom_call" | custom-call | flops 1495000064 | tf_op jit(solution)/shard_map/early/pallas_call | solution.py:107
  12.8 4.7 %collective-permute-done.refs_0_ = bf16[2,128,512]{2,1,0:T(8,128)(2,1)} collective-permute-done((bf16[2,128,512]{2,1,0:T(8,128)(2,1)S(1)}, bf16[2,128,512]{2,1,0:T(8,128)(2,1)}, u32[]{:S(2)}, u32[]{:S(2)}) %collective-permute-start) | collective-permute-done | bytes 262176 | tf_op jit(solution)/shard_map/ppermute | solution.py:448
  17.6 3.3 %synthesis.2 = (f32[256,1024]{1,0:T(8,128)S(1)}, f32[16,1024]{1,0:T(8,128)S(1)}, f32[16,1024]{1,0:T(8,128)S(1)}, f32[8,256]{1,0:T(8,128)S(1)}) custom-call(s32[1,1]{1,0:T(1,128)} %bitcast.blk_ref, s32[1,1]{1,0:T(1,128)} %bitcast.1.mer_ref, s32[2,5]{1,0:T(2,128)S(1)} %bitcast.7, bf16[2,128,512]{2,1,0:T(8,128)(2,1)} %collective-permute-done.refs_0_, ...), custom_call_target="tpu_custom_call" | custom-call | flops 3449999872 | tf_op jit(solution)/shard_map/synthesis/pallas_call | solution.py:107
  20.9 1.6 %collective-permute-start.3 = (f32[16,1024]{1,0:T(8,128)S(1)}, f32[16,1024]{1,0:T(8,128)S(1)}, u32[]{:S(2)}, u32[]{:S(2)}) collective-permute-start(f32[16,1024]{1,0:T(8,128)S(1)} %get-tuple-element.36), channel_id=1, source_target_pairs={{0,4},{4,0},{8,12},{12,8},{16,20},{20,16},{24,28},{28,24},{32,36},... | collective-permute-start | bytes 196616 | tf_op jit(solution)/shard_map/ppermute | solution.py:448
  22.5 3.0 %collective-permute-start.4 = (f32[16,1024]{1,0:T(8,128)S(1)}, f32[16,1024]{1,0:T(8,128)S(1)}, u32[]{:S(2)}, u32[]{:S(2)}) collective-permute-start(f32[16,1024]{1,0:T(8,128)S(1)} %get-tuple-element.37), channel_id=1, source_target_pairs={{4,8},{8,4},{12,16},{16,12},{20,24},{24,20},{28,32},{32,28},{36,40... | collective-permute-start | bytes 196616 | tf_op jit(solution)/shard_map/ppermute | solution.py:453
  25.5 2.6 %collective-permute-done.4.chip_ref = f32[16,1024]{1,0:T(8,128)S(1)} collective-permute-done((f32[16,1024]{1,0:T(8,128)S(1)}, f32[16,1024]{1,0:T(8,128)S(1)}, u32[]{:S(2)}, u32[]{:S(2)}) %collective-permute-start.4) | collective-permute-done | bytes 65568 | tf_op jit(solution)/shard_map/ppermute | solution.py:453
  29.8 2.4 %collective-permute-start.13 = (bf16[2,128,256]{2,1,0:T(8,128)(2,1)S(1)}, bf16[2,128,256]{2,1,0:T(8,128)(2,1)S(1)}, u32[]{:S(2)}, u32[]{:S(2)}) collective-permute-start(bf16[2,128,256]{2,1,0:T(8,128)(2,1)S(1)} %analysis.19), channel_id=1, source_target_pairs={{0,3},{1,2},{2,1},{3,0},{4,7},{5,6},{6,5},{7,4},{8,11},{9,10},{10,... | collective-permute-start | bytes 393224 | tf_op jit(solution)/shard_map/ppermute | solution.py:448
  32.8 1.5 %collective-permute-start.11 = (bf16[2,128,256]{2,1,0:T(8,128)(2,1)S(1)}, bf16[2,128,256]{2,1,0:T(8,128)(2,1)S(1)}, u32[]{:S(2)}, u32[]{:S(2)}) collective-permute-start(bf16[2,128,256]{2,1,0:T(8,128)(2,1)S(1)} %analysis.17), channel_id=1, source_target_pairs={{0,2},{1,3},{2,0},{3,1},{4,6},{5,7},{6,4},{7,5},{8,10},{9,11},{10,... | collective-permute-start | bytes 393224 | tf_op jit(solution)/shard_map/ppermute | solution.py:448
  34.8 2.4 %collective-permute-start.7 = (bf16[2,128,256]{2,1,0:T(8,128)(2,1)S(1)}, bf16[2,128,256]{2,1,0:T(8,128)(2,1)S(1)}, u32[]{:S(2)}, u32[]{:S(2)}) collective-permute-start(bf16[2,128,256]{2,1,0:T(8,128)(2,1)S(1)} %analysis.15), channel_id=1, source_target_pairs={{0,3},{1,2},{2,1},{3,0},{4,7},{5,6},{6,5},{7,4},{8,11},{9,10},{10,... | collective-permute-start | bytes 393224 | tf_op jit(solution)/shard_map/ppermute | solution.py:448
  40.0 1.8 %collective-permute-start.5 = (bf16[2,128,256]{2,1,0:T(8,128)(2,1)S(1)}, bf16[2,128,256]{2,1,0:T(8,128)(2,1)S(1)}, u32[]{:S(2)}, u32[]{:S(2)}) collective-permute-start(bf16[2,128,256]{2,1,0:T(8,128)(2,1)S(1)} %analysis.13), channel_id=1, source_target_pairs={{0,2},{1,3},{2,0},{3,1},{4,6},{5,7},{6,4},{7,5},{8,10},{9,11},{10,... | collective-permute-start | bytes 393224 | tf_op jit(solution)/shard_map/ppermute | solution.py:448
  42.0 1.5 %collective-permute-start.14 = (bf16[2,128,256]{2,1,0:T(8,128)(2,1)S(1)}, bf16[2,128,256]{2,1,0:T(8,128)(2,1)S(1)}, u32[]{:S(2)}, u32[]{:S(2)}) collective-permute-start(bf16[2,128,256]{2,1,0:T(8,128)(2,1)S(1)} %get-tuple-element.40.refs_0_), channel_id=1, source_target_pairs={{0,2},{1,3},{2,0},{3,1},{4,6},{5,7},{6,4},{7,5},{8,10},{9,11},{10,... | collective-permute-start | bytes 393224 | tf_op jit(solution)/shard_map/ppermute | solution.py:448
  43.5 1.4 %collective-permute-start.15 = (bf16[2,128,256]{2,1,0:T(8,128)(2,1)S(1)}, bf16[2,128,256]{2,1,0:T(8,128)(2,1)S(1)}, u32[]{:S(2)}, u32[]{:S(2)}) collective-permute-start(bf16[2,128,256]{2,1,0:T(8,128)(2,1)S(1)} %get-tuple-element.40.refs_0_), channel_id=1, source_target_pairs={{0,1},{1,0},{2,3},{3,2},{4,5},{5,4},{6,7},{7,6},{8,9},{9,8},{10,11... | collective-permute-start | bytes 393224 | tf_op jit(solution)/shard_map/ppermute | solution.py:448
  45.8 1.5 %collective-permute-done.5.b_ref = bf16[2,128,256]{2,1,0:T(8,128)(2,1)S(1)} collective-permute-done((bf16[2,128,256]{2,1,0:T(8,128)(2,1)S(1)}, bf16[2,128,256]{2,1,0:T(8,128)(2,1)S(1)}, u32[]{:S(2)}, u32[]{:S(2)}) %collective-permute-start.5) | collective-permute-done | bytes 131104 | tf_op jit(solution)/shard_map/ppermute | solution.py:448
  48.4 2.1 %collective-permute-start.8 = (bf16[2,128,256]{2,1,0:T(8,128)(2,1)S(1)}, bf16[2,128,256]{2,1,0:T(8,128)(2,1)S(1)}, u32[]{:S(2)}, u32[]{:S(2)}) collective-permute-start(bf16[2,128,256]{2,1,0:T(8,128)(2,1)S(1)} %get-tuple-element.39.refs_0_), channel_id=1, source_target_pairs={{0,2},{1,3},{2,0},{3,1},{4,6},{5,7},{6,4},{7,5},{8,10},{9,11},{10,... | collective-permute-start | bytes 393224 | tf_op jit(solution)/shard_map/ppermute | solution.py:448
  50.9 4.1 %collective-permute-done.16.refs_3_ = bf16[2,128,256]{2,1,0:T(8,128)(2,1)S(1)} collective-permute-done((bf16[2,128,256]{2,1,0:T(8,128)(2,1)S(1)}, bf16[2,128,256]{2,1,0:T(8,128)(2,1)S(1)}, u32[]{:S(2)}, u32[]{:S(2)}) %collective-permute-start.16) | collective-permute-done | bytes 131104 | tf_op jit(solution)/shard_map/ppermute | solution.py:448
  55.0 1.3 %early.3.refs_4_ = f32[256,1024]{1,0:T(8,128)S(1)} custom-call(s32[1,1]{1,0:T(1,128)} %bitcast.blk_ref, bf16[2,128,256]{2,1,0:T(8,128)(2,1)S(1)} %get-tuple-element.40.refs_0_, bf16[2,128,256]{2,1,0:T(8,128)(2,1)S(1)} %collective-permute-done.14.refs_1_, bf16[2,128,256]{2,1,0:T(8,128)(2,1)S(1)} %collective-permute-done.15.refs_2_, ...), custom_call_target="tpu_custom_call" | custom-call | flops 1495000064 | tf_op jit(solution)/shard_map/early/pallas_call | solution.py:107
  56.9 2.9 %synthesis.3 = (f32[256,1024]{1,0:T(8,128)S(1)}, f32[16,1024]{1,0:T(8,128)S(1)}, f32[16,1024]{1,0:T(8,128)S(1)}, f32[8,256]{1,0:T(8,128)S(1)}) custom-call(s32[1,1]{1,0:T(1,128)} %bitcast.blk_ref, s32[1,1]{1,0:T(1,128)} %bitcast.1.mer_ref, s32[2,5]{1,0:T(2,128)S(1)} %bitcast.9, bf16[2,128,256]{2,1,0:T(8,128)(2,1)S(1)} %get-tuple-element.39.refs_0_, ...), custom_call_target="tpu_custom_call" | custom-call | flops 3449999872 | tf_op jit(solution)/shard_map/synthesis/pallas_call | solution.py:107
  59.8 5.3 %collective-permute-start.18 = (f32[16,1024]{1,0:T(8,128)S(1)}, f32[16,1024]{1,0:T(8,128)S(1)}, u32[]{:S(2)}, u32[]{:S(2)}) collective-permute-start(f32[16,1024]{1,0:T(8,128)S(1)} %get-tuple-element.44), channel_id=1, source_target_pairs={{4,8},{8,4},{12,16},{16,12},{20,24},{24,20},{28,32},{32,28},{36,40... | collective-permute-start | bytes 196616 | tf_op jit(solution)/shard_map/ppermute | solution.py:453
  65.1 1.8 %collective-permute-start.19 = (f32[8,256]{1,0:T(8,128)S(1)}, f32[8,256]{1,0:T(8,128)S(1)}, u32[]{:S(2)}, u32[]{:S(2)}) collective-permute-start(f32[8,256]{1,0:T(8,128)S(1)} %get-tuple-element.46.refs_0_), channel_id=1, source_target_pairs={{0,32},{4,36},{8,40},{12,44},{16,48},{20,52},{24,56},{28,60},{32,0... | collective-permute-start | bytes 24584 | tf_op jit(solution)/shard_map/ppermute | solution.py:448
  69.4 1.3 %collective-permute-start.22 = (bf16[2,128,512]{2,1,0:T(8,128)(2,1)S(1)}, bf16[2,128,512]{2,1,0:T(8,128)(2,1)S(1)}, u32[]{:S(2)}, u32[]{:S(2)}) collective-permute-start(bf16[2,128,512]{2,1,0:T(8,128)(2,1)S(1)} %analysis.23), channel_id=1, source_target_pairs={{0,1},{1,0},{2,3},{3,2},{4,5},{5,4},{6,7},{7,6},{8,9},{9,8},{10,11... | collective-permute-start | bytes 786440 | tf_op jit(solution)/shard_map/ppermute | solution.py:448
  70.6 2.2 %collective-permute-start.21 = (bf16[2,128,512]{2,1,0:T(8,128)(2,1)S(1)}, bf16[2,128,512]{2,1,0:T(8,128)(2,1)S(1)}, u32[]{:S(2)}, u32[]{:S(2)}) collective-permute-start(bf16[2,128,512]{2,1,0:T(8,128)(2,1)S(1)} %analysis.20), channel_id=1, source_target_pairs={{0,2},{1,3},{2,0},{3,1},{4,6},{5,7},{6,4},{7,5},{8,10},{9,11},{10,... | collective-permute-start | bytes 786440 | tf_op jit(solution)/shard_map/ppermute | solution.py:448
  72.8 9.9 %collective-permute-start.20 = (f32[16,256]{1,0:T(8,128)S(1)}, f32[16,256]{1,0:T(8,128)S(1)}, u32[]{:S(2)}, u32[]{:S(2)}) collective-permute-start(f32[16,256]{1,0:T(8,128)S(1)} %join.4.refs_0_), channel_id=1, source_target_pairs={{0,128},{4,132},{8,136},{12,140},{16,144},{20,148},{24,152},{28,15... | collective-permute-start | bytes 49160 | tf_op jit(solution)/shard_map/ppermute | solution.py:448
  85.3 2.9 %collective-permute-done.24.refs_1_ = f32[32,256]{1,0:T(8,128)S(1)} collective-permute-done((f32[32,256]{1,0:T(8,128)S(1)}, f32[32,256]{1,0:T(8,128)S(1)}, u32[]{:S(2)}, u32[]{:S(2)}) %collective-permute-start.24) | collective-permute-done | bytes 32800 | tf_op jit(solution)/shard_map/ppermute | solution.py:448
  88.3 5.2 %collective-permute-start.26 = (f32[64,256]{1,0:T(8,128)S(1)}, f32[64,256]{1,0:T(8,128)S(1)}, u32[]{:S(2)}, u32[]{:S(2)}) collective-permute-start(f32[64,256]{1,0:T(8,128)S(1)} %join.6.refs_0_), channel_id=1, source_target_pairs={{0,16},{4,20},{8,24},{12,28},{16,0},{20,4},{24,8},{28,12},{32,48},... | collective-permute-start | bytes 196616 | tf_op jit(solution)/shard_map/ppermute | solution.py:448
  93.5 3.0 %collective-permute-done.26.refs_2_ = f32[64,256]{1,0:T(8,128)S(1)} collective-permute-done((f32[64,256]{1,0:T(8,128)S(1)}, f32[64,256]{1,0:T(8,128)S(1)}, u32[]{:S(2)}, u32[]{:S(2)}) %collective-permute-start.26) | collective-permute-done | bytes 65568 | tf_op jit(solution)/shard_map/ppermute | solution.py:448
  96.6 1.3 %collective-permute-done.27.refs_3_ = f32[64,256]{1,0:T(8,128)S(1)} collective-permute-done((f32[64,256]{1,0:T(8,128)S(1)}, f32[64,256]{1,0:T(8,128)S(1)}, u32[]{:S(2)}, u32[]{:S(2)}) %collective-permute-start.27) | collective-permute-done | bytes 65568 | tf_op jit(solution)/shard_map/ppermute | solution.py:448
  97.9 3.1 %collective-permute-start.28 = (f32[256,256]{1,0:T(8,128)S(1)}, f32[256,256]{1,0:T(8,128)S(1)}, u32[]{:S(2)}, u32[]{:S(2)}) collective-permute-start(f32[256,256]{1,0:T(8,128)S(1)} %join.7.refs_0_), channel_id=1, source_target_pairs={{0,4},{4,0},{8,12},{12,8},{16,20},{20,16},{24,28},{28,24},{32,36},... | collective-permute-start | bytes 786440 | tf_op jit(solution)/shard_map/ppermute | solution.py:448
  101.0 1.2 %finish.1 = f32[125,2,512]{2,1,0:T(2,128)} custom-call(s32[1,1]{1,0:T(1,128)} %bitcast.blk_ref, bf16[2,128,512]{2,1,0:T(8,128)(2,1)S(1)} %analysis.22.a_ref, bf16[2,128,512]{2,1,0:T(8,128)(2,1)S(1)} %collective-permute-done.21.b_ref, bf16[2,128,512]{2,1,0:T(8,128)(2,1)S(1)} %collective-permute-done.22.c_ref, ...), custom_call_target="tpu_custom_call" | custom-call | flops 1380000000 | tf_op jit(solution)/shard_map/finish/pallas_call | solution.py:107
  102.2 1.2 %owners.1 = f32[64,256]{1,0:T(8,128)} custom-call(s32[1,1]{1,0:T(1,128)} %bitcast.6.first_ref, f32[256,256]{1,0:T(8,128)S(1)} %join.7.refs_0_, f32[256,256]{1,0:T(8,128)S(1)} %collective-permute-done.28.refs_1_), custom_call_target="tpu_custom_call" | custom-call | flops 1380000000 | tf_op jit(solution)/shard_map/owners/pallas_call | solution.py:107
  (73 shorter events, 17.0 us)
Async XLA Ops:
  1.9 9.7 %collective-permute-start.2 = (bf16[2,128,512]{2,1,0:T(8,128)(2,1)S(1)}, bf16[2,128,512]{2,1,0:T(8,128)(2,1)S(1)}, u32[]{:S(2)}, u32[]{:S(2)}) collective-permute-start(bf16[2,128,512]{2,1,0:T(8,128)(2,1)S(1)} %get-tuple-element.28.refs_0_), channel_id=1, source_target_pairs={{0,2},{1,3},{2,0},{3,1},{4,6},{5,7},{6,4},{7,5},{8,10},{9,11},{10,... | collective-permute-start | bytes 786440 | tf_op jit(solution)/shard_map/ppermute | solution.py:448
  5.7 11.9 %collective-permute-start = (bf16[2,128,512]{2,1,0:T(8,128)(2,1)S(1)}, bf16[2,128,512]{2,1,0:T(8,128)(2,1)}, u32[]{:S(2)}, u32[]{:S(2)}) collective-permute-start(bf16[2,128,512]{2,1,0:T(8,128)(2,1)S(1)} %get-tuple-element.28.refs_0_), channel_id=1, source_target_pairs={{0,1},{1,0},{2,3},{3,2},{4,5},{5,4},{6,7},{7,6},{8,9},{9,8},{10,11... | collective-permute-start | bytes 786440 | tf_op jit(solution)/shard_map/ppermute | solution.py:448
  6.1 11.5 %collective-permute-start.1 = (bf16[2,128,512]{2,1,0:T(8,128)(2,1)S(1)}, bf16[2,128,512]{2,1,0:T(8,128)(2,1)}, u32[]{:S(2)}, u32[]{:S(2)}) collective-permute-start(bf16[2,128,512]{2,1,0:T(8,128)(2,1)S(1)} %get-tuple-element.28.refs_0_), channel_id=1, source_target_pairs={{0,3},{1,2},{2,1},{3,0},{4,7},{5,6},{6,5},{7,4},{8,11},{9,10},{10,... | collective-permute-start | bytes 786440 | tf_op jit(solution)/shard_map/ppermute | solution.py:448
  11.5 6.1 %copy-start.1 = (bf16[125,1024]{1,0:T(8,128)(2,1)S(1)}, bf16[125,1024]{1,0:T(8,128)(2,1)}, u32[]{:S(2)}) copy-start(bf16[125,1024]{1,0:T(8,128)(2,1)} %refs_5_.1) | copy-start | bytes 768004
  11.5 6.1 %copy-start.2 = (s32[1,2,5]{2,1,0:T(2,128)S(1)}, s32[1,2,5]{2,1,0:T(2,128)}, u32[]{:S(2)}) copy-start(s32[1,2,5]{2,1,0:T(2,128)} %param.20) | copy-start | bytes 124
  11.5 6.1 %copy-start.3 = (bf16[1024,256]{1,0:T(8,128)(2,1)S(1)}, bf16[1024,256]{1,0:T(8,128)(2,1)}, u32[]{:S(2)}) copy-start(bf16[1024,256]{1,0:T(8,128)(2,1)} %constant.27.clone.refs_10_.refs_12_) | copy-start | bytes 1572868
  20.9 4.6 %collective-permute-start.3 = (f32[16,1024]{1,0:T(8,128)S(1)}, f32[16,1024]{1,0:T(8,128)S(1)}, u32[]{:S(2)}, u32[]{:S(2)}) collective-permute-start(f32[16,1024]{1,0:T(8,128)S(1)} %get-tuple-element.36), channel_id=1, source_target_pairs={{0,4},{4,0},{8,12},{12,8},{16,20},{20,16},{24,28},{28,24},{32,36},... | collective-permute-start | bytes 196616 | tf_op jit(solution)/shard_map/ppermute | solution.py:448
  22.5 5.6 %collective-permute-start.4 = (f32[16,1024]{1,0:T(8,128)S(1)}, f32[16,1024]{1,0:T(8,128)S(1)}, u32[]{:S(2)}, u32[]{:S(2)}) collective-permute-start(f32[16,1024]{1,0:T(8,128)S(1)} %get-tuple-element.37), channel_id=1, source_target_pairs={{4,8},{8,4},{12,16},{16,12},{20,24},{24,20},{28,32},{32,28},{36,40... | collective-permute-start | bytes 196616 | tf_op jit(solution)/shard_map/ppermute | solution.py:453
  29.8 10.2 %collective-permute-start.13 = (bf16[2,128,256]{2,1,0:T(8,128)(2,1)S(1)}, bf16[2,128,256]{2,1,0:T(8,128)(2,1)S(1)}, u32[]{:S(2)}, u32[]{:S(2)}) collective-permute-start(bf16[2,128,256]{2,1,0:T(8,128)(2,1)S(1)} %analysis.19), channel_id=1, source_target_pairs={{0,3},{1,2},{2,1},{3,0},{4,7},{5,6},{6,5},{7,4},{8,11},{9,10},{10,... | collective-permute-start | bytes 393224 | tf_op jit(solution)/shard_map/ppermute | solution.py:448
  32.7 9.1 %collective-permute-start.12 = (bf16[2,128,256]{2,1,0:T(8,128)(2,1)S(1)}, bf16[2,128,256]{2,1,0:T(8,128)(2,1)S(1)}, u32[]{:S(2)}, u32[]{:S(2)}) collective-permute-start(bf16[2,128,256]{2,1,0:T(8,128)(2,1)S(1)} %analysis.18), channel_id=1, source_target_pairs={{0,1},{1,0},{2,3},{3,2},{4,5},{5,4},{6,7},{7,6},{8,9},{9,8},{10,11... | collective-permute-start | bytes 393224 | tf_op jit(solution)/shard_map/ppermute | solution.py:448
  32.8 9.0 %collective-permute-start.11 = (bf16[2,128,256]{2,1,0:T(8,128)(2,1)S(1)}, bf16[2,128,256]{2,1,0:T(8,128)(2,1)S(1)}, u32[]{:S(2)}, u32[]{:S(2)}) collective-permute-start(bf16[2,128,256]{2,1,0:T(8,128)(2,1)S(1)} %analysis.17), channel_id=1, source_target_pairs={{0,2},{1,3},{2,0},{3,1},{4,6},{5,7},{6,4},{7,5},{8,10},{9,11},{10,... | collective-permute-start | bytes 393224 | tf_op jit(solution)/shard_map/ppermute | solution.py:448
  34.8 10.2 %collective-permute-start.7 = (bf16[2,128,256]{2,1,0:T(8,128)(2,1)S(1)}, bf16[2,128,256]{2,1,0:T(8,128)(2,1)S(1)}, u32[]{:S(2)}, u32[]{:S(2)}) collective-permute-start(bf16[2,128,256]{2,1,0:T(8,128)(2,1)S(1)} %analysis.15), channel_id=1, source_target_pairs={{0,3},{1,2},{2,1},{3,0},{4,7},{5,6},{6,5},{7,4},{8,11},{9,10},{10,... | collective-permute-start | bytes 393224 | tf_op jit(solution)/shard_map/ppermute | solution.py:448
  38.9 6.9 %collective-permute-start.6 = (bf16[2,128,256]{2,1,0:T(8,128)(2,1)S(1)}, bf16[2,128,256]{2,1,0:T(8,128)(2,1)S(1)}, u32[]{:S(2)}, u32[]{:S(2)}) collective-permute-start(bf16[2,128,256]{2,1,0:T(8,128)(2,1)S(1)} %analysis.14), channel_id=1, source_target_pairs={{0,1},{1,0},{2,3},{3,2},{4,5},{5,4},{6,7},{7,6},{8,9},{9,8},{10,11... | collective-permute-start | bytes 393224 | tf_op jit(solution)/shard_map/ppermute | solution.py:448
  40.0 7.3 %collective-permute-start.5 = (bf16[2,128,256]{2,1,0:T(8,128)(2,1)S(1)}, bf16[2,128,256]{2,1,0:T(8,128)(2,1)S(1)}, u32[]{:S(2)}, u32[]{:S(2)}) collective-permute-start(bf16[2,128,256]{2,1,0:T(8,128)(2,1)S(1)} %analysis.13), channel_id=1, source_target_pairs={{0,2},{1,3},{2,0},{3,1},{4,6},{5,7},{6,4},{7,5},{8,10},{9,11},{10,... | collective-permute-start | bytes 393224 | tf_op jit(solution)/shard_map/ppermute | solution.py:448
  42.0 8.6 %collective-permute-start.14 = (bf16[2,128,256]{2,1,0:T(8,128)(2,1)S(1)}, bf16[2,128,256]{2,1,0:T(8,128)(2,1)S(1)}, u32[]{:S(2)}, u32[]{:S(2)}) collective-permute-start(bf16[2,128,256]{2,1,0:T(8,128)(2,1)S(1)} %get-tuple-element.40.refs_0_), channel_id=1, source_target_pairs={{0,2},{1,3},{2,0},{3,1},{4,6},{5,7},{6,4},{7,5},{8,10},{9,11},{10,... | collective-permute-start | bytes 393224 | tf_op jit(solution)/shard_map/ppermute | solution.py:448
  43.5 7.3 %collective-permute-start.15 = (bf16[2,128,256]{2,1,0:T(8,128)(2,1)S(1)}, bf16[2,128,256]{2,1,0:T(8,128)(2,1)S(1)}, u32[]{:S(2)}, u32[]{:S(2)}) collective-permute-start(bf16[2,128,256]{2,1,0:T(8,128)(2,1)S(1)} %get-tuple-element.40.refs_0_), channel_id=1, source_target_pairs={{0,1},{1,0},{2,3},{3,2},{4,5},{5,4},{6,7},{7,6},{8,9},{9,8},{10,11... | collective-permute-start | bytes 393224 | tf_op jit(solution)/shard_map/ppermute | solution.py:448
  45.0 10.0 %collective-permute-start.16 = (bf16[2,128,256]{2,1,0:T(8,128)(2,1)S(1)}, bf16[2,128,256]{2,1,0:T(8,128)(2,1)S(1)}, u32[]{:S(2)}, u32[]{:S(2)}) collective-permute-start(bf16[2,128,256]{2,1,0:T(8,128)(2,1)S(1)} %get-tuple-element.40.refs_0_), channel_id=1, source_target_pairs={{0,3},{1,2},{2,1},{3,0},{4,7},{5,6},{6,5},{7,4},{8,11},{9,10},{10,... | collective-permute-start | bytes 393224 | tf_op jit(solution)/shard_map/ppermute | solution.py:448
  47.5 9.4 %collective-permute-start.10 = (bf16[2,128,256]{2,1,0:T(8,128)(2,1)S(1)}, bf16[2,128,256]{2,1,0:T(8,128)(2,1)S(1)}, u32[]{:S(2)}, u32[]{:S(2)}) collective-permute-start(bf16[2,128,256]{2,1,0:T(8,128)(2,1)S(1)} %get-tuple-element.39.refs_0_), channel_id=1, source_target_pairs={{0,3},{1,2},{2,1},{3,0},{4,7},{5,6},{6,5},{7,4},{8,11},{9,10},{10,... | collective-permute-start | bytes 393224 | tf_op jit(solution)/shard_map/ppermute | solution.py:448
  48.4 8.5 %collective-permute-start.8 = (bf16[2,128,256]{2,1,0:T(8,128)(2,1)S(1)}, bf16[2,128,256]{2,1,0:T(8,128)(2,1)S(1)}, u32[]{:S(2)}, u32[]{:S(2)}) collective-permute-start(bf16[2,128,256]{2,1,0:T(8,128)(2,1)S(1)} %get-tuple-element.39.refs_0_), channel_id=1, source_target_pairs={{0,2},{1,3},{2,0},{3,1},{4,6},{5,7},{6,4},{7,5},{8,10},{9,11},{10,... | collective-permute-start | bytes 393224 | tf_op jit(solution)/shard_map/ppermute | solution.py:448
  50.6 6.3 %collective-permute-start.9 = (bf16[2,128,256]{2,1,0:T(8,128)(2,1)S(1)}, bf16[2,128,256]{2,1,0:T(8,128)(2,1)S(1)}, u32[]{:S(2)}, u32[]{:S(2)}) collective-permute-start(bf16[2,128,256]{2,1,0:T(8,128)(2,1)S(1)} %get-tuple-element.39.refs_0_), channel_id=1, source_target_pairs={{0,1},{1,0},{2,3},{3,2},{4,5},{5,4},{6,7},{7,6},{8,9},{9,8},{10,11... | collective-permute-start | bytes 393224 | tf_op jit(solution)/shard_map/ppermute | solution.py:448
  59.8 7.1 %collective-permute-start.17 = (f32[16,1024]{1,0:T(8,128)S(1)}, f32[16,1024]{1,0:T(8,128)S(1)}, u32[]{:S(2)}, u32[]{:S(2)}) collective-permute-start(f32[16,1024]{1,0:T(8,128)S(1)} %get-tuple-element.43), channel_id=1, source_target_pairs={{0,4},{4,0},{8,12},{12,8},{16,20},{20,16},{24,28},{28,24},{32,36},... | collective-permute-start | bytes 196616 | tf_op jit(solution)/shard_map/ppermute | solution.py:448
  59.8 7.2 %collective-permute-start.18 = (f32[16,1024]{1,0:T(8,128)S(1)}, f32[16,1024]{1,0:T(8,128)S(1)}, u32[]{:S(2)}, u32[]{:S(2)}) collective-permute-start(f32[16,1024]{1,0:T(8,128)S(1)} %get-tuple-element.44), channel_id=1, source_target_pairs={{4,8},{8,4},{12,16},{16,12},{20,24},{24,20},{28,32},{32,28},{36,40... | collective-permute-start | bytes 196616 | tf_op jit(solution)/shard_map/ppermute | solution.py:453
  65.1 3.5 %collective-permute-start.19 = (f32[8,256]{1,0:T(8,128)S(1)}, f32[8,256]{1,0:T(8,128)S(1)}, u32[]{:S(2)}, u32[]{:S(2)}) collective-permute-start(f32[8,256]{1,0:T(8,128)S(1)} %get-tuple-element.46.refs_0_), channel_id=1, source_target_pairs={{0,32},{4,36},{8,40},{12,44},{16,48},{20,52},{24,56},{28,60},{32,0... | collective-permute-start | bytes 24584 | tf_op jit(solution)/shard_map/ppermute | solution.py:448
  69.4 18.9 %collective-permute-start.22 = (bf16[2,128,512]{2,1,0:T(8,128)(2,1)S(1)}, bf16[2,128,512]{2,1,0:T(8,128)(2,1)S(1)}, u32[]{:S(2)}, u32[]{:S(2)}) collective-permute-start(bf16[2,128,512]{2,1,0:T(8,128)(2,1)S(1)} %analysis.23), channel_id=1, source_target_pairs={{0,1},{1,0},{2,3},{3,2},{4,5},{5,4},{6,7},{7,6},{8,9},{9,8},{10,11... | collective-permute-start | bytes 786440 | tf_op jit(solution)/shard_map/ppermute | solution.py:448
  70.6 17.6 %collective-permute-start.21 = (bf16[2,128,512]{2,1,0:T(8,128)(2,1)S(1)}, bf16[2,128,512]{2,1,0:T(8,128)(2,1)S(1)}, u32[]{:S(2)}, u32[]{:S(2)}) collective-permute-start(bf16[2,128,512]{2,1,0:T(8,128)(2,1)S(1)} %analysis.20), channel_id=1, source_target_pairs={{0,2},{1,3},{2,0},{3,1},{4,6},{5,7},{6,4},{7,5},{8,10},{9,11},{10,... | collective-permute-start | bytes 786440 | tf_op jit(solution)/shard_map/ppermute | solution.py:448
  72.8 11.7 %collective-permute-start.20 = (f32[16,256]{1,0:T(8,128)S(1)}, f32[16,256]{1,0:T(8,128)S(1)}, u32[]{:S(2)}, u32[]{:S(2)}) collective-permute-start(f32[16,256]{1,0:T(8,128)S(1)} %join.4.refs_0_), channel_id=1, source_target_pairs={{0,128},{4,132},{8,136},{12,140},{16,144},{20,148},{24,152},{28,15... | collective-permute-start | bytes 49160 | tf_op jit(solution)/shard_map/ppermute | solution.py:448
  83.5 14.4 %collective-permute-start.23 = (bf16[2,128,512]{2,1,0:T(8,128)(2,1)S(1)}, bf16[2,128,512]{2,1,0:T(8,128)(2,1)S(1)}, u32[]{:S(2)}, u32[]{:S(2)}) collective-permute-start(bf16[2,128,512]{2,1,0:T(8,128)(2,1)S(1)} %analysis.21), channel_id=1, source_target_pairs={{0,3},{1,2},{2,1},{3,0},{4,7},{5,6},{6,5},{7,4},{8,11},{9,10},{10,... | collective-permute-start | bytes 786440 | tf_op jit(solution)/shard_map/ppermute | solution.py:448
  84.5 3.7 %collective-permute-start.24 = (f32[32,256]{1,0:T(8,128)S(1)}, f32[32,256]{1,0:T(8,128)S(1)}, u32[]{:S(2)}, u32[]{:S(2)}) collective-permute-start(f32[32,256]{1,0:T(8,128)S(1)} %join.5.refs_0_), channel_id=1, source_target_pairs={{0,64},{4,68},{8,72},{12,76},{16,80},{20,84},{24,88},{28,92},{32,9... | collective-permute-start | bytes 98312 | tf_op jit(solution)/shard_map/ppermute | solution.py:448
  88.2 5.3 %collective-permute-start.25 = (f32[64,256]{1,0:T(8,128)S(1)}, f32[64,256]{1,0:T(8,128)S(1)}, u32[]{:S(2)}, u32[]{:S(2)}) collective-permute-start(f32[64,256]{1,0:T(8,128)S(1)} %join.6.refs_0_), channel_id=1, source_target_pairs={{0,8},{4,12},{8,0},{12,4},{16,24},{20,28},{24,16},{28,20},{32,40},... | collective-permute-start | bytes 196616 | tf_op jit(solution)/shard_map/ppermute | solution.py:448
  88.3 8.3 %collective-permute-start.26 = (f32[64,256]{1,0:T(8,128)S(1)}, f32[64,256]{1,0:T(8,128)S(1)}, u32[]{:S(2)}, u32[]{:S(2)}) collective-permute-start(f32[64,256]{1,0:T(8,128)S(1)} %join.6.refs_0_), channel_id=1, source_target_pairs={{0,16},{4,20},{8,24},{12,28},{16,0},{20,4},{24,8},{28,12},{32,48},... | collective-permute-start | bytes 196616 | tf_op jit(solution)/shard_map/ppermute | solution.py:448
  93.5 4.3 %collective-permute-start.27 = (f32[64,256]{1,0:T(8,128)S(1)}, f32[64,256]{1,0:T(8,128)S(1)}, u32[]{:S(2)}, u32[]{:S(2)}) collective-permute-start(f32[64,256]{1,0:T(8,128)S(1)} %join.6.refs_0_), channel_id=1, source_target_pairs={{0,24},{4,28},{8,16},{12,20},{16,8},{20,12},{24,0},{28,4},{32,56},... | collective-permute-start | bytes 196616 | tf_op jit(solution)/shard_map/ppermute | solution.py:448
  97.9 4.3 %collective-permute-start.28 = (f32[256,256]{1,0:T(8,128)S(1)}, f32[256,256]{1,0:T(8,128)S(1)}, u32[]{:S(2)}, u32[]{:S(2)}) collective-permute-start(f32[256,256]{1,0:T(8,128)S(1)} %join.7.refs_0_), channel_id=1, source_target_pairs={{0,4},{4,0},{8,12},{12,8},{16,20},{20,16},{24,28},{28,24},{32,36},... | collective-permute-start | bytes 786440 | tf_op jit(solution)/shard_map/ppermute | solution.py:448
  (5 other events, 20.8 us)

commit v4 on v3

--- a/solution.py
+++ b/solution.py
@@ -235,6 +235,14 @@
     return total
 
 
+def copy_rows(mer_ref, nodes_ref, row, out_refs):
+    for o_ref, side in zip(out_refs, sides(mer_ref)):
+        for part in range(2):
+            rows = [row(part, nodes_ref[side, k]) for k in range(nodes_ref.shape[1])]
+            rows.append(jnp.zeros((8 - len(rows), o_ref.shape[1]), f32))
+            o_ref[8 * part : 8 * part + 8, :] = jnp.concatenate(rows)
+
+
 def early_kernel(places, blk_ref, *refs):
     *block_refs, table_ref, phys_ref = refs
     phys_ref[...] = coefficients_times_table(blk_ref, places, block_refs, table_ref)
@@ -247,8 +255,8 @@
 
 
 def synthesis_kernel(section, places, blk_ref, mer_ref, nodes_ref, *refs):
+    block_refs = refs[: len(places)]
     (
-        *block_refs,
         phys_ref,
         kappa_ref,
         fwd_ref,
@@ -260,12 +268,11 @@
         sum_cols_ref,
         before_ref,
         stress_ref,
-        core_ref,
-        chip_ref,
         density_ref,
+        *row_refs,
         dens_ref,
         padded_ref,
-    ) = refs
+    ) = refs[len(places) :]
     points, samples = kappa_ref.shape
     inv_radius = column_ref[:, 0:1]
     quad = column_ref[:, 1:2]
@@ -280,8 +287,8 @@
     along_s, along_z = along[:PTS], along[PTS:]
     modulus = padded_ref[3].astype(f32) * quad
     stress = jnp.concatenate([along_s * modulus, along_z * modulus]).astype(bf16)
-    stress_ref[:PTS] = dot(backward_ref[...], jnp.concatenate([stress, stress]))
-    stress_ref[PTS:] = around * modulus * inv_radius
+    stress_ref[:PTS] = dot(backward_ref[...], jnp.concatenate([stress, stress])).astype(stress_ref.dtype)
+    stress_ref[PTS:] = (around * modulus * inv_radius).astype(stress_ref.dtype)
     dens = (
         along_s * padded_ref[0].astype(f32)
         + along_z * padded_ref[1].astype(f32)
@@ -291,24 +298,21 @@
     dens_ref[:PTS] = dens_high
     dens_ref[PTS:] = (dens - dens_high.astype(f32)).astype(bf16)
     by_sector = dot(dens_ref[...], sum_cols_ref[...])
-    density = before_ref[...] + exact_dot(sum_rows_ref[...], by_sector[:PTS] + by_sector[PTS:])
-    density_ref[...] = density
-    spare = jnp.zeros((8 - nodes_ref.shape[1], samples), f32)
-    for o_ref, side in zip((core_ref, chip_ref), sides(mer_ref)):
-        for part in range(2):
-            rows = [stress_ref[pl.ds(PTS * part + nodes_ref[side, k], 1), :] for k in range(nodes_ref.shape[1])]
-            o_ref[8 * part : 8 * part + 8, :] = jnp.concatenate([*rows, spare])
+    density_ref[...] = before_ref[...] + exact_dot(sum_rows_ref[...], by_sector[:PTS] + by_sector[PTS:])
+    if row_refs:
+        copy_rows(mer_ref, nodes_ref, lambda part, at: stress_ref[pl.ds(PTS * part + at, 1), :], row_refs)
 
 
 def synthesis(section, blk, mer, nodes, blocks, phys, kappa, fwd, table, consts, columns, before):
     forward, backward, sum_rows, sum_cols = consts
     samples = kappa.shape[1]
+    last = section == STEPS - 1
     outs = [
-        jax.ShapeDtypeStruct((2 * PTS, samples), f32),
-        jax.ShapeDtypeStruct((16, samples), f32),
-        jax.ShapeDtypeStruct((16, samples), f32),
+        jax.ShapeDtypeStruct((2 * PTS, samples), bf16 if last else f32),
         jax.ShapeDtypeStruct(before.shape, f32),
     ]
+    if not last:
+        outs += [jax.ShapeDtypeStruct((16, samples), f32)] * 2
     scratch = [
         pltpu.VMEM((2 * PTS, samples), bf16),
         pltpu.VMEM((4, PTS, samples), bf16),
@@ -378,22 +382,41 @@
     return call(kernel, "update", outs, [blk, *parts, now, prev, columns], 1, us=0.3)
 
 
-def finish_kernel(blk_ref, a_ref, b_ref, c_ref, d_ref, *refs):
-    *now_refs, prev_ref, column_ref, out_ref = refs
+def shared_kernel(mer_ref, nodes_ref, a_ref, b_ref, c_ref, d_ref, total_ref, core_ref, chip_ref):
+    for c in range(2):
+        total_ref[c] = sum(p[c].astype(f32) for p in (a_ref, b_ref, c_ref, d_ref))
+    copy_rows(mer_ref, nodes_ref, lambda c, at: total_ref[c, pl.ds(at, 1), :], (core_ref, chip_ref))
+
+
+def shared(mer, nodes, parts):
+    rows = jax.ShapeDtypeStruct((16, parts[0].shape[2]), f32)
+    outs = [jax.ShapeDtypeStruct(parts[0].shape, f32), rows, rows]
+    return call(shared_kernel, "shared", outs, [mer, nodes, *parts], 2, us=0.5)
+
+
+def finish_kernel(blk_ref, mer_ref, nodes_ref, force_ref, core_ref, chip_ref, *refs):
+    *now_refs, prev_ref, column_ref, out_ref, total_ref = refs
+    total_ref[...] = force_ref[...]
+    for r_ref, side in zip((core_ref, chip_ref), sides(mer_ref)):
+        rows = r_ref[...]
+        for c in range(2):
+            for k in range(nodes_ref.shape[1]):
+                at = 8 * c + k
+                total_ref[c, pl.ds(nodes_ref[side, k], 1), :] += rows[at : at + 1]
     points, _, total = out_ref.shape
     width = now_refs[0].shape[2]
     for i, now_ref in enumerate(now_refs):
         cols = slice(i * width, (i + 1) * width)
         for c in range(2):
-            parts = [p[c, :, cols] for p in (a_ref, b_ref, c_ref, d_ref)]
-            prev = prev_ref[c, :, cols]
-            value = next_values(c, cols, total, parts, now_ref[c], prev, column_ref, blk_ref[0, 0] * total)
+            force, prev = total_ref[c, :, cols], prev_ref[c, :, cols]
+            value = next_values(c, cols, total, [force], now_ref[c], prev, column_ref, blk_ref[0, 0] * total)
             out_ref[:, c, cols] = value[:points]
 
 
-def finish(blk, parts, now, prev, columns, points):
-    shape = jax.ShapeDtypeStruct((points, 2, parts[0].shape[2]), f32)
-    return call(finish_kernel, "finish", shape, [blk, *parts, *now, prev, columns], 1, us=1.2)
+def finish(blk, mer, nodes, force, core, chip, now, prev, columns, points):
+    shape = jax.ShapeDtypeStruct((points, 2, force.shape[2]), f32)
+    operands = [blk, mer, nodes, force, core, chip, *now, prev, columns]
+    return call(finish_kernel, "finish", shape, operands, 3, [pltpu.VMEM(force.shape, f32)], us=1.3)
 
 
 def join_kernel(*refs):
@@ -415,33 +438,29 @@
     return join(x, *[swapped(x, "mer", b) for b in bits])
 
 
-def owners_kernel(first_ref, *refs):
-    *row_refs, out_ref = refs
+def owners_kernel(first_ref, rows_ref, before_ref, out_ref):
     regions = out_ref.shape[0]
-    total = jnp.zeros(out_ref.shape, f32)
-    for rows_ref in row_refs:
-        rows = rows_ref[...]
-        count = rows.shape[0]
-        names = rows[:, :128].reshape(count // ELEM_ROWS, ELEM_ROWS, 128)
-        names = jnp.broadcast_to(names[:, ID_ROW : ID_ROW + 1], names.shape)
-        element = lax.broadcasted_iota(jnp.int32, names.shape, 1)
-        lane = lax.broadcasted_iota(jnp.int32, names.shape, 2)
-        ids = jnp.sum(jnp.where((lane == element) & (element < ID_ROW), names, 0.0), axis=2, keepdims=True)
-        ids = jnp.where(element[:, :, :1] < ID_ROW, ids, -1.0).reshape(count, 1)
-        mine = (lax.broadcasted_iota(jnp.int32, (count, regions), 1) + first_ref[0, 0]).astype(f32)
-        total = total + lax.dot_general(
-            jnp.where(ids == mine, 1.0, 0.0),
-            rows,
-            (((0,), (0,)), ((), ())),
-            preferred_element_type=f32,
-            precision=lax.Precision.HIGHEST,
-        )
-    out_ref[...] = total
-
-
-def owners(first, halves, regions):
-    shape = jax.ShapeDtypeStruct((regions, halves[0].shape[1]), f32)
-    return call(owners_kernel, "owners", shape, [first, *halves], 1, us=1.2)
+    rows = rows_ref[...]
+    count = rows.shape[0]
+    names = rows[:, :128].reshape(count // ELEM_ROWS, ELEM_ROWS, 128)
+    names = jnp.broadcast_to(names[:, ID_ROW : ID_ROW + 1], names.shape)
+    element = lax.broadcasted_iota(jnp.int32, names.shape, 1)
+    lane = lax.broadcasted_iota(jnp.int32, names.shape, 2)
+    ids = jnp.sum(jnp.where((lane == element) & (element < ID_ROW), names, 0.0), axis=2, keepdims=True)
+    ids = jnp.where(element[:, :, :1] < ID_ROW, ids, -1.0).reshape(count, 1)
+    mine = (lax.broadcasted_iota(jnp.int32, (count, regions), 1) + first_ref[0, 0]).astype(f32)
+    out_ref[...] = before_ref[...] + lax.dot_general(
+        jnp.where(ids == mine, 1.0, 0.0),
+        rows,
+        (((0,), (0,)), ((), ())),
+        preferred_element_type=f32,
+        precision=lax.Precision.HIGHEST,
+    )
+
+
+def owners(first, rows, before):
+    shape = jax.ShapeDtypeStruct(before.shape, f32)
+    return call(owners_kernel, "owners", shape, [first, rows, before], 1, us=0.8)
 
 
 def swapped(x, axis, bits):
@@ -490,8 +509,8 @@
     table = fourier_table(table_blk, samp_count)
 
     late = {place: blocks.pop(place) for place in ((1, 0), (3, 0))}
-    phys = early(blk, blocks, table)
-    stress, core, chip, density = synthesis(
+    phys = tied(early(blk, blocks, table), previous)
+    stress, density, core, chip = synthesis(
         0, blk, mer, nodes, late, phys, kappa, fwd, table, consts, columns, density
     )
     chip, core = across_chips(chip), swapped(core, "mer", 1)
@@ -503,30 +522,31 @@
     ]
     middle, blocks = [], []
     for h in pieces:
-        parts = [forces[h][0]] + [swapped(forces[h][bits], "blk", bits) for bits in PARTNERS[1:]]
+        sent = [forces[h][bits] for bits in PARTNERS]
+        parts = [swapped(x, "blk", bits) if bits else x for x, bits in zip(sent, PARTNERS)]
         following, send = update(h, blk, parts, current, previous, columns)
         middle.append(following)
         blocks.append(everywhere(send, h))
 
-    stress, core, chip, density = synthesis(
+    stress, density = synthesis(
         1, blk, mer, nodes, blocks[1], early(blk, blocks[0], table), kappa, fwd, table, consts, columns, density
     )
+    gathered = swapped(density, "mer", 8)
+    forces = {bits: analysis(bits, 0, blk, stress, table, count) for bits in (2, 1)}
+    gathered = join(tied(density, forces[2]), gathered)
+    forces[3] = analysis(3, 0, blk, tied(stress, gathered), table, count)
+    gathered = joined(tied(gathered, [forces[1], forces[3]]), 56)
+    forces[0] = analysis(0, 0, blk, stress, table, count)
+    parts = [swapped(forces[bits], "blk", bits) if bits else forces[0] for bits in PARTNERS]
+    gathered = joined(tied(gathered, [parts[1], forces[0]]), 16)
+    force, core, chip = shared(mer, nodes, parts)
     chip, core = across_chips(chip), swapped(core, "mer", 1)
-    gathered = swapped(density, "mer", 8)
-    stress = merge(mer, nodes, stress, core, chip)
-    forces = {2: analysis(2, 0, blk, stress, table, count)}
-    gathered = join(tied(density, forces[2]), gathered)
-    forces[1] = analysis(1, 0, blk, tied(stress, gathered), table, count)
-    gathered = joined(gathered, 32)
-    forces[3] = analysis(3, 0, blk, stress, table, count)
-    gathered = tied(gathered, forces[3])
-    forces[0] = analysis(0, 0, blk, tied(stress, gathered), table, count)
-    gathered = joined(gathered, 16)
-    parts = [forces[0]] + [swapped(forces[bits], "blk", bits) for bits in PARTNERS[1:]]
-    gathered = joined(tied(gathered, [parts[1], parts[2], forces[0]]), 2, 4, 6)
-    gathered = tied(gathered, parts[3])
-    displacement = finish(blk, parts, middle, current, columns, points)
-    return (displacement, owners(first, [gathered, swapped(gathered, "mer", 1)], regions))
+    gathered = tied(gathered, force)
+    near = [swapped(gathered, "mer", bits) for bits in (4, 2)]
+    gathered = join(gathered, *near, swapped(tied(gathered, [chip, core]), "mer", 6))
+    displacement = finish(blk, mer, nodes, force, core, chip, middle, current, columns, points)
+    kernel = owners(first, gathered, jnp.zeros((regions, sectors), f32))
+    return (displacement, owners(first, swapped(gathered, "mer", 1), kernel))
 
 
 def solution(mesh):

time: 104 us -> 98.5 us (0.947)
  waiting for transfers between devices: 21 us -> 13.7 us
  Pallas kernels: 26.2 us -> 28.6 us
    ppermute x27, waiting for transfers between devices: 18.3 us -> 10.9 us  [swapped(): lax.ppermute(x, axis, [(i, i ^ bits) for i in range(lax.axis_size(axis))])]
    ppermute x2, starting transfers between devices: 8.3 us -> 4.9 us  [across_chips(): lax.ppermute(x, 'mer', [(i, i + 1 if i % 2 else i - 1) for i in ends])]
    ppermute x27, starting transfers between devices: 45.7 us -> 48.2 us  [swapped(): lax.ppermute(x, axis, [(i, i ^ bits) for i in range(lax.axis_size(axis))])]
    pallas_call x28 -> x29, Pallas kernels: 23.8 us -> 25.5 us  [call(): pl.pallas_call(kernel, in_specs=[SMEM] * scalars + [VMEM] * (len(operands...]
  transfers between devices with their start and end apart: 29 -> 29, of which waited for: 9 -> 9; matrix products, arithmetic and copies ran while one was open for 0% -> 0% of each run, Pallas kernels for 15% -> 17%
where the time goes in v4:
time: 98.5 us; the launch traced here: 98.3 us
  starting transfers between devices  53.1 us (54%)
  Pallas kernels  28.6 us (29%)
  waiting for transfers between devices  13.7 us (14%)
  local copies, waits for them, and re-layouts  1.87 us (2%)
  between operations  1.04 us (1%)
    ppermute x27, starting transfers between devices, swapped(): lax.ppermute(x, axis, [(i, i ^ bits) for i in range(lax.axis_size(axis))])  48.2 us
    pallas_call x29, Pallas kernels, call(): pl.pallas_call(kernel, in_specs=[SMEM] * scalars + [VMEM] * (len(operands...  25.5 us
    ppermute x27, waiting for transfers between devices, swapped(): lax.ppermute(x, axis, [(i, i ^ bits) for i in range(lax.axis_size(axis))])  10.9 us
    ppermute x2, starting transfers between devices, across_chips(): lax.ppermute(x, 'mer', [(i, i + 1 if i % 2 else i - 1) for i in ends])  4.9 us
    pallas_call x2, Pallas kernels, arrange(): pl.pallas_call(arrange_kernel, in_specs=[SMEM, hbm, hbm], out_specs=[VMEM...  3.1 us
    ppermute x2, waiting for transfers between devices, across_chips(): lax.ppermute(x, 'mer', [(i, i + 1 if i % 2 else i - 1) for i in ends])  2.72 us
  transfers between devices with their start and end apart: 29, of which 9 were waited for; matrix products, arithmetic and copies ran while one was open for 0% of the time, Pallas kernels for 17%

profile of v4, /device:TPU:1, one launch (start us, length us, event | category | flops | bytes accessed | tf_op | source)
XLA Modules:
  0.0 98.3 jit_solution(11698835534330308212)
XLA Ops:
  0.6 1.9 %arrange.2 = (f32[2,128,512]{2,1,0:T(8,128)S(1)}, bf16[2,128,512]{2,1,0:T(8,128)(2,1)}) custom-call(s32[1,1]{1,0:T(1,128)} %bitcast.blk_ref, s32[1,5]{1,0:T(1,128)} %bitcast.12, f32[125,2,512]{2,1,0:T(2,128)} %disp_hbm.2), custom_call_target="tpu_custom_call" | custom-call | tf_op jit(solution)/shard_map/arrange/pallas_call | solution.py:178
  2.6 3.8 %collective-permute-start.2 = (bf16[2,128,512]{2,1,0:T(8,128)(2,1)}, bf16[2,128,512]{2,1,0:T(8,128)(2,1)}, u32[]{:S(2)}, u32[]{:S(2)}) collective-permute-start(bf16[2,128,512]{2,1,0:T(8,128)(2,1)} %get-tuple-element.30.refs_0_), channel_id=1, source_target_pairs={{0,2},{1,3},{2,0},{3,1},{4,6},{5,7},{6,4},{7,5},{8,10},{9,11},{10,... | collective-permute-start | bytes 786440 | tf_op jit(solution)/shard_map/ppermute | solution.py:467
  7.2 1.2 %setup.1 = (f32[128,4]{1,0:T(8,128)S(1)}, f32[8,256]{1,0:T(8,128)S(1)}) custom-call(s32[1,5]{1,0:T(1,128)} %bitcast.13, s32[1,5]{1,0:T(1,128)} %bitcast.15, f32[1,125]{1,0:T(1,128)} %bitcast.16, f32[125,1]{1,0:T(8,128)} %constant.25.clone.weight_ref), custom_call_target="tpu_custom_call" | custom-call | flops 1150000000 | tf_op jit(solution)/shard_map/setup/pallas_call | solution.py:107
  8.3 1.2 %arrange.3.prev_ref = f32[2,128,512]{2,1,0:T(8,128)S(1)} custom-call(s32[1,1]{1,0:T(1,128)} %bitcast.blk_ref, s32[1,5]{1,0:T(1,128)} %bitcast.14, f32[125,2,512]{2,1,0:T(2,128)} %disp_hbm.3), custom_call_target="tpu_custom_call" | custom-call | tf_op jit(solution)/shard_map/arrange/pallas_call | solution.py:178
  10.7 2.7 %table.1.refs_2_.refs_5_.table_ref.refs_4_.refs_7_ = bf16[2,2048,1024]{2,1,0:T(8,128)(2,1)S(1)} custom-call(s32[1,1]{1,0:T(1,128)} %bitcast.blk_ref, f32[2,96,1024]{2,1,0:T(8,128)S(1)} %copy-done), custom_call_target="tpu_custom_call" | custom-call | flops 1150000000 | tf_op jit(solution)/shard_map/table/pallas_call | solution.py:107
  13.4 2.4 %early.2.refs_2_ = f32[256,1024]{1,0:T(8,128)S(1)} custom-call(s32[1,1]{1,0:T(1,128)} %bitcast.blk_ref, bf16[2,128,512]{2,1,0:T(8,128)(2,1)} %get-tuple-element.30.refs_0_, bf16[2,128,512]{2,1,0:T(8,128)(2,1)} %collective-permute-done.2.refs_1_, bf16[2,2048,1024]{2,1,0:T(8,128)(2,1)S(1)} %table.1.refs_2_.refs_5_.table_ref.refs_4_.refs_7_), custom_call_target="tpu_custom_call" | custom-call | flops 1495000064 | tf_op jit(solution)/shard_map/early/pallas_call | solution.py:107
  15.8 2.7 %collective-permute-done.refs_0_ = bf16[2,128,512]{2,1,0:T(8,128)(2,1)} collective-permute-done((bf16[2,128,512]{2,1,0:T(8,128)(2,1)}, bf16[2,128,512]{2,1,0:T(8,128)(2,1)}, u32[]{:S(2)}, u32[]{:S(2)}) %collective-permute-start) | collective-permute-done | bytes 262176 | tf_op jit(solution)/shard_map/ppermute | solution.py:467
  18.5 3.3 %synthesis.2 = (f32[256,1024]{1,0:T(8,128)S(1)}, f32[8,256]{1,0:T(8,128)S(1)}, f32[16,1024]{1,0:T(8,128)S(1)}, f32[16,1024]{1,0:T(8,128)S(1)}) custom-call(s32[1,1]{1,0:T(1,128)} %bitcast.blk_ref, s32[1,1]{1,0:T(1,128)} %bitcast.1.mer_ref, s32[2,5]{1,0:T(2,128)S(1)} %bitcast.7, bf16[2,128,512]{2,1,0:T(8,128)(2,1)} %collective-permute-done.refs_0_, ...), custom_call_target="tpu_custom_call" | custom-call | flops 3449999872 | tf_op jit(solution)/shard_map/synthesis/pallas_call | solution.py:107
  21.9 1.6 %collective-permute-start.3 = (f32[16,1024]{1,0:T(8,128)S(1)}, f32[16,1024]{1,0:T(8,128)S(1)}, u32[]{:S(2)}, u32[]{:S(2)}) collective-permute-start(f32[16,1024]{1,0:T(8,128)S(1)} %get-tuple-element.39), channel_id=1, source_target_pairs={{0,4},{4,0},{8,12},{12,8},{16,20},{20,16},{24,28},{28,24},{32,36},... | collective-permute-start | bytes 196616 | tf_op jit(solution)/shard_map/ppermute | solution.py:467
  23.4 3.0 %collective-permute-start.4 = (f32[16,1024]{1,0:T(8,128)S(1)}, f32[16,1024]{1,0:T(8,128)S(1)}, u32[]{:S(2)}, u32[]{:S(2)}) collective-permute-start(f32[16,1024]{1,0:T(8,128)S(1)} %get-tuple-element.40), channel_id=1, source_target_pairs={{4,8},{8,4},{12,16},{16,12},{20,24},{24,20},{28,32},{32,28},{36,40... | collective-permute-start | bytes 196616 | tf_op jit(solution)/shard_map/ppermute | solution.py:472
  26.4 2.6 %collective-permute-done.4.chip_ref = f32[16,1024]{1,0:T(8,128)S(1)} collective-permute-done((f32[16,1024]{1,0:T(8,128)S(1)}, f32[16,1024]{1,0:T(8,128)S(1)}, u32[]{:S(2)}, u32[]{:S(2)}) %collective-permute-start.4) | collective-permute-done | bytes 65568 | tf_op jit(solution)/shard_map/ppermute | solution.py:472
  30.7 2.4 %collective-permute-start.13 = (bf16[2,128,256]{2,1,0:T(8,128)(2,1)S(1)}, bf16[2,128,256]{2,1,0:T(8,128)(2,1)S(1)}, u32[]{:S(2)}, u32[]{:S(2)}) collective-permute-start(bf16[2,128,256]{2,1,0:T(8,128)(2,1)S(1)} %analysis.19), channel_id=1, source_target_pairs={{0,3},{1,2},{2,1},{3,0},{4,7},{5,6},{6,5},{7,4},{8,11},{9,10},{10,... | collective-permute-start | bytes 393224 | tf_op jit(solution)/shard_map/ppermute | solution.py:467
  33.7 1.5 %collective-permute-start.11 = (bf16[2,128,256]{2,1,0:T(8,128)(2,1)S(1)}, bf16[2,128,256]{2,1,0:T(8,128)(2,1)S(1)}, u32[]{:S(2)}, u32[]{:S(2)}) collective-permute-start(bf16[2,128,256]{2,1,0:T(8,128)(2,1)S(1)} %analysis.17), channel_id=1, source_target_pairs={{0,2},{1,3},{2,0},{3,1},{4,6},{5,7},{6,4},{7,5},{8,10},{9,11},{10,... | collective-permute-start | bytes 393224 | tf_op jit(solution)/shard_map/ppermute | solution.py:467
  35.7 2.4 %collective-permute-start.7 = (bf16[2,128,256]{2,1,0:T(8,128)(2,1)S(1)}, bf16[2,128,256]{2,1,0:T(8,128)(2,1)S(1)}, u32[]{:S(2)}, u32[]{:S(2)}) collective-permute-start(bf16[2,128,256]{2,1,0:T(8,128)(2,1)S(1)} %analysis.15), channel_id=1, source_target_pairs={{0,3},{1,2},{2,1},{3,0},{4,7},{5,6},{6,5},{7,4},{8,11},{9,10},{10,... | collective-permute-start | bytes 393224 | tf_op jit(solution)/shard_map/ppermute | solution.py:467
  39.7 1.8 %collective-permute-start.5 = (bf16[2,128,256]{2,1,0:T(8,128)(2,1)S(1)}, bf16[2,128,256]{2,1,0:T(8,128)(2,1)S(1)}, u32[]{:S(2)}, u32[]{:S(2)}) collective-permute-start(bf16[2,128,256]{2,1,0:T(8,128)(2,1)S(1)} %analysis.13), channel_id=1, source_target_pairs={{0,2},{1,3},{2,0},{3,1},{4,6},{5,7},{6,4},{7,5},{8,10},{9,11},{10,... | collective-permute-start | bytes 393224 | tf_op jit(solution)/shard_map/ppermute | solution.py:467
  42.4 1.5 %collective-permute-start.14 = (bf16[2,128,256]{2,1,0:T(8,128)(2,1)S(1)}, bf16[2,128,256]{2,1,0:T(8,128)(2,1)S(1)}, u32[]{:S(2)}, u32[]{:S(2)}) collective-permute-start(bf16[2,128,256]{2,1,0:T(8,128)(2,1)S(1)} %get-tuple-element.43.refs_0_), channel_id=1, source_target_pairs={{0,2},{1,3},{2,0},{3,1},{4,6},{5,7},{6,4},{7,5},{8,10},{9,11},{10,... | collective-permute-start | bytes 393224 | tf_op jit(solution)/shard_map/ppermute | solution.py:467
  43.9 1.5 %collective-permute-start.15 = (bf16[2,128,256]{2,1,0:T(8,128)(2,1)S(1)}, bf16[2,128,256]{2,1,0:T(8,128)(2,1)S(1)}, u32[]{:S(2)}, u32[]{:S(2)}) collective-permute-start(bf16[2,128,256]{2,1,0:T(8,128)(2,1)S(1)} %get-tuple-element.43.refs_0_), channel_id=1, source_target_pairs={{0,1},{1,0},{2,3},{3,2},{4,5},{5,4},{6,7},{7,6},{8,9},{9,8},{10,11... | collective-permute-start | bytes 393224 | tf_op jit(solution)/shard_map/ppermute | solution.py:467
  47.1 1.7 %collective-permute-start.10 = (bf16[2,128,256]{2,1,0:T(8,128)(2,1)S(1)}, bf16[2,128,256]{2,1,0:T(8,128)(2,1)S(1)}, u32[]{:S(2)}, u32[]{:S(2)}) collective-permute-start(bf16[2,128,256]{2,1,0:T(8,128)(2,1)S(1)} %get-tuple-element.42.refs_0_), channel_id=1, source_target_pairs={{0,3},{1,2},{2,1},{3,0},{4,7},{5,6},{6,5},{7,4},{8,11},{9,10},{10,... | collective-permute-start | bytes 393224 | tf_op jit(solution)/shard_map/ppermute | solution.py:467
  48.8 1.4 %collective-permute-start.8 = (bf16[2,128,256]{2,1,0:T(8,128)(2,1)S(1)}, bf16[2,128,256]{2,1,0:T(8,128)(2,1)S(1)}, u32[]{:S(2)}, u32[]{:S(2)}) collective-permute-start(bf16[2,128,256]{2,1,0:T(8,128)(2,1)S(1)} %get-tuple-element.42.refs_0_), channel_id=1, source_target_pairs={{0,2},{1,3},{2,0},{3,1},{4,6},{5,7},{6,4},{7,5},{8,10},{9,11},{10,... | collective-permute-start | bytes 393224 | tf_op jit(solution)/shard_map/ppermute | solution.py:467
  50.7 3.8 %collective-permute-done.16.refs_3_ = bf16[2,128,256]{2,1,0:T(8,128)(2,1)S(1)} collective-permute-done((bf16[2,128,256]{2,1,0:T(8,128)(2,1)S(1)}, bf16[2,128,256]{2,1,0:T(8,128)(2,1)S(1)}, u32[]{:S(2)}, u32[]{:S(2)}) %collective-permute-start.16) | collective-permute-done | bytes 131104 | tf_op jit(solution)/shard_map/ppermute | solution.py:467
  54.5 1.2 %early.3.refs_4_ = f32[256,1024]{1,0:T(8,128)S(1)} custom-call(s32[1,1]{1,0:T(1,128)} %bitcast.blk_ref, bf16[2,128,256]{2,1,0:T(8,128)(2,1)S(1)} %get-tuple-element.43.refs_0_, bf16[2,128,256]{2,1,0:T(8,128)(2,1)S(1)} %collective-permute-done.14.refs_1_, bf16[2,128,256]{2,1,0:T(8,128)(2,1)S(1)} %collective-permute-done.15.refs_2_, ...), custom_call_target="tpu_custom_call" | custom-call | flops 1495000064 | tf_op jit(solution)/shard_map/early/pallas_call | solution.py:107
  56.8 2.9 %synthesis.3 = (bf16[256,1024]{1,0:T(8,128)(2,1)S(1)}, f32[8,256]{1,0:T(8,128)S(1)}) custom-call(s32[1,1]{1,0:T(1,128)} %bitcast.blk_ref, s32[1,1]{1,0:T(1,128)} %bitcast.1.mer_ref, s32[2,5]{1,0:T(2,128)S(1)} %bitcast.9, bf16[2,128,256]{2,1,0:T(8,128)(2,1)S(1)} %get-tuple-element.42.refs_0_, bf16[2,128,256]{2,1,0:T(8,128)(2,1)S(1)} %collective-permute-done.8.refs_1_, ...), custom_call_target="tpu_custom_call" | custom-call | flops 3449999872 | tf_op jit(solution)/shard_map/synthesis/pallas_call | solution.py:107
  60.4 1.4 %collective-permute-start.19 = (f32[8,256]{1,0:T(8,128)S(1)}, f32[8,256]{1,0:T(8,128)S(1)}, u32[]{:S(2)}, u32[]{:S(2)}) collective-permute-start(f32[8,256]{1,0:T(8,128)S(1)} %get-tuple-element.47.refs_0_), channel_id=1, source_target_pairs={{0,32},{4,36},{8,40},{12,44},{16,48},{20,52},{24,56},{28,60},{32,0... | collective-permute-start | bytes 24584 | tf_op jit(solution)/shard_map/ppermute | solution.py:467
  62.6 1.9 %collective-permute-start.17 = (bf16[2,128,512]{2,1,0:T(8,128)(2,1)S(1)}, bf16[2,128,512]{2,1,0:T(8,128)(2,1)S(1)}, u32[]{:S(2)}, u32[]{:S(2)}) collective-permute-start(bf16[2,128,512]{2,1,0:T(8,128)(2,1)S(1)} %analysis.21), channel_id=1, source_target_pairs={{0,2},{1,3},{2,0},{3,1},{4,6},{5,7},{6,4},{7,5},{8,10},{9,11},{10,... | collective-permute-start | bytes 786440 | tf_op jit(solution)/shard_map/ppermute | solution.py:467
  66.8 4.7 %collective-permute-start.23 = (f32[16,256]{1,0:T(8,128)S(1)}, f32[16,256]{1,0:T(8,128)S(1)}, u32[]{:S(2)}, u32[]{:S(2)}) collective-permute-start(f32[16,256]{1,0:T(8,128)S(1)} %join.4.refs_0_), channel_id=1, source_target_pairs={{0,224},{4,228},{8,232},{12,236},{16,240},{20,244},{24,248},{28,25... | collective-permute-start | bytes 49160 | tf_op jit(solution)/shard_map/ppermute | solution.py:467
  72.9 3.0 %collective-permute-start.24 = (f32[32,256]{1,0:T(8,128)S(1)}, f32[32,256]{1,0:T(8,128)S(1)}, u32[]{:S(2)}, u32[]{:S(2)}) collective-permute-start(f32[32,256]{1,0:T(8,128)S(1)} %join.5.refs_0_), channel_id=1, source_target_pairs={{0,64},{4,68},{8,72},{12,76},{16,80},{20,84},{24,88},{28,92},{32,9... | collective-permute-start | bytes 98312 | tf_op jit(solution)/shard_map/ppermute | solution.py:467
  76.6 7.1 %collective-permute-start.21 = (f32[16,512]{1,0:T(8,128)S(1)}, f32[16,512]{1,0:T(8,128)S(1)}, u32[]{:S(2)}, u32[]{:S(2)}) collective-permute-start(f32[16,512]{1,0:T(8,128)S(1)} %get-tuple-element.50), channel_id=1, source_target_pairs={{0,4},{4,0},{8,12},{12,8},{16,20},{20,16},{24,28},{28,24},{32,36},... | collective-permute-start | bytes 98312 | tf_op jit(solution)/shard_map/ppermute | solution.py:467
  83.7 1.9 %collective-permute-start.22 = (f32[16,512]{1,0:T(8,128)S(1)}, f32[16,512]{1,0:T(8,128)S(1)}, u32[]{:S(2)}, u32[]{:S(2)}) collective-permute-start(f32[16,512]{1,0:T(8,128)S(1)} %get-tuple-element.51), channel_id=1, source_target_pairs={{4,8},{8,4},{12,16},{16,12},{20,24},{24,20},{28,32},{32,28},{36,40... | collective-permute-start | bytes 98312 | tf_op jit(solution)/shard_map/ppermute | solution.py:472
  85.6 3.1 %collective-permute-start.25 = (f32[64,256]{1,0:T(8,128)S(1)}, f32[64,256]{1,0:T(8,128)S(1)}, u32[]{:S(2)}, u32[]{:S(2)}) collective-permute-start(f32[64,256]{1,0:T(8,128)S(1)} %join.6.refs_0_), channel_id=1, source_target_pairs={{0,16},{4,20},{8,24},{12,28},{16,0},{20,4},{24,8},{28,12},{32,48},... | collective-permute-start | bytes 196616 | tf_op jit(solution)/shard_map/ppermute | solution.py:467
  88.9 4.4 %collective-permute-start.27 = (f32[64,256]{1,0:T(8,128)S(1)}, f32[64,256]{1,0:T(8,128)S(1)}, u32[]{:S(2)}, u32[]{:S(2)}) collective-permute-start(f32[64,256]{1,0:T(8,128)S(1)} %join.6.refs_0_), channel_id=1, source_target_pairs={{0,24},{4,28},{8,16},{12,20},{16,8},{20,12},{24,0},{28,4},{32,56},... | collective-permute-start | bytes 196616 | tf_op jit(solution)/shard_map/ppermute | solution.py:467
  93.3 1.6 %collective-permute-done.27.refs_3_ = f32[64,256]{1,0:T(8,128)S(1)} collective-permute-done((f32[64,256]{1,0:T(8,128)S(1)}, f32[64,256]{1,0:T(8,128)S(1)}, u32[]{:S(2)}, u32[]{:S(2)}) %collective-permute-start.27) | collective-permute-done | bytes 65568 | tf_op jit(solution)/shard_map/ppermute | solution.py:467
  95.1 1.7 %finish.1 = f32[125,2,512]{2,1,0:T(2,128)} custom-call(s32[1,1]{1,0:T(1,128)} %bitcast.blk_ref, s32[1,1]{1,0:T(1,128)} %bitcast.1.mer_ref, s32[2,5]{1,0:T(2,128)S(1)} %bitcast.11, f32[2,128,512]{2,1,0:T(8,128)S(1)} %get-tuple-element.49.force_ref, f32[16,512]{1,0:T(8,128)S(1)} %collective-permute-done.21.core_ref, ...), custom_call_target="tpu_custom_call" | custom-call | flops 1495000064 | tf_op jit(solution)/shard_map/finish/pallas_call | solution.py:107
  (79 shorter events, 18.1 us)
Async XLA Ops:
  2.6 10.9 %collective-permute-start.2 = (bf16[2,128,512]{2,1,0:T(8,128)(2,1)}, bf16[2,128,512]{2,1,0:T(8,128)(2,1)}, u32[]{:S(2)}, u32[]{:S(2)}) collective-permute-start(bf16[2,128,512]{2,1,0:T(8,128)(2,1)} %get-tuple-element.30.refs_0_), channel_id=1, source_target_pairs={{0,2},{1,3},{2,0},{3,1},{4,6},{5,7},{6,4},{7,5},{8,10},{9,11},{10,... | collective-permute-start | bytes 786440 | tf_op jit(solution)/shard_map/ppermute | solution.py:467
  6.4 12.1 %collective-permute-start = (bf16[2,128,512]{2,1,0:T(8,128)(2,1)}, bf16[2,128,512]{2,1,0:T(8,128)(2,1)}, u32[]{:S(2)}, u32[]{:S(2)}) collective-permute-start(bf16[2,128,512]{2,1,0:T(8,128)(2,1)} %get-tuple-element.30.refs_0_), channel_id=1, source_target_pairs={{0,1},{1,0},{2,3},{3,2},{4,5},{5,4},{6,7},{7,6},{8,9},{9,8},{10,11... | collective-permute-start | bytes 786440 | tf_op jit(solution)/shard_map/ppermute | solution.py:467
  6.8 11.7 %collective-permute-start.1 = (bf16[2,128,512]{2,1,0:T(8,128)(2,1)}, bf16[2,128,512]{2,1,0:T(8,128)(2,1)}, u32[]{:S(2)}, u32[]{:S(2)}) collective-permute-start(bf16[2,128,512]{2,1,0:T(8,128)(2,1)} %get-tuple-element.30.refs_0_), channel_id=1, source_target_pairs={{0,3},{1,2},{2,1},{3,0},{4,7},{5,6},{6,5},{7,4},{8,11},{9,10},{10,... | collective-permute-start | bytes 786440 | tf_op jit(solution)/shard_map/ppermute | solution.py:467
  13.3 5.2 %copy-start.1 = (bf16[125,1024]{1,0:T(8,128)(2,1)S(1)}, bf16[125,1024]{1,0:T(8,128)(2,1)}, u32[]{:S(2)}) copy-start(bf16[125,1024]{1,0:T(8,128)(2,1)} %refs_5_.1) | copy-start | bytes 768004
  13.3 5.2 %copy-start.4 = (s32[1,2,5]{2,1,0:T(2,128)S(1)}, s32[1,2,5]{2,1,0:T(2,128)}, u32[]{:S(2)}) copy-start(s32[1,2,5]{2,1,0:T(2,128)} %param.20) | copy-start | bytes 124
  21.9 4.6 %collective-permute-start.3 = (f32[16,1024]{1,0:T(8,128)S(1)}, f32[16,1024]{1,0:T(8,128)S(1)}, u32[]{:S(2)}, u32[]{:S(2)}) collective-permute-start(f32[16,1024]{1,0:T(8,128)S(1)} %get-tuple-element.39), channel_id=1, source_target_pairs={{0,4},{4,0},{8,12},{12,8},{16,20},{20,16},{24,28},{28,24},{32,36},... | collective-permute-start | bytes 196616 | tf_op jit(solution)/shard_map/ppermute | solution.py:467
  23.4 5.6 %collective-permute-start.4 = (f32[16,1024]{1,0:T(8,128)S(1)}, f32[16,1024]{1,0:T(8,128)S(1)}, u32[]{:S(2)}, u32[]{:S(2)}) collective-permute-start(f32[16,1024]{1,0:T(8,128)S(1)} %get-tuple-element.40), channel_id=1, source_target_pairs={{4,8},{8,4},{12,16},{16,12},{20,24},{24,20},{28,32},{32,28},{36,40... | collective-permute-start | bytes 196616 | tf_op jit(solution)/shard_map/ppermute | solution.py:472
  30.7 9.0 %collective-permute-start.13 = (bf16[2,128,256]{2,1,0:T(8,128)(2,1)S(1)}, bf16[2,128,256]{2,1,0:T(8,128)(2,1)S(1)}, u32[]{:S(2)}, u32[]{:S(2)}) collective-permute-start(bf16[2,128,256]{2,1,0:T(8,128)(2,1)S(1)} %analysis.19), channel_id=1, source_target_pairs={{0,3},{1,2},{2,1},{3,0},{4,7},{5,6},{6,5},{7,4},{8,11},{9,10},{10,... | collective-permute-start | bytes 393224 | tf_op jit(solution)/shard_map/ppermute | solution.py:467
  33.6 7.9 %collective-permute-start.12 = (bf16[2,128,256]{2,1,0:T(8,128)(2,1)S(1)}, bf16[2,128,256]{2,1,0:T(8,128)(2,1)S(1)}, u32[]{:S(2)}, u32[]{:S(2)}) collective-permute-start(bf16[2,128,256]{2,1,0:T(8,128)(2,1)S(1)} %analysis.18), channel_id=1, source_target_pairs={{0,1},{1,0},{2,3},{3,2},{4,5},{5,4},{6,7},{7,6},{8,9},{9,8},{10,11... | collective-permute-start | bytes 393224 | tf_op jit(solution)/shard_map/ppermute | solution.py:467
  33.7 7.8 %collective-permute-start.11 = (bf16[2,128,256]{2,1,0:T(8,128)(2,1)S(1)}, bf16[2,128,256]{2,1,0:T(8,128)(2,1)S(1)}, u32[]{:S(2)}, u32[]{:S(2)}) collective-permute-start(bf16[2,128,256]{2,1,0:T(8,128)(2,1)S(1)} %analysis.17), channel_id=1, source_target_pairs={{0,2},{1,3},{2,0},{3,1},{4,6},{5,7},{6,4},{7,5},{8,10},{9,11},{10,... | collective-permute-start | bytes 393224 | tf_op jit(solution)/shard_map/ppermute | solution.py:467
  35.7 9.6 %collective-permute-start.7 = (bf16[2,128,256]{2,1,0:T(8,128)(2,1)S(1)}, bf16[2,128,256]{2,1,0:T(8,128)(2,1)S(1)}, u32[]{:S(2)}, u32[]{:S(2)}) collective-permute-start(bf16[2,128,256]{2,1,0:T(8,128)(2,1)S(1)} %analysis.15), channel_id=1, source_target_pairs={{0,3},{1,2},{2,1},{3,0},{4,7},{5,6},{6,5},{7,4},{8,11},{9,10},{10,... | collective-permute-start | bytes 393224 | tf_op jit(solution)/shard_map/ppermute | solution.py:467
  38.6 7.5 %collective-permute-start.6 = (bf16[2,128,256]{2,1,0:T(8,128)(2,1)S(1)}, bf16[2,128,256]{2,1,0:T(8,128)(2,1)S(1)}, u32[]{:S(2)}, u32[]{:S(2)}) collective-permute-start(bf16[2,128,256]{2,1,0:T(8,128)(2,1)S(1)} %analysis.14), channel_id=1, source_target_pairs={{0,1},{1,0},{2,3},{3,2},{4,5},{5,4},{6,7},{7,6},{8,9},{9,8},{10,11... | collective-permute-start | bytes 393224 | tf_op jit(solution)/shard_map/ppermute | solution.py:467
  39.7 7.2 %collective-permute-start.5 = (bf16[2,128,256]{2,1,0:T(8,128)(2,1)S(1)}, bf16[2,128,256]{2,1,0:T(8,128)(2,1)S(1)}, u32[]{:S(2)}, u32[]{:S(2)}) collective-permute-start(bf16[2,128,256]{2,1,0:T(8,128)(2,1)S(1)} %analysis.13), channel_id=1, source_target_pairs={{0,2},{1,3},{2,0},{3,1},{4,6},{5,7},{6,4},{7,5},{8,10},{9,11},{10,... | collective-permute-start | bytes 393224 | tf_op jit(solution)/shard_map/ppermute | solution.py:467
  42.4 7.8 %collective-permute-start.14 = (bf16[2,128,256]{2,1,0:T(8,128)(2,1)S(1)}, bf16[2,128,256]{2,1,0:T(8,128)(2,1)S(1)}, u32[]{:S(2)}, u32[]{:S(2)}) collective-permute-start(bf16[2,128,256]{2,1,0:T(8,128)(2,1)S(1)} %get-tuple-element.43.refs_0_), channel_id=1, source_target_pairs={{0,2},{1,3},{2,0},{3,1},{4,6},{5,7},{6,4},{7,5},{8,10},{9,11},{10,... | collective-permute-start | bytes 393224 | tf_op jit(solution)/shard_map/ppermute | solution.py:467
  43.9 6.8 %collective-permute-start.15 = (bf16[2,128,256]{2,1,0:T(8,128)(2,1)S(1)}, bf16[2,128,256]{2,1,0:T(8,128)(2,1)S(1)}, u32[]{:S(2)}, u32[]{:S(2)}) collective-permute-start(bf16[2,128,256]{2,1,0:T(8,128)(2,1)S(1)} %get-tuple-element.43.refs_0_), channel_id=1, source_target_pairs={{0,1},{1,0},{2,3},{3,2},{4,5},{5,4},{6,7},{7,6},{8,9},{9,8},{10,11... | collective-permute-start | bytes 393224 | tf_op jit(solution)/shard_map/ppermute | solution.py:467
  45.3 9.1 %collective-permute-start.16 = (bf16[2,128,256]{2,1,0:T(8,128)(2,1)S(1)}, bf16[2,128,256]{2,1,0:T(8,128)(2,1)S(1)}, u32[]{:S(2)}, u32[]{:S(2)}) collective-permute-start(bf16[2,128,256]{2,1,0:T(8,128)(2,1)S(1)} %get-tuple-element.43.refs_0_), channel_id=1, source_target_pairs={{0,3},{1,2},{2,1},{3,0},{4,7},{5,6},{6,5},{7,4},{8,11},{9,10},{10,... | collective-permute-start | bytes 393224 | tf_op jit(solution)/shard_map/ppermute | solution.py:467
  47.1 9.7 %collective-permute-start.10 = (bf16[2,128,256]{2,1,0:T(8,128)(2,1)S(1)}, bf16[2,128,256]{2,1,0:T(8,128)(2,1)S(1)}, u32[]{:S(2)}, u32[]{:S(2)}) collective-permute-start(bf16[2,128,256]{2,1,0:T(8,128)(2,1)S(1)} %get-tuple-element.42.refs_0_), channel_id=1, source_target_pairs={{0,3},{1,2},{2,1},{3,0},{4,7},{5,6},{6,5},{7,4},{8,11},{9,10},{10,... | collective-permute-start | bytes 393224 | tf_op jit(solution)/shard_map/ppermute | solution.py:467
  48.8 8.0 %collective-permute-start.8 = (bf16[2,128,256]{2,1,0:T(8,128)(2,1)S(1)}, bf16[2,128,256]{2,1,0:T(8,128)(2,1)S(1)}, u32[]{:S(2)}, u32[]{:S(2)}) collective-permute-start(bf16[2,128,256]{2,1,0:T(8,128)(2,1)S(1)} %get-tuple-element.42.refs_0_), channel_id=1, source_target_pairs={{0,2},{1,3},{2,0},{3,1},{4,6},{5,7},{6,4},{7,5},{8,10},{9,11},{10,... | collective-permute-start | bytes 393224 | tf_op jit(solution)/shard_map/ppermute | solution.py:467
  50.2 6.6 %collective-permute-start.9 = (bf16[2,128,256]{2,1,0:T(8,128)(2,1)S(1)}, bf16[2,128,256]{2,1,0:T(8,128)(2,1)S(1)}, u32[]{:S(2)}, u32[]{:S(2)}) collective-permute-start(bf16[2,128,256]{2,1,0:T(8,128)(2,1)S(1)} %get-tuple-element.42.refs_0_), channel_id=1, source_target_pairs={{0,1},{1,0},{2,3},{3,2},{4,5},{5,4},{6,7},{7,6},{8,9},{9,8},{10,11... | collective-permute-start | bytes 393224 | tf_op jit(solution)/shard_map/ppermute | solution.py:467
  60.4 4.9 %collective-permute-start.19 = (f32[8,256]{1,0:T(8,128)S(1)}, f32[8,256]{1,0:T(8,128)S(1)}, u32[]{:S(2)}, u32[]{:S(2)}) collective-permute-start(f32[8,256]{1,0:T(8,128)S(1)} %get-tuple-element.47.refs_0_), channel_id=1, source_target_pairs={{0,32},{4,36},{8,40},{12,44},{16,48},{20,52},{24,56},{28,60},{32,0... | collective-permute-start | bytes 24584 | tf_op jit(solution)/shard_map/ppermute | solution.py:467
  62.6 10.3 %collective-permute-start.17 = (bf16[2,128,512]{2,1,0:T(8,128)(2,1)S(1)}, bf16[2,128,512]{2,1,0:T(8,128)(2,1)S(1)}, u32[]{:S(2)}, u32[]{:S(2)}) collective-permute-start(bf16[2,128,512]{2,1,0:T(8,128)(2,1)S(1)} %analysis.21), channel_id=1, source_target_pairs={{0,2},{1,3},{2,0},{3,1},{4,6},{5,7},{6,4},{7,5},{8,10},{9,11},{10,... | collective-permute-start | bytes 786440 | tf_op jit(solution)/shard_map/ppermute | solution.py:467
  64.4 11.4 %collective-permute-start.18 = (bf16[2,128,512]{2,1,0:T(8,128)(2,1)S(1)}, bf16[2,128,512]{2,1,0:T(8,128)(2,1)S(1)}, u32[]{:S(2)}, u32[]{:S(2)}) collective-permute-start(bf16[2,128,512]{2,1,0:T(8,128)(2,1)S(1)} %analysis.22), channel_id=1, source_target_pairs={{0,1},{1,0},{2,3},{3,2},{4,5},{5,4},{6,7},{7,6},{8,9},{9,8},{10,11... | collective-permute-start | bytes 786440 | tf_op jit(solution)/shard_map/ppermute | solution.py:467
  66.0 9.8 %collective-permute-start.20 = (bf16[2,128,512]{2,1,0:T(8,128)(2,1)S(1)}, bf16[2,128,512]{2,1,0:T(8,128)(2,1)S(1)}, u32[]{:S(2)}, u32[]{:S(2)}) collective-permute-start(bf16[2,128,512]{2,1,0:T(8,128)(2,1)S(1)} %analysis.23), channel_id=1, source_target_pairs={{0,3},{1,2},{2,1},{3,0},{4,7},{5,6},{6,5},{7,4},{8,11},{9,10},{10,... | collective-permute-start | bytes 786440 | tf_op jit(solution)/shard_map/ppermute | solution.py:467
  66.8 6.1 %collective-permute-start.23 = (f32[16,256]{1,0:T(8,128)S(1)}, f32[16,256]{1,0:T(8,128)S(1)}, u32[]{:S(2)}, u32[]{:S(2)}) collective-permute-start(f32[16,256]{1,0:T(8,128)S(1)} %join.4.refs_0_), channel_id=1, source_target_pairs={{0,224},{4,228},{8,232},{12,236},{16,240},{20,244},{24,248},{28,25... | collective-permute-start | bytes 49160 | tf_op jit(solution)/shard_map/ppermute | solution.py:467
  72.9 12.7 %collective-permute-start.24 = (f32[32,256]{1,0:T(8,128)S(1)}, f32[32,256]{1,0:T(8,128)S(1)}, u32[]{:S(2)}, u32[]{:S(2)}) collective-permute-start(f32[32,256]{1,0:T(8,128)S(1)} %join.5.refs_0_), channel_id=1, source_target_pairs={{0,64},{4,68},{8,72},{12,76},{16,80},{20,84},{24,88},{28,92},{32,9... | collective-permute-start | bytes 98312 | tf_op jit(solution)/shard_map/ppermute | solution.py:467
  76.6 18.5 %copy-start.3 = (f32[2,128,256]{2,1,0:T(8,128)S(1)}, f32[2,128,256]{2,1,0:T(8,128)}, u32[]{:S(2)}) copy-start(f32[2,128,256]{2,1,0:T(8,128)} %copy-done.2) | copy-start | bytes 786436
  76.6 12.2 %collective-permute-start.21 = (f32[16,512]{1,0:T(8,128)S(1)}, f32[16,512]{1,0:T(8,128)S(1)}, u32[]{:S(2)}, u32[]{:S(2)}) collective-permute-start(f32[16,512]{1,0:T(8,128)S(1)} %get-tuple-element.50), channel_id=1, source_target_pairs={{0,4},{4,0},{8,12},{12,8},{16,20},{20,16},{24,28},{28,24},{32,36},... | collective-permute-start | bytes 98312 | tf_op jit(solution)/shard_map/ppermute | solution.py:467
  83.7 5.2 %collective-permute-start.22 = (f32[16,512]{1,0:T(8,128)S(1)}, f32[16,512]{1,0:T(8,128)S(1)}, u32[]{:S(2)}, u32[]{:S(2)}) collective-permute-start(f32[16,512]{1,0:T(8,128)S(1)} %get-tuple-element.51), channel_id=1, source_target_pairs={{4,8},{8,4},{12,16},{16,12},{20,24},{24,20},{28,32},{32,28},{36,40... | collective-permute-start | bytes 98312 | tf_op jit(solution)/shard_map/ppermute | solution.py:472
  85.6 7.7 %collective-permute-start.25 = (f32[64,256]{1,0:T(8,128)S(1)}, f32[64,256]{1,0:T(8,128)S(1)}, u32[]{:S(2)}, u32[]{:S(2)}) collective-permute-start(f32[64,256]{1,0:T(8,128)S(1)} %join.6.refs_0_), channel_id=1, source_target_pairs={{0,16},{4,20},{8,24},{12,28},{16,0},{20,4},{24,8},{28,12},{32,48},... | collective-permute-start | bytes 196616 | tf_op jit(solution)/shard_map/ppermute | solution.py:467
  88.8 4.6 %collective-permute-start.26 = (f32[64,256]{1,0:T(8,128)S(1)}, f32[64,256]{1,0:T(8,128)S(1)}, u32[]{:S(2)}, u32[]{:S(2)}) collective-permute-start(f32[64,256]{1,0:T(8,128)S(1)} %join.6.refs_0_), channel_id=1, source_target_pairs={{0,8},{4,12},{8,0},{12,4},{16,24},{20,28},{24,16},{28,20},{32,40},... | collective-permute-start | bytes 196616 | tf_op jit(solution)/shard_map/ppermute | solution.py:467
  88.9 6.1 %collective-permute-start.27 = (f32[64,256]{1,0:T(8,128)S(1)}, f32[64,256]{1,0:T(8,128)S(1)}, u32[]{:S(2)}, u32[]{:S(2)}) collective-permute-start(f32[64,256]{1,0:T(8,128)S(1)} %join.6.refs_0_), channel_id=1, source_target_pairs={{0,24},{4,28},{8,16},{12,20},{16,8},{20,12},{24,0},{28,4},{32,56},... | collective-permute-start | bytes 196616 | tf_op jit(solution)/shard_map/ppermute | solution.py:467
  95.0 2.2 %collective-permute-start.28 = (f32[256,256]{1,0:T(8,128)S(1)}, f32[256,256]{1,0:T(8,128)S(1)}, u32[]{:S(2)}, u32[]{:S(2)}) collective-permute-start(f32[256,256]{1,0:T(8,128)S(1)} %join.7.rows_ref), channel_id=1, source_target_pairs={{0,4},{4,0},{8,12},{12,8},{16,20},{20,16},{24,28},{28,24},{32,36},... | collective-permute-start | bytes 786440 | tf_op jit(solution)/shard_map/ppermute | solution.py:467
  (7 other events, 24.7 us)

commit v5 on v4

--- a/solution.py
+++ b/solution.py
@@ -16,7 +16,7 @@
 ELEM_ROWS = 8
 ID_ROW = 5
 TABLE_STRIDE = 64
-FLOPS_US = 1150000000
+FLOPS_US = 3450000000
 PARTNERS = (0, 2, 1, 3)
 
 time_step_sq = 0.0004
@@ -237,10 +237,11 @@
 
 def copy_rows(mer_ref, nodes_ref, row, out_refs):
     for o_ref, side in zip(out_refs, sides(mer_ref)):
+        rows = []
         for part in range(2):
-            rows = [row(part, nodes_ref[side, k]) for k in range(nodes_ref.shape[1])]
-            rows.append(jnp.zeros((8 - len(rows), o_ref.shape[1]), f32))
-            o_ref[8 * part : 8 * part + 8, :] = jnp.concatenate(rows)
+            rows += [row(part, nodes_ref[side, k]) for k in range(nodes_ref.shape[1])]
+            rows.append(jnp.zeros((8 - nodes_ref.shape[1], o_ref.shape[1]), f32))
+        o_ref[...] = jnp.concatenate(rows).astype(o_ref.dtype)
 
 
 def early_kernel(places, blk_ref, *refs):
@@ -312,7 +313,7 @@
         jax.ShapeDtypeStruct(before.shape, f32),
     ]
     if not last:
-        outs += [jax.ShapeDtypeStruct((16, samples), f32)] * 2
+        outs += [jax.ShapeDtypeStruct((16, samples), bf16)] * 2
     scratch = [
         pltpu.VMEM((2 * PTS, samples), bf16),
         pltpu.VMEM((4, PTS, samples), bf16),
@@ -324,7 +325,7 @@
 def merge_kernel(mer_ref, nodes_ref, stress_ref, core_ref, chip_ref, out_ref, total_ref):
     total_ref[...] = stress_ref[...]
     for r_ref, side in zip((core_ref, chip_ref), sides(mer_ref)):
-        rows = r_ref[...]
+        rows = r_ref[...].astype(f32)
         for part in range(2):
             for k in range(nodes_ref.shape[1]):
                 at = 8 * part + k

time: 98.5 us -> 97 us (0.985)
  starting transfers between devices: 53.1 us -> 51.3 us
  waiting for transfers between devices: 13.7 us -> 15.2 us
  Pallas kernels: 28.6 us -> 27.3 us
    ppermute x27, starting transfers between devices: 48.2 us -> 46.4 us  [swapped(): lax.ppermute(x, axis, [(i, i ^ bits) for i in range(lax.axis_size(axis))])]
    ppermute x2, waiting for transfers between devices: 2.72 us -> 4.26 us  [across_chips(): lax.ppermute(x, 'mer', [(i, i + 1 if i % 2 else i - 1) for i in ends])]
where the time goes in v5:
time: 97 us; the launch traced here: 96.4 us
  starting transfers between devices  51.3 us (53%)
  Pallas kernels  27.3 us (28%)
  waiting for transfers between devices  15.2 us (16%)
  local copies, waits for them, and re-layouts  1.63 us (2%)
  between operations  1.01 us (1%)
    ppermute x27, starting transfers between devices, swapped(): lax.ppermute(x, axis, [(i, i ^ bits) for i in range(lax.axis_size(axis))])  46.4 us
    pallas_call x29, Pallas kernels, call(): pl.pallas_call(kernel, in_specs=[SMEM] * scalars + [VMEM] * (len(operands...  24.9 us
    ppermute x27, waiting for transfers between devices, swapped(): lax.ppermute(x, axis, [(i, i ^ bits) for i in range(lax.axis_size(axis))])  10.9 us
    ppermute x2, starting transfers between devices, across_chips(): lax.ppermute(x, 'mer', [(i, i + 1 if i % 2 else i - 1) for i in ends])  4.91 us
    ppermute x2, waiting for transfers between devices, across_chips(): lax.ppermute(x, 'mer', [(i, i + 1 if i % 2 else i - 1) for i in ends])  4.26 us
    pallas_call x2, Pallas kernels, arrange(): pl.pallas_call(arrange_kernel, in_specs=[SMEM, hbm, hbm], out_specs=[VMEM...  2.4 us
  transfers between devices with their start and end apart: 29, of which 9 were waited for; matrix products, arithmetic and copies ran while one was open for 0% of the time, Pallas kernels for 17%

profile of v5, /device:TPU:1, one launch (start us, length us, event | category | flops | bytes accessed | tf_op | source)
XLA Modules:
  0.0 96.4 jit_solution(10125587104716272240)
XLA Ops:
  0.6 1.2 %arrange.2 = (f32[2,128,512]{2,1,0:T(8,128)S(1)}, bf16[2,128,512]{2,1,0:T(8,128)(2,1)S(1)}) custom-call(s32[1,1]{1,0:T(1,128)} %bitcast.blk_ref, s32[1,5]{1,0:T(1,128)} %bitcast.12, f32[125,2,512]{2,1,0:T(2,128)} %disp_hbm.2), custom_call_target="tpu_custom_call" | custom-call | tf_op jit(solution)/shard_map/arrange/pallas_call | solution.py:178
  1.9 3.8 %collective-permute-start.2 = (bf16[2,128,512]{2,1,0:T(8,128)(2,1)S(1)}, bf16[2,128,512]{2,1,0:T(8,128)(2,1)}, u32[]{:S(2)}, u32[]{:S(2)}) collective-permute-start(bf16[2,128,512]{2,1,0:T(8,128)(2,1)S(1)} %get-tuple-element.30.refs_0_), channel_id=1, source_target_pairs={{0,2},{1,3},{2,0},{3,1},{4,6},{5,7},{6,4},{7,5},{8,10},{9,11},{10,... | collective-permute-start | bytes 786440 | tf_op jit(solution)/shard_map/ppermute | solution.py:468
  7.6 1.2 %arrange.3.prev_ref = f32[2,128,512]{2,1,0:T(8,128)S(1)} custom-call(s32[1,1]{1,0:T(1,128)} %bitcast.blk_ref, s32[1,5]{1,0:T(1,128)} %bitcast.14, f32[125,2,512]{2,1,0:T(2,128)} %disp_hbm.3), custom_call_target="tpu_custom_call" | custom-call | tf_op jit(solution)/shard_map/arrange/pallas_call | solution.py:178
  10.4 2.7 %table.1.refs_2_.refs_5_.table_ref.refs_4_.refs_7_ = bf16[2,2048,1024]{2,1,0:T(8,128)(2,1)S(1)} custom-call(s32[1,1]{1,0:T(1,128)} %bitcast.blk_ref, f32[2,96,1024]{2,1,0:T(8,128)S(1)} %copy-done.2), custom_call_target="tpu_custom_call" | custom-call | flops 3449999872 | tf_op jit(solution)/shard_map/table/pallas_call | solution.py:107
  13.2 2.3 %early.2.refs_2_ = f32[256,1024]{1,0:T(8,128)S(1)} custom-call(s32[1,1]{1,0:T(1,128)} %bitcast.blk_ref, bf16[2,128,512]{2,1,0:T(8,128)(2,1)S(1)} %get-tuple-element.30.refs_0_, bf16[2,128,512]{2,1,0:T(8,128)(2,1)} %collective-permute-done.2.refs_1_, bf16[2,2048,1024]{2,1,0:T(8,128)(2,1)S(1)} %table.1.refs_2_.refs_5_.table_ref.refs_4_.refs_7_), custom_call_target="tpu_custom_call" | custom-call | flops 4485000192 | tf_op jit(solution)/shard_map/early/pallas_call | solution.py:107
  15.5 2.0 %collective-permute-done.refs_0_ = bf16[2,128,512]{2,1,0:T(8,128)(2,1)S(1)} collective-permute-done((bf16[2,128,512]{2,1,0:T(8,128)(2,1)S(1)}, bf16[2,128,512]{2,1,0:T(8,128)(2,1)S(1)}, u32[]{:S(2)}, u32[]{:S(2)}) %collective-permute-start) | collective-permute-done | bytes 262176 | tf_op jit(solution)/shard_map/ppermute | solution.py:468
  17.5 2.8 %synthesis.2 = (f32[256,1024]{1,0:T(8,128)S(1)}, f32[8,256]{1,0:T(8,128)S(1)}, bf16[16,1024]{1,0:T(8,128)(2,1)S(1)}, bf16[16,1024]{1,0:T(8,128)(2,1)S(1)}) custom-call(s32[1,1]{1,0:T(1,128)} %bitcast.blk_ref, s32[1,1]{1,0:T(1,128)} %bitcast.1.mer_ref, s32[2,5]{1,0:T(2,128)S(1)} %bitcast.7, bf16[2,128,512]{2,1,0:T(8,128)(2,1)S(1)} %collective-permute-done.refs_0_, ...), custom_call_target="tpu_custom_call" | custom-call | flops 10350000128 | tf_op jit(solution)/shard_map/synthesis/pallas_call | solution.py:107
  20.4 1.5 %collective-permute-start.3 = (bf16[16,1024]{1,0:T(8,128)(2,1)S(1)}, bf16[16,1024]{1,0:T(8,128)(2,1)S(1)}, u32[]{:S(2)}, u32[]{:S(2)}) collective-permute-start(bf16[16,1024]{1,0:T(8,128)(2,1)S(1)} %get-tuple-element.39), channel_id=1, source_target_pairs={{0,4},{4,0},{8,12},{12,8},{16,20},{20,16},{24,28},{28,24},{32,36},... | collective-permute-start | bytes 98312 | tf_op jit(solution)/shard_map/ppermute | solution.py:468
  21.9 3.0 %collective-permute-start.4 = (bf16[16,1024]{1,0:T(8,128)(2,1)S(1)}, bf16[16,1024]{1,0:T(8,128)(2,1)S(1)}, u32[]{:S(2)}, u32[]{:S(2)}) collective-permute-start(bf16[16,1024]{1,0:T(8,128)(2,1)S(1)} %get-tuple-element.40), channel_id=1, source_target_pairs={{4,8},{8,4},{12,16},{16,12},{20,24},{24,20},{28,32},{32,28},{36,40... | collective-permute-start | bytes 98312 | tf_op jit(solution)/shard_map/ppermute | solution.py:473
  24.9 2.2 %collective-permute-done.4.chip_ref = bf16[16,1024]{1,0:T(8,128)(2,1)S(1)} collective-permute-done((bf16[16,1024]{1,0:T(8,128)(2,1)S(1)}, bf16[16,1024]{1,0:T(8,128)(2,1)S(1)}, u32[]{:S(2)}, u32[]{:S(2)}) %collective-permute-start.4) | collective-permute-done | bytes 32800 | tf_op jit(solution)/shard_map/ppermute | solution.py:473
  28.9 2.4 %collective-permute-start.13 = (bf16[2,128,256]{2,1,0:T(8,128)(2,1)S(1)}, bf16[2,128,256]{2,1,0:T(8,128)(2,1)S(1)}, u32[]{:S(2)}, u32[]{:S(2)}) collective-permute-start(bf16[2,128,256]{2,1,0:T(8,128)(2,1)S(1)} %analysis.19), channel_id=1, source_target_pairs={{0,3},{1,2},{2,1},{3,0},{4,7},{5,6},{6,5},{7,4},{8,11},{9,10},{10,... | collective-permute-start | bytes 393224 | tf_op jit(solution)/shard_map/ppermute | solution.py:468
  31.9 1.5 %collective-permute-start.11 = (bf16[2,128,256]{2,1,0:T(8,128)(2,1)S(1)}, bf16[2,128,256]{2,1,0:T(8,128)(2,1)S(1)}, u32[]{:S(2)}, u32[]{:S(2)}) collective-permute-start(bf16[2,128,256]{2,1,0:T(8,128)(2,1)S(1)} %analysis.17), channel_id=1, source_target_pairs={{0,2},{1,3},{2,0},{3,1},{4,6},{5,7},{6,4},{7,5},{8,10},{9,11},{10,... | collective-permute-start | bytes 393224 | tf_op jit(solution)/shard_map/ppermute | solution.py:468
  33.9 2.4 %collective-permute-start.7 = (bf16[2,128,256]{2,1,0:T(8,128)(2,1)S(1)}, bf16[2,128,256]{2,1,0:T(8,128)(2,1)S(1)}, u32[]{:S(2)}, u32[]{:S(2)}) collective-permute-start(bf16[2,128,256]{2,1,0:T(8,128)(2,1)S(1)} %analysis.15), channel_id=1, source_target_pairs={{0,3},{1,2},{2,1},{3,0},{4,7},{5,6},{6,5},{7,4},{8,11},{9,10},{10,... | collective-permute-start | bytes 393224 | tf_op jit(solution)/shard_map/ppermute | solution.py:468
  37.9 1.8 %collective-permute-start.5 = (bf16[2,128,256]{2,1,0:T(8,128)(2,1)S(1)}, bf16[2,128,256]{2,1,0:T(8,128)(2,1)S(1)}, u32[]{:S(2)}, u32[]{:S(2)}) collective-permute-start(bf16[2,128,256]{2,1,0:T(8,128)(2,1)S(1)} %analysis.13), channel_id=1, source_target_pairs={{0,2},{1,3},{2,0},{3,1},{4,6},{5,7},{6,4},{7,5},{8,10},{9,11},{10,... | collective-permute-start | bytes 393224 | tf_op jit(solution)/shard_map/ppermute | solution.py:468
  39.8 1.6 %collective-permute-start.14 = (bf16[2,128,256]{2,1,0:T(8,128)(2,1)S(1)}, bf16[2,128,256]{2,1,0:T(8,128)(2,1)S(1)}, u32[]{:S(2)}, u32[]{:S(2)}) collective-permute-start(bf16[2,128,256]{2,1,0:T(8,128)(2,1)S(1)} %get-tuple-element.43.refs_0_), channel_id=1, source_target_pairs={{0,2},{1,3},{2,0},{3,1},{4,6},{5,7},{6,4},{7,5},{8,10},{9,11},{10,... | collective-permute-start | bytes 393224 | tf_op jit(solution)/shard_map/ppermute | solution.py:468
  41.4 1.5 %collective-permute-start.15 = (bf16[2,128,256]{2,1,0:T(8,128)(2,1)S(1)}, bf16[2,128,256]{2,1,0:T(8,128)(2,1)S(1)}, u32[]{:S(2)}, u32[]{:S(2)}) collective-permute-start(bf16[2,128,256]{2,1,0:T(8,128)(2,1)S(1)} %get-tuple-element.43.refs_0_), channel_id=1, source_target_pairs={{0,1},{1,0},{2,3},{3,2},{4,5},{5,4},{6,7},{7,6},{8,9},{9,8},{10,11... | collective-permute-start | bytes 393224 | tf_op jit(solution)/shard_map/ppermute | solution.py:468
  43.7 1.5 %collective-permute-done.5.b_ref = bf16[2,128,256]{2,1,0:T(8,128)(2,1)S(1)} collective-permute-done((bf16[2,128,256]{2,1,0:T(8,128)(2,1)S(1)}, bf16[2,128,256]{2,1,0:T(8,128)(2,1)S(1)}, u32[]{:S(2)}, u32[]{:S(2)}) %collective-permute-start.5) | collective-permute-done | bytes 131104 | tf_op jit(solution)/shard_map/ppermute | solution.py:468
  46.5 2.0 %collective-permute-start.8 = (bf16[2,128,256]{2,1,0:T(8,128)(2,1)S(1)}, bf16[2,128,256]{2,1,0:T(8,128)(2,1)S(1)}, u32[]{:S(2)}, u32[]{:S(2)}) collective-permute-start(bf16[2,128,256]{2,1,0:T(8,128)(2,1)S(1)} %get-tuple-element.42.refs_0_), channel_id=1, source_target_pairs={{0,2},{1,3},{2,0},{3,1},{4,6},{5,7},{6,4},{7,5},{8,10},{9,11},{10,... | collective-permute-start | bytes 393224 | tf_op jit(solution)/shard_map/ppermute | solution.py:468
  48.9 3.7 %collective-permute-done.16.refs_3_ = bf16[2,128,256]{2,1,0:T(8,128)(2,1)S(1)} collective-permute-done((bf16[2,128,256]{2,1,0:T(8,128)(2,1)S(1)}, bf16[2,128,256]{2,1,0:T(8,128)(2,1)S(1)}, u32[]{:S(2)}, u32[]{:S(2)}) %collective-permute-start.16) | collective-permute-done | bytes 131104 | tf_op jit(solution)/shard_map/ppermute | solution.py:468
  52.6 1.3 %early.3.refs_4_ = f32[256,1024]{1,0:T(8,128)S(1)} custom-call(s32[1,1]{1,0:T(1,128)} %bitcast.blk_ref, bf16[2,128,256]{2,1,0:T(8,128)(2,1)S(1)} %get-tuple-element.43.refs_0_, bf16[2,128,256]{2,1,0:T(8,128)(2,1)S(1)} %collective-permute-done.14.refs_1_, bf16[2,128,256]{2,1,0:T(8,128)(2,1)S(1)} %collective-permute-done.15.refs_2_, ...), custom_call_target="tpu_custom_call" | custom-call | flops 4485000192 | tf_op jit(solution)/shard_map/early/pallas_call | solution.py:107
  54.9 2.9 %synthesis.3 = (bf16[256,1024]{1,0:T(8,128)(2,1)S(1)}, f32[8,256]{1,0:T(8,128)S(1)}) custom-call(s32[1,1]{1,0:T(1,128)} %bitcast.blk_ref, s32[1,1]{1,0:T(1,128)} %bitcast.1.mer_ref, s32[2,5]{1,0:T(2,128)S(1)} %bitcast.9, bf16[2,128,256]{2,1,0:T(8,128)(2,1)S(1)} %get-tuple-element.42.refs_0_, bf16[2,128,256]{2,1,0:T(8,128)(2,1)S(1)} %collective-permute-done.8.refs_1_, ...), custom_call_target="tpu_custom_call" | custom-call | flops 10350000128 | tf_op jit(solution)/shard_map/synthesis/pallas_call | solution.py:107
  58.5 1.4 %collective-permute-start.19 = (f32[8,256]{1,0:T(8,128)S(1)}, f32[8,256]{1,0:T(8,128)S(1)}, u32[]{:S(2)}, u32[]{:S(2)}) collective-permute-start(f32[8,256]{1,0:T(8,128)S(1)} %get-tuple-element.47.refs_0_), channel_id=1, source_target_pairs={{0,32},{4,36},{8,40},{12,44},{16,48},{20,52},{24,56},{28,60},{32,0... | collective-permute-start | bytes 24584 | tf_op jit(solution)/shard_map/ppermute | solution.py:468
  60.7 1.7 %collective-permute-start.17 = (bf16[2,128,512]{2,1,0:T(8,128)(2,1)S(1)}, bf16[2,128,512]{2,1,0:T(8,128)(2,1)S(1)}, u32[]{:S(2)}, u32[]{:S(2)}) collective-permute-start(bf16[2,128,512]{2,1,0:T(8,128)(2,1)S(1)} %analysis.21), channel_id=1, source_target_pairs={{0,2},{1,3},{2,0},{3,1},{4,6},{5,7},{6,4},{7,5},{8,10},{9,11},{10,... | collective-permute-start | bytes 786440 | tf_op jit(solution)/shard_map/ppermute | solution.py:468
  64.9 4.7 %collective-permute-start.23 = (f32[16,256]{1,0:T(8,128)S(1)}, f32[16,256]{1,0:T(8,128)S(1)}, u32[]{:S(2)}, u32[]{:S(2)}) collective-permute-start(f32[16,256]{1,0:T(8,128)S(1)} %join.4.refs_0_), channel_id=1, source_target_pairs={{0,224},{4,228},{8,232},{12,236},{16,240},{20,244},{24,248},{28,25... | collective-permute-start | bytes 49160 | tf_op jit(solution)/shard_map/ppermute | solution.py:468
  71.0 2.7 %collective-permute-start.24 = (f32[32,256]{1,0:T(8,128)S(1)}, f32[32,256]{1,0:T(8,128)S(1)}, u32[]{:S(2)}, u32[]{:S(2)}) collective-permute-start(f32[32,256]{1,0:T(8,128)S(1)} %join.5.refs_0_), channel_id=1, source_target_pairs={{0,64},{4,68},{8,72},{12,76},{16,80},{20,84},{24,88},{28,92},{32,9... | collective-permute-start | bytes 98312 | tf_op jit(solution)/shard_map/ppermute | solution.py:468
  74.5 8.5 %collective-permute-start.21 = (f32[16,512]{1,0:T(8,128)S(1)}, f32[16,512]{1,0:T(8,128)S(1)}, u32[]{:S(2)}, u32[]{:S(2)}) collective-permute-start(f32[16,512]{1,0:T(8,128)S(1)} %get-tuple-element.50), channel_id=1, source_target_pairs={{0,4},{4,0},{8,12},{12,8},{16,20},{20,16},{24,28},{28,24},{32,36},... | collective-permute-start | bytes 98312 | tf_op jit(solution)/shard_map/ppermute | solution.py:468
  83.0 1.9 %collective-permute-start.22 = (f32[16,512]{1,0:T(8,128)S(1)}, f32[16,512]{1,0:T(8,128)S(1)}, u32[]{:S(2)}, u32[]{:S(2)}) collective-permute-start(f32[16,512]{1,0:T(8,128)S(1)} %get-tuple-element.51), channel_id=1, source_target_pairs={{4,8},{8,4},{12,16},{16,12},{20,24},{24,20},{28,32},{32,28},{36,40... | collective-permute-start | bytes 98312 | tf_op jit(solution)/shard_map/ppermute | solution.py:473
  84.9 1.9 %collective-permute-start.25 = (f32[64,256]{1,0:T(8,128)S(1)}, f32[64,256]{1,0:T(8,128)S(1)}, u32[]{:S(2)}, u32[]{:S(2)}) collective-permute-start(f32[64,256]{1,0:T(8,128)S(1)} %join.6.refs_0_), channel_id=1, source_target_pairs={{0,16},{4,20},{8,24},{12,28},{16,0},{20,4},{24,8},{28,12},{32,48},... | collective-permute-start | bytes 196616 | tf_op jit(solution)/shard_map/ppermute | solution.py:468
  86.8 2.1 %collective-permute-done.22.chip_ref = f32[16,512]{1,0:T(8,128)S(1)} collective-permute-done((f32[16,512]{1,0:T(8,128)S(1)}, f32[16,512]{1,0:T(8,128)S(1)}, u32[]{:S(2)}, u32[]{:S(2)}) %collective-permute-start.22) | collective-permute-done | bytes 32800 | tf_op jit(solution)/shard_map/ppermute | solution.py:473
  88.8 2.5 %collective-permute-start.27 = (f32[64,256]{1,0:T(8,128)S(1)}, f32[64,256]{1,0:T(8,128)S(1)}, u32[]{:S(2)}, u32[]{:S(2)}) collective-permute-start(f32[64,256]{1,0:T(8,128)S(1)} %join.6.refs_0_), channel_id=1, source_target_pairs={{0,24},{4,28},{8,16},{12,20},{16,8},{20,12},{24,0},{28,4},{32,56},... | collective-permute-start | bytes 196616 | tf_op jit(solution)/shard_map/ppermute | solution.py:468
  91.3 1.9 %collective-permute-done.27.refs_3_ = f32[64,256]{1,0:T(8,128)S(1)} collective-permute-done((f32[64,256]{1,0:T(8,128)S(1)}, f32[64,256]{1,0:T(8,128)S(1)}, u32[]{:S(2)}, u32[]{:S(2)}) %collective-permute-start.27) | collective-permute-done | bytes 65568 | tf_op jit(solution)/shard_map/ppermute | solution.py:468
  93.3 1.7 %finish.1 = f32[125,2,512]{2,1,0:T(2,128)} custom-call(s32[1,1]{1,0:T(1,128)} %bitcast.blk_ref, s32[1,1]{1,0:T(1,128)} %bitcast.1.mer_ref, s32[2,5]{1,0:T(2,128)S(1)} %bitcast.11, f32[2,128,512]{2,1,0:T(8,128)S(1)} %get-tuple-element.49.force_ref, f32[16,512]{1,0:T(8,128)S(1)} %collective-permute-done.21.core_ref, ...), custom_call_target="tpu_custom_call" | custom-call | flops 4485000192 | tf_op jit(solution)/shard_map/finish/pallas_call | solution.py:107
  (75 shorter events, 19.3 us)
Async XLA Ops:
  1.9 11.3 %collective-permute-start.2 = (bf16[2,128,512]{2,1,0:T(8,128)(2,1)S(1)}, bf16[2,128,512]{2,1,0:T(8,128)(2,1)}, u32[]{:S(2)}, u32[]{:S(2)}) collective-permute-start(bf16[2,128,512]{2,1,0:T(8,128)(2,1)S(1)} %get-tuple-element.30.refs_0_), channel_id=1, source_target_pairs={{0,2},{1,3},{2,0},{3,1},{4,6},{5,7},{6,4},{7,5},{8,10},{9,11},{10,... | collective-permute-start | bytes 786440 | tf_op jit(solution)/shard_map/ppermute | solution.py:468
  5.7 11.8 %collective-permute-start = (bf16[2,128,512]{2,1,0:T(8,128)(2,1)S(1)}, bf16[2,128,512]{2,1,0:T(8,128)(2,1)S(1)}, u32[]{:S(2)}, u32[]{:S(2)}) collective-permute-start(bf16[2,128,512]{2,1,0:T(8,128)(2,1)S(1)} %get-tuple-element.30.refs_0_), channel_id=1, source_target_pairs={{0,1},{1,0},{2,3},{3,2},{4,5},{5,4},{6,7},{7,6},{8,9},{9,8},{10,11... | collective-permute-start | bytes 786440 | tf_op jit(solution)/shard_map/ppermute | solution.py:468
  6.1 11.4 %collective-permute-start.1 = (bf16[2,128,512]{2,1,0:T(8,128)(2,1)S(1)}, bf16[2,128,512]{2,1,0:T(8,128)(2,1)S(1)}, u32[]{:S(2)}, u32[]{:S(2)}) collective-permute-start(bf16[2,128,512]{2,1,0:T(8,128)(2,1)S(1)} %get-tuple-element.30.refs_0_), channel_id=1, source_target_pairs={{0,3},{1,2},{2,1},{3,0},{4,7},{5,6},{6,5},{7,4},{8,11},{9,10},{10,... | collective-permute-start | bytes 786440 | tf_op jit(solution)/shard_map/ppermute | solution.py:468
  13.1 4.4 %copy-start = (bf16[125,1024]{1,0:T(8,128)(2,1)S(1)}, bf16[125,1024]{1,0:T(8,128)(2,1)}, u32[]{:S(2)}) copy-start(bf16[125,1024]{1,0:T(8,128)(2,1)} %refs_5_.1) | copy-start | bytes 768004
  13.1 4.4 %copy-start.1 = (s32[1,2,5]{2,1,0:T(2,128)S(1)}, s32[1,2,5]{2,1,0:T(2,128)}, u32[]{:S(2)}) copy-start(s32[1,2,5]{2,1,0:T(2,128)} %param.20) | copy-start | bytes 124
  13.1 4.4 %copy-start.3 = (bf16[1024,256]{1,0:T(8,128)(2,1)S(1)}, bf16[1024,256]{1,0:T(8,128)(2,1)}, u32[]{:S(2)}) copy-start(bf16[1024,256]{1,0:T(8,128)(2,1)} %constant.29.clone.refs_10_.refs_12_) | copy-start | bytes 1572868
  20.4 4.5 %collective-permute-start.3 = (bf16[16,1024]{1,0:T(8,128)(2,1)S(1)}, bf16[16,1024]{1,0:T(8,128)(2,1)S(1)}, u32[]{:S(2)}, u32[]{:S(2)}) collective-permute-start(bf16[16,1024]{1,0:T(8,128)(2,1)S(1)} %get-tuple-element.39), channel_id=1, source_target_pairs={{0,4},{4,0},{8,12},{12,8},{16,20},{20,16},{24,28},{28,24},{32,36},... | collective-permute-start | bytes 98312 | tf_op jit(solution)/shard_map/ppermute | solution.py:468
  21.9 5.2 %collective-permute-start.4 = (bf16[16,1024]{1,0:T(8,128)(2,1)S(1)}, bf16[16,1024]{1,0:T(8,128)(2,1)S(1)}, u32[]{:S(2)}, u32[]{:S(2)}) collective-permute-start(bf16[16,1024]{1,0:T(8,128)(2,1)S(1)} %get-tuple-element.40), channel_id=1, source_target_pairs={{4,8},{8,4},{12,16},{16,12},{20,24},{24,20},{28,32},{32,28},{36,40... | collective-permute-start | bytes 98312 | tf_op jit(solution)/shard_map/ppermute | solution.py:473
  28.9 9.0 %collective-permute-start.13 = (bf16[2,128,256]{2,1,0:T(8,128)(2,1)S(1)}, bf16[2,128,256]{2,1,0:T(8,128)(2,1)S(1)}, u32[]{:S(2)}, u32[]{:S(2)}) collective-permute-start(bf16[2,128,256]{2,1,0:T(8,128)(2,1)S(1)} %analysis.19), channel_id=1, source_target_pairs={{0,3},{1,2},{2,1},{3,0},{4,7},{5,6},{6,5},{7,4},{8,11},{9,10},{10,... | collective-permute-start | bytes 393224 | tf_op jit(solution)/shard_map/ppermute | solution.py:468
  31.8 7.9 %collective-permute-start.12 = (bf16[2,128,256]{2,1,0:T(8,128)(2,1)S(1)}, bf16[2,128,256]{2,1,0:T(8,128)(2,1)S(1)}, u32[]{:S(2)}, u32[]{:S(2)}) collective-permute-start(bf16[2,128,256]{2,1,0:T(8,128)(2,1)S(1)} %analysis.18), channel_id=1, source_target_pairs={{0,1},{1,0},{2,3},{3,2},{4,5},{5,4},{6,7},{7,6},{8,9},{9,8},{10,11... | collective-permute-start | bytes 393224 | tf_op jit(solution)/shard_map/ppermute | solution.py:468
  31.9 7.8 %collective-permute-start.11 = (bf16[2,128,256]{2,1,0:T(8,128)(2,1)S(1)}, bf16[2,128,256]{2,1,0:T(8,128)(2,1)S(1)}, u32[]{:S(2)}, u32[]{:S(2)}) collective-permute-start(bf16[2,128,256]{2,1,0:T(8,128)(2,1)S(1)} %analysis.17), channel_id=1, source_target_pairs={{0,2},{1,3},{2,0},{3,1},{4,6},{5,7},{6,4},{7,5},{8,10},{9,11},{10,... | collective-permute-start | bytes 393224 | tf_op jit(solution)/shard_map/ppermute | solution.py:468
  33.9 9.0 %collective-permute-start.7 = (bf16[2,128,256]{2,1,0:T(8,128)(2,1)S(1)}, bf16[2,128,256]{2,1,0:T(8,128)(2,1)S(1)}, u32[]{:S(2)}, u32[]{:S(2)}) collective-permute-start(bf16[2,128,256]{2,1,0:T(8,128)(2,1)S(1)} %analysis.15), channel_id=1, source_target_pairs={{0,3},{1,2},{2,1},{3,0},{4,7},{5,6},{6,5},{7,4},{8,11},{9,10},{10,... | collective-permute-start | bytes 393224 | tf_op jit(solution)/shard_map/ppermute | solution.py:468
  36.8 6.9 %collective-permute-start.6 = (bf16[2,128,256]{2,1,0:T(8,128)(2,1)S(1)}, bf16[2,128,256]{2,1,0:T(8,128)(2,1)S(1)}, u32[]{:S(2)}, u32[]{:S(2)}) collective-permute-start(bf16[2,128,256]{2,1,0:T(8,128)(2,1)S(1)} %analysis.14), channel_id=1, source_target_pairs={{0,1},{1,0},{2,3},{3,2},{4,5},{5,4},{6,7},{7,6},{8,9},{9,8},{10,11... | collective-permute-start | bytes 393224 | tf_op jit(solution)/shard_map/ppermute | solution.py:468
  37.9 7.4 %collective-permute-start.5 = (bf16[2,128,256]{2,1,0:T(8,128)(2,1)S(1)}, bf16[2,128,256]{2,1,0:T(8,128)(2,1)S(1)}, u32[]{:S(2)}, u32[]{:S(2)}) collective-permute-start(bf16[2,128,256]{2,1,0:T(8,128)(2,1)S(1)} %analysis.13), channel_id=1, source_target_pairs={{0,2},{1,3},{2,0},{3,1},{4,6},{5,7},{6,4},{7,5},{8,10},{9,11},{10,... | collective-permute-start | bytes 393224 | tf_op jit(solution)/shard_map/ppermute | solution.py:468
  39.8 8.6 %collective-permute-start.14 = (bf16[2,128,256]{2,1,0:T(8,128)(2,1)S(1)}, bf16[2,128,256]{2,1,0:T(8,128)(2,1)S(1)}, u32[]{:S(2)}, u32[]{:S(2)}) collective-permute-start(bf16[2,128,256]{2,1,0:T(8,128)(2,1)S(1)} %get-tuple-element.43.refs_0_), channel_id=1, source_target_pairs={{0,2},{1,3},{2,0},{3,1},{4,6},{5,7},{6,4},{7,5},{8,10},{9,11},{10,... | collective-permute-start | bytes 393224 | tf_op jit(solution)/shard_map/ppermute | solution.py:468
  41.4 7.5 %collective-permute-start.15 = (bf16[2,128,256]{2,1,0:T(8,128)(2,1)S(1)}, bf16[2,128,256]{2,1,0:T(8,128)(2,1)S(1)}, u32[]{:S(2)}, u32[]{:S(2)}) collective-permute-start(bf16[2,128,256]{2,1,0:T(8,128)(2,1)S(1)} %get-tuple-element.43.refs_0_), channel_id=1, source_target_pairs={{0,1},{1,0},{2,3},{3,2},{4,5},{5,4},{6,7},{7,6},{8,9},{9,8},{10,11... | collective-permute-start | bytes 393224 | tf_op jit(solution)/shard_map/ppermute | solution.py:468
  42.9 9.7 %collective-permute-start.16 = (bf16[2,128,256]{2,1,0:T(8,128)(2,1)S(1)}, bf16[2,128,256]{2,1,0:T(8,128)(2,1)S(1)}, u32[]{:S(2)}, u32[]{:S(2)}) collective-permute-start(bf16[2,128,256]{2,1,0:T(8,128)(2,1)S(1)} %get-tuple-element.43.refs_0_), channel_id=1, source_target_pairs={{0,3},{1,2},{2,1},{3,0},{4,7},{5,6},{6,5},{7,4},{8,11},{9,10},{10,... | collective-permute-start | bytes 393224 | tf_op jit(solution)/shard_map/ppermute | solution.py:468
  45.4 9.5 %collective-permute-start.10 = (bf16[2,128,256]{2,1,0:T(8,128)(2,1)S(1)}, bf16[2,128,256]{2,1,0:T(8,128)(2,1)S(1)}, u32[]{:S(2)}, u32[]{:S(2)}) collective-permute-start(bf16[2,128,256]{2,1,0:T(8,128)(2,1)S(1)} %get-tuple-element.42.refs_0_), channel_id=1, source_target_pairs={{0,3},{1,2},{2,1},{3,0},{4,7},{5,6},{6,5},{7,4},{8,11},{9,10},{10,... | collective-permute-start | bytes 393224 | tf_op jit(solution)/shard_map/ppermute | solution.py:468
  46.5 8.4 %collective-permute-start.8 = (bf16[2,128,256]{2,1,0:T(8,128)(2,1)S(1)}, bf16[2,128,256]{2,1,0:T(8,128)(2,1)S(1)}, u32[]{:S(2)}, u32[]{:S(2)}) collective-permute-start(bf16[2,128,256]{2,1,0:T(8,128)(2,1)S(1)} %get-tuple-element.42.refs_0_), channel_id=1, source_target_pairs={{0,2},{1,3},{2,0},{3,1},{4,6},{5,7},{6,4},{7,5},{8,10},{9,11},{10,... | collective-permute-start | bytes 393224 | tf_op jit(solution)/shard_map/ppermute | solution.py:468
  48.5 6.4 %collective-permute-start.9 = (bf16[2,128,256]{2,1,0:T(8,128)(2,1)S(1)}, bf16[2,128,256]{2,1,0:T(8,128)(2,1)S(1)}, u32[]{:S(2)}, u32[]{:S(2)}) collective-permute-start(bf16[2,128,256]{2,1,0:T(8,128)(2,1)S(1)} %get-tuple-element.42.refs_0_), channel_id=1, source_target_pairs={{0,1},{1,0},{2,3},{3,2},{4,5},{5,4},{6,7},{7,6},{8,9},{9,8},{10,11... | collective-permute-start | bytes 393224 | tf_op jit(solution)/shard_map/ppermute | solution.py:468
  58.5 4.5 %collective-permute-start.19 = (f32[8,256]{1,0:T(8,128)S(1)}, f32[8,256]{1,0:T(8,128)S(1)}, u32[]{:S(2)}, u32[]{:S(2)}) collective-permute-start(f32[8,256]{1,0:T(8,128)S(1)} %get-tuple-element.47.refs_0_), channel_id=1, source_target_pairs={{0,32},{4,36},{8,40},{12,44},{16,48},{20,52},{24,56},{28,60},{32,0... | collective-permute-start | bytes 24584 | tf_op jit(solution)/shard_map/ppermute | solution.py:468
  60.7 10.3 %collective-permute-start.17 = (bf16[2,128,512]{2,1,0:T(8,128)(2,1)S(1)}, bf16[2,128,512]{2,1,0:T(8,128)(2,1)S(1)}, u32[]{:S(2)}, u32[]{:S(2)}) collective-permute-start(bf16[2,128,512]{2,1,0:T(8,128)(2,1)S(1)} %analysis.21), channel_id=1, source_target_pairs={{0,2},{1,3},{2,0},{3,1},{4,6},{5,7},{6,4},{7,5},{8,10},{9,11},{10,... | collective-permute-start | bytes 786440 | tf_op jit(solution)/shard_map/ppermute | solution.py:468
  62.5 11.3 %collective-permute-start.18 = (bf16[2,128,512]{2,1,0:T(8,128)(2,1)S(1)}, bf16[2,128,512]{2,1,0:T(8,128)(2,1)S(1)}, u32[]{:S(2)}, u32[]{:S(2)}) collective-permute-start(bf16[2,128,512]{2,1,0:T(8,128)(2,1)S(1)} %analysis.22), channel_id=1, source_target_pairs={{0,1},{1,0},{2,3},{3,2},{4,5},{5,4},{6,7},{7,6},{8,9},{9,8},{10,11... | collective-permute-start | bytes 786440 | tf_op jit(solution)/shard_map/ppermute | solution.py:468
  63.8 9.9 %collective-permute-start.20 = (bf16[2,128,512]{2,1,0:T(8,128)(2,1)S(1)}, bf16[2,128,512]{2,1,0:T(8,128)(2,1)S(1)}, u32[]{:S(2)}, u32[]{:S(2)}) collective-permute-start(bf16[2,128,512]{2,1,0:T(8,128)(2,1)S(1)} %analysis.23), channel_id=1, source_target_pairs={{0,3},{1,2},{2,1},{3,0},{4,7},{5,6},{6,5},{7,4},{8,11},{9,10},{10,... | collective-permute-start | bytes 786440 | tf_op jit(solution)/shard_map/ppermute | solution.py:468
  64.9 6.1 %collective-permute-start.23 = (f32[16,256]{1,0:T(8,128)S(1)}, f32[16,256]{1,0:T(8,128)S(1)}, u32[]{:S(2)}, u32[]{:S(2)}) collective-permute-start(f32[16,256]{1,0:T(8,128)S(1)} %join.4.refs_0_), channel_id=1, source_target_pairs={{0,224},{4,228},{8,232},{12,236},{16,240},{20,244},{24,248},{28,25... | collective-permute-start | bytes 49160 | tf_op jit(solution)/shard_map/ppermute | solution.py:468
  71.0 13.9 %collective-permute-start.24 = (f32[32,256]{1,0:T(8,128)S(1)}, f32[32,256]{1,0:T(8,128)S(1)}, u32[]{:S(2)}, u32[]{:S(2)}) collective-permute-start(f32[32,256]{1,0:T(8,128)S(1)} %join.5.refs_0_), channel_id=1, source_target_pairs={{0,64},{4,68},{8,72},{12,76},{16,80},{20,84},{24,88},{28,92},{32,9... | collective-permute-start | bytes 98312 | tf_op jit(solution)/shard_map/ppermute | solution.py:468
  74.5 12.3 %collective-permute-start.21 = (f32[16,512]{1,0:T(8,128)S(1)}, f32[16,512]{1,0:T(8,128)S(1)}, u32[]{:S(2)}, u32[]{:S(2)}) collective-permute-start(f32[16,512]{1,0:T(8,128)S(1)} %get-tuple-element.50), channel_id=1, source_target_pairs={{0,4},{4,0},{8,12},{12,8},{16,20},{20,16},{24,28},{28,24},{32,36},... | collective-permute-start | bytes 98312 | tf_op jit(solution)/shard_map/ppermute | solution.py:468
  83.0 5.9 %collective-permute-start.22 = (f32[16,512]{1,0:T(8,128)S(1)}, f32[16,512]{1,0:T(8,128)S(1)}, u32[]{:S(2)}, u32[]{:S(2)}) collective-permute-start(f32[16,512]{1,0:T(8,128)S(1)} %get-tuple-element.51), channel_id=1, source_target_pairs={{4,8},{8,4},{12,16},{16,12},{20,24},{24,20},{28,32},{32,28},{36,40... | collective-permute-start | bytes 98312 | tf_op jit(solution)/shard_map/ppermute | solution.py:473
  84.9 6.4 %collective-permute-start.25 = (f32[64,256]{1,0:T(8,128)S(1)}, f32[64,256]{1,0:T(8,128)S(1)}, u32[]{:S(2)}, u32[]{:S(2)}) collective-permute-start(f32[64,256]{1,0:T(8,128)S(1)} %join.6.refs_0_), channel_id=1, source_target_pairs={{0,16},{4,20},{8,24},{12,28},{16,0},{20,4},{24,8},{28,12},{32,48},... | collective-permute-start | bytes 196616 | tf_op jit(solution)/shard_map/ppermute | solution.py:468
  86.8 4.5 %collective-permute-start.26 = (f32[64,256]{1,0:T(8,128)S(1)}, f32[64,256]{1,0:T(8,128)S(1)}, u32[]{:S(2)}, u32[]{:S(2)}) collective-permute-start(f32[64,256]{1,0:T(8,128)S(1)} %join.6.refs_0_), channel_id=1, source_target_pairs={{0,8},{4,12},{8,0},{12,4},{16,24},{20,28},{24,16},{28,20},{32,40},... | collective-permute-start | bytes 196616 | tf_op jit(solution)/shard_map/ppermute | solution.py:468
  88.8 4.3 %collective-permute-start.27 = (f32[64,256]{1,0:T(8,128)S(1)}, f32[64,256]{1,0:T(8,128)S(1)}, u32[]{:S(2)}, u32[]{:S(2)}) collective-permute-start(f32[64,256]{1,0:T(8,128)S(1)} %join.6.refs_0_), channel_id=1, source_target_pairs={{0,24},{4,28},{8,16},{12,20},{16,8},{20,12},{24,0},{28,4},{32,56},... | collective-permute-start | bytes 196616 | tf_op jit(solution)/shard_map/ppermute | solution.py:468
  93.2 2.2 %collective-permute-start.28 = (f32[256,256]{1,0:T(8,128)S(1)}, f32[256,256]{1,0:T(8,128)S(1)}, u32[]{:S(2)}, u32[]{:S(2)}) collective-permute-start(f32[256,256]{1,0:T(8,128)S(1)} %join.7.rows_ref), channel_id=1, source_target_pairs={{0,4},{4,0},{8,12},{12,8},{16,20},{20,16},{24,28},{28,24},{32,36},... | collective-permute-start | bytes 786440 | tf_op jit(solution)/shard_map/ppermute | solution.py:468
  (5 other events, 16.6 us)

commit v6 on v5

--- a/solution.py
+++ b/solution.py
@@ -390,7 +390,7 @@
 
 
 def shared(mer, nodes, parts):
-    rows = jax.ShapeDtypeStruct((16, parts[0].shape[2]), f32)
+    rows = jax.ShapeDtypeStruct((16, parts[0].shape[2]), bf16)
     outs = [jax.ShapeDtypeStruct(parts[0].shape, f32), rows, rows]
     return call(shared_kernel, "shared", outs, [mer, nodes, *parts], 2, us=0.5)
 
@@ -399,7 +399,7 @@
     *now_refs, prev_ref, column_ref, out_ref, total_ref = refs
     total_ref[...] = force_ref[...]
     for r_ref, side in zip((core_ref, chip_ref), sides(mer_ref)):
-        rows = r_ref[...]
+        rows = r_ref[...].astype(f32)
         for c in range(2):
             for k in range(nodes_ref.shape[1]):
                 at = 8 * c + k

time: 97 us -> 99 us (1.021)
  waiting for transfers between devices: 15.2 us -> 18.5 us
  starting transfers between devices: 51.3 us -> 50.3 us
    ppermute x27, waiting for transfers between devices: 10.9 us -> 13.2 us  [swapped(): lax.ppermute(x, axis, [(i, i ^ bits) for i in range(lax.axis_size(axis))])]
    ppermute x2, waiting for transfers between devices: 4.26 us -> 5.3 us  [across_chips(): lax.ppermute(x, 'mer', [(i, i + 1 if i % 2 else i - 1) for i in ends])]
  transfers between devices with their start and end apart: 29 -> 29, of which waited for: 9 -> 10; matrix products, arithmetic and copies ran while one was open for 0% -> 0% of each run, Pallas kernels for 17% -> 17%
where the time goes in v6:
time: 99 us; the launch traced here: 98.8 us
  starting transfers between devices  50.3 us (51%)
  Pallas kernels  27.3 us (28%)
  waiting for transfers between devices  18.5 us (19%)
  local copies, waits for them, and re-layouts  1.63 us (2%)
  between operations  1.02 us (1%)
    ppermute x27, starting transfers between devices, swapped(): lax.ppermute(x, axis, [(i, i ^ bits) for i in range(lax.axis_size(axis))])  45.4 us
    pallas_call x29, Pallas kernels, call(): pl.pallas_call(kernel, in_specs=[SMEM] * scalars + [VMEM] * (len(operands...  24.9 us
    ppermute x27, waiting for transfers between devices, swapped(): lax.ppermute(x, axis, [(i, i ^ bits) for i in range(lax.axis_size(axis))])  13.2 us
    ppermute x2, waiting for transfers between devices, across_chips(): lax.ppermute(x, 'mer', [(i, i + 1 if i % 2 else i - 1) for i in ends])  5.3 us
    ppermute x2, starting transfers between devices, across_chips(): lax.ppermute(x, 'mer', [(i, i + 1 if i % 2 else i - 1) for i in ends])  4.91 us
    pallas_call x2, Pallas kernels, arrange(): pl.pallas_call(arrange_kernel, in_specs=[SMEM, hbm, hbm], out_specs=[VMEM...  2.4 us
  transfers between devices with their start and end apart: 29, of which 10 were waited for; matrix products, arithmetic and copies ran while one was open for 0% of the time, Pallas kernels for 17%

profile of v6, /device:TPU:1, one launch (start us, length us, event | category | flops | bytes accessed | tf_op | source)
XLA Modules:
  0.0 98.8 jit_solution(12670105782625976647)
XLA Ops:
  0.6 1.2 %arrange.2 = (f32[2,128,512]{2,1,0:T(8,128)S(1)}, bf16[2,128,512]{2,1,0:T(8,128)(2,1)S(1)}) custom-call(s32[1,1]{1,0:T(1,128)} %bitcast.blk_ref, s32[1,5]{1,0:T(1,128)} %bitcast.12, f32[125,2,512]{2,1,0:T(2,128)} %disp_hbm.2), custom_call_target="tpu_custom_call" | custom-call | tf_op jit(solution)/shard_map/arrange/pallas_call | solution.py:178
  1.9 3.8 %collective-permute-start.2 = (bf16[2,128,512]{2,1,0:T(8,128)(2,1)S(1)}, bf16[2,128,512]{2,1,0:T(8,128)(2,1)}, u32[]{:S(2)}, u32[]{:S(2)}) collective-permute-start(bf16[2,128,512]{2,1,0:T(8,128)(2,1)S(1)} %get-tuple-element.30.refs_0_), channel_id=1, source_target_pairs={{0,2},{1,3},{2,0},{3,1},{4,6},{5,7},{6,4},{7,5},{8,10},{9,11},{10,... | collective-permute-start | bytes 786440 | tf_op jit(solution)/shard_map/ppermute | solution.py:468
  7.6 1.2 %arrange.3.prev_ref = f32[2,128,512]{2,1,0:T(8,128)S(1)} custom-call(s32[1,1]{1,0:T(1,128)} %bitcast.blk_ref, s32[1,5]{1,0:T(1,128)} %bitcast.14, f32[125,2,512]{2,1,0:T(2,128)} %disp_hbm.3), custom_call_target="tpu_custom_call" | custom-call | tf_op jit(solution)/shard_map/arrange/pallas_call | solution.py:178
  10.4 2.7 %table.1.refs_2_.refs_5_.table_ref.refs_4_.refs_7_ = bf16[2,2048,1024]{2,1,0:T(8,128)(2,1)S(1)} custom-call(s32[1,1]{1,0:T(1,128)} %bitcast.blk_ref, f32[2,96,1024]{2,1,0:T(8,128)S(1)} %copy-done.2), custom_call_target="tpu_custom_call" | custom-call | flops 3449999872 | tf_op jit(solution)/shard_map/table/pallas_call | solution.py:107
  13.2 2.3 %early.2.refs_2_ = f32[256,1024]{1,0:T(8,128)S(1)} custom-call(s32[1,1]{1,0:T(1,128)} %bitcast.blk_ref, bf16[2,128,512]{2,1,0:T(8,128)(2,1)S(1)} %get-tuple-element.30.refs_0_, bf16[2,128,512]{2,1,0:T(8,128)(2,1)} %collective-permute-done.2.refs_1_, bf16[2,2048,1024]{2,1,0:T(8,128)(2,1)S(1)} %table.1.refs_2_.refs_5_.table_ref.refs_4_.refs_7_), custom_call_target="tpu_custom_call" | custom-call | flops 4485000192 | tf_op jit(solution)/shard_map/early/pallas_call | solution.py:107
  15.5 2.0 %collective-permute-done.refs_0_ = bf16[2,128,512]{2,1,0:T(8,128)(2,1)S(1)} collective-permute-done((bf16[2,128,512]{2,1,0:T(8,128)(2,1)S(1)}, bf16[2,128,512]{2,1,0:T(8,128)(2,1)S(1)}, u32[]{:S(2)}, u32[]{:S(2)}) %collective-permute-start) | collective-permute-done | bytes 262176 | tf_op jit(solution)/shard_map/ppermute | solution.py:468
  17.5 2.8 %synthesis.2 = (f32[256,1024]{1,0:T(8,128)S(1)}, f32[8,256]{1,0:T(8,128)S(1)}, bf16[16,1024]{1,0:T(8,128)(2,1)S(1)}, bf16[16,1024]{1,0:T(8,128)(2,1)S(1)}) custom-call(s32[1,1]{1,0:T(1,128)} %bitcast.blk_ref, s32[1,1]{1,0:T(1,128)} %bitcast.1.mer_ref, s32[2,5]{1,0:T(2,128)S(1)} %bitcast.7, bf16[2,128,512]{2,1,0:T(8,128)(2,1)S(1)} %collective-permute-done.refs_0_, ...), custom_call_target="tpu_custom_call" | custom-call | flops 10350000128 | tf_op jit(solution)/shard_map/synthesis/pallas_call | solution.py:107
  20.4 1.5 %collective-permute-start.3 = (bf16[16,1024]{1,0:T(8,128)(2,1)S(1)}, bf16[16,1024]{1,0:T(8,128)(2,1)S(1)}, u32[]{:S(2)}, u32[]{:S(2)}) collective-permute-start(bf16[16,1024]{1,0:T(8,128)(2,1)S(1)} %get-tuple-element.39), channel_id=1, source_target_pairs={{0,4},{4,0},{8,12},{12,8},{16,20},{20,16},{24,28},{28,24},{32,36},... | collective-permute-start | bytes 98312 | tf_op jit(solution)/shard_map/ppermute | solution.py:468
  21.9 3.0 %collective-permute-start.4 = (bf16[16,1024]{1,0:T(8,128)(2,1)S(1)}, bf16[16,1024]{1,0:T(8,128)(2,1)S(1)}, u32[]{:S(2)}, u32[]{:S(2)}) collective-permute-start(bf16[16,1024]{1,0:T(8,128)(2,1)S(1)} %get-tuple-element.40), channel_id=1, source_target_pairs={{4,8},{8,4},{12,16},{16,12},{20,24},{24,20},{28,32},{32,28},{36,40... | collective-permute-start | bytes 98312 | tf_op jit(solution)/shard_map/ppermute | solution.py:473
  24.9 2.2 %collective-permute-done.4.chip_ref = bf16[16,1024]{1,0:T(8,128)(2,1)S(1)} collective-permute-done((bf16[16,1024]{1,0:T(8,128)(2,1)S(1)}, bf16[16,1024]{1,0:T(8,128)(2,1)S(1)}, u32[]{:S(2)}, u32[]{:S(2)}) %collective-permute-start.4) | collective-permute-done | bytes 32800 | tf_op jit(solution)/shard_map/ppermute | solution.py:473
  28.9 2.4 %collective-permute-start.13 = (bf16[2,128,256]{2,1,0:T(8,128)(2,1)S(1)}, bf16[2,128,256]{2,1,0:T(8,128)(2,1)S(1)}, u32[]{:S(2)}, u32[]{:S(2)}) collective-permute-start(bf16[2,128,256]{2,1,0:T(8,128)(2,1)S(1)} %analysis.19), channel_id=1, source_target_pairs={{0,3},{1,2},{2,1},{3,0},{4,7},{5,6},{6,5},{7,4},{8,11},{9,10},{10,... | collective-permute-start | bytes 393224 | tf_op jit(solution)/shard_map/ppermute | solution.py:468
  31.9 1.5 %collective-permute-start.11 = (bf16[2,128,256]{2,1,0:T(8,128)(2,1)S(1)}, bf16[2,128,256]{2,1,0:T(8,128)(2,1)S(1)}, u32[]{:S(2)}, u32[]{:S(2)}) collective-permute-start(bf16[2,128,256]{2,1,0:T(8,128)(2,1)S(1)} %analysis.17), channel_id=1, source_target_pairs={{0,2},{1,3},{2,0},{3,1},{4,6},{5,7},{6,4},{7,5},{8,10},{9,11},{10,... | collective-permute-start | bytes 393224 | tf_op jit(solution)/shard_map/ppermute | solution.py:468
  33.9 2.4 %collective-permute-start.7 = (bf16[2,128,256]{2,1,0:T(8,128)(2,1)S(1)}, bf16[2,128,256]{2,1,0:T(8,128)(2,1)S(1)}, u32[]{:S(2)}, u32[]{:S(2)}) collective-permute-start(bf16[2,128,256]{2,1,0:T(8,128)(2,1)S(1)} %analysis.15), channel_id=1, source_target_pairs={{0,3},{1,2},{2,1},{3,0},{4,7},{5,6},{6,5},{7,4},{8,11},{9,10},{10,... | collective-permute-start | bytes 393224 | tf_op jit(solution)/shard_map/ppermute | solution.py:468
  37.9 1.8 %collective-permute-start.5 = (bf16[2,128,256]{2,1,0:T(8,128)(2,1)S(1)}, bf16[2,128,256]{2,1,0:T(8,128)(2,1)S(1)}, u32[]{:S(2)}, u32[]{:S(2)}) collective-permute-start(bf16[2,128,256]{2,1,0:T(8,128)(2,1)S(1)} %analysis.13), channel_id=1, source_target_pairs={{0,2},{1,3},{2,0},{3,1},{4,6},{5,7},{6,4},{7,5},{8,10},{9,11},{10,... | collective-permute-start | bytes 393224 | tf_op jit(solution)/shard_map/ppermute | solution.py:468
  39.9 1.6 %collective-permute-start.14 = (bf16[2,128,256]{2,1,0:T(8,128)(2,1)S(1)}, bf16[2,128,256]{2,1,0:T(8,128)(2,1)S(1)}, u32[]{:S(2)}, u32[]{:S(2)}) collective-permute-start(bf16[2,128,256]{2,1,0:T(8,128)(2,1)S(1)} %get-tuple-element.43.refs_0_), channel_id=1, source_target_pairs={{0,2},{1,3},{2,0},{3,1},{4,6},{5,7},{6,4},{7,5},{8,10},{9,11},{10,... | collective-permute-start | bytes 393224 | tf_op jit(solution)/shard_map/ppermute | solution.py:468
  41.4 1.4 %collective-permute-start.15 = (bf16[2,128,256]{2,1,0:T(8,128)(2,1)S(1)}, bf16[2,128,256]{2,1,0:T(8,128)(2,1)S(1)}, u32[]{:S(2)}, u32[]{:S(2)}) collective-permute-start(bf16[2,128,256]{2,1,0:T(8,128)(2,1)S(1)} %get-tuple-element.43.refs_0_), channel_id=1, source_target_pairs={{0,1},{1,0},{2,3},{3,2},{4,5},{5,4},{6,7},{7,6},{8,9},{9,8},{10,11... | collective-permute-start | bytes 393224 | tf_op jit(solution)/shard_map/ppermute | solution.py:468
  43.7 1.5 %collective-permute-done.5.b_ref = bf16[2,128,256]{2,1,0:T(8,128)(2,1)S(1)} collective-permute-done((bf16[2,128,256]{2,1,0:T(8,128)(2,1)S(1)}, bf16[2,128,256]{2,1,0:T(8,128)(2,1)S(1)}, u32[]{:S(2)}, u32[]{:S(2)}) %collective-permute-start.5) | collective-permute-done | bytes 131104 | tf_op jit(solution)/shard_map/ppermute | solution.py:468
  46.5 2.0 %collective-permute-start.8 = (bf16[2,128,256]{2,1,0:T(8,128)(2,1)S(1)}, bf16[2,128,256]{2,1,0:T(8,128)(2,1)S(1)}, u32[]{:S(2)}, u32[]{:S(2)}) collective-permute-start(bf16[2,128,256]{2,1,0:T(8,128)(2,1)S(1)} %get-tuple-element.42.refs_0_), channel_id=1, source_target_pairs={{0,2},{1,3},{2,0},{3,1},{4,6},{5,7},{6,4},{7,5},{8,10},{9,11},{10,... | collective-permute-start | bytes 393224 | tf_op jit(solution)/shard_map/ppermute | solution.py:468
  48.9 3.7 %collective-permute-done.16.refs_3_ = bf16[2,128,256]{2,1,0:T(8,128)(2,1)S(1)} collective-permute-done((bf16[2,128,256]{2,1,0:T(8,128)(2,1)S(1)}, bf16[2,128,256]{2,1,0:T(8,128)(2,1)S(1)}, u32[]{:S(2)}, u32[]{:S(2)}) %collective-permute-start.16) | collective-permute-done | bytes 131104 | tf_op jit(solution)/shard_map/ppermute | solution.py:468
  52.6 1.3 %early.3.refs_4_ = f32[256,1024]{1,0:T(8,128)S(1)} custom-call(s32[1,1]{1,0:T(1,128)} %bitcast.blk_ref, bf16[2,128,256]{2,1,0:T(8,128)(2,1)S(1)} %get-tuple-element.43.refs_0_, bf16[2,128,256]{2,1,0:T(8,128)(2,1)S(1)} %collective-permute-done.14.refs_1_, bf16[2,128,256]{2,1,0:T(8,128)(2,1)S(1)} %collective-permute-done.15.refs_2_, ...), custom_call_target="tpu_custom_call" | custom-call | flops 4485000192 | tf_op jit(solution)/shard_map/early/pallas_call | solution.py:107
  54.9 2.9 %synthesis.3 = (bf16[256,1024]{1,0:T(8,128)(2,1)S(1)}, f32[8,256]{1,0:T(8,128)S(1)}) custom-call(s32[1,1]{1,0:T(1,128)} %bitcast.blk_ref, s32[1,1]{1,0:T(1,128)} %bitcast.1.mer_ref, s32[2,5]{1,0:T(2,128)S(1)} %bitcast.9, bf16[2,128,256]{2,1,0:T(8,128)(2,1)S(1)} %get-tuple-element.42.refs_0_, bf16[2,128,256]{2,1,0:T(8,128)(2,1)S(1)} %collective-permute-done.8.refs_1_, ...), custom_call_target="tpu_custom_call" | custom-call | flops 10350000128 | tf_op jit(solution)/shard_map/synthesis/pallas_call | solution.py:107
  58.5 1.4 %collective-permute-start.19 = (f32[8,256]{1,0:T(8,128)S(1)}, f32[8,256]{1,0:T(8,128)S(1)}, u32[]{:S(2)}, u32[]{:S(2)}) collective-permute-start(f32[8,256]{1,0:T(8,128)S(1)} %get-tuple-element.47.refs_0_), channel_id=1, source_target_pairs={{0,32},{4,36},{8,40},{12,44},{16,48},{20,52},{24,56},{28,60},{32,0... | collective-permute-start | bytes 24584 | tf_op jit(solution)/shard_map/ppermute | solution.py:468
  60.7 1.7 %collective-permute-start.17 = (bf16[2,128,512]{2,1,0:T(8,128)(2,1)S(1)}, bf16[2,128,512]{2,1,0:T(8,128)(2,1)S(1)}, u32[]{:S(2)}, u32[]{:S(2)}) collective-permute-start(bf16[2,128,512]{2,1,0:T(8,128)(2,1)S(1)} %analysis.21), channel_id=1, source_target_pairs={{0,2},{1,3},{2,0},{3,1},{4,6},{5,7},{6,4},{7,5},{8,10},{9,11},{10,... | collective-permute-start | bytes 786440 | tf_op jit(solution)/shard_map/ppermute | solution.py:468
  64.9 4.7 %collective-permute-start.23 = (f32[16,256]{1,0:T(8,128)S(1)}, f32[16,256]{1,0:T(8,128)S(1)}, u32[]{:S(2)}, u32[]{:S(2)}) collective-permute-start(f32[16,256]{1,0:T(8,128)S(1)} %join.4.refs_0_), channel_id=1, source_target_pairs={{0,224},{4,228},{8,232},{12,236},{16,240},{20,244},{24,248},{28,25... | collective-permute-start | bytes 49160 | tf_op jit(solution)/shard_map/ppermute | solution.py:468
  71.0 2.7 %collective-permute-start.24 = (f32[32,256]{1,0:T(8,128)S(1)}, f32[32,256]{1,0:T(8,128)S(1)}, u32[]{:S(2)}, u32[]{:S(2)}) collective-permute-start(f32[32,256]{1,0:T(8,128)S(1)} %join.5.refs_0_), channel_id=1, source_target_pairs={{0,64},{4,68},{8,72},{12,76},{16,80},{20,84},{24,88},{28,92},{32,9... | collective-permute-start | bytes 98312 | tf_op jit(solution)/shard_map/ppermute | solution.py:468
  74.5 8.5 %collective-permute-start.21 = (bf16[16,512]{1,0:T(8,128)(2,1)S(1)}, bf16[16,512]{1,0:T(8,128)(2,1)S(1)}, u32[]{:S(2)}, u32[]{:S(2)}) collective-permute-start(bf16[16,512]{1,0:T(8,128)(2,1)S(1)} %get-tuple-element.50), channel_id=1, source_target_pairs={{0,4},{4,0},{8,12},{12,8},{16,20},{20,16},{24,28},{28,24},{32,36},... | collective-permute-start | bytes 49160 | tf_op jit(solution)/shard_map/ppermute | solution.py:468
  83.0 1.9 %collective-permute-start.22 = (bf16[16,512]{1,0:T(8,128)(2,1)S(1)}, bf16[16,512]{1,0:T(8,128)(2,1)S(1)}, u32[]{:S(2)}, u32[]{:S(2)}) collective-permute-start(bf16[16,512]{1,0:T(8,128)(2,1)S(1)} %get-tuple-element.51), channel_id=1, source_target_pairs={{4,8},{8,4},{12,16},{16,12},{20,24},{24,20},{28,32},{32,28},{36,40... | collective-permute-start | bytes 49160 | tf_op jit(solution)/shard_map/ppermute | solution.py:473
  84.9 3.1 %collective-permute-done.22.chip_ref = bf16[16,512]{1,0:T(8,128)(2,1)S(1)} collective-permute-done((bf16[16,512]{1,0:T(8,128)(2,1)S(1)}, bf16[16,512]{1,0:T(8,128)(2,1)S(1)}, u32[]{:S(2)}, u32[]{:S(2)}) %collective-permute-start.22) | collective-permute-done | bytes 16416 | tf_op jit(solution)/shard_map/ppermute | solution.py:473
  88.0 2.8 %collective-permute-start.27 = (f32[64,256]{1,0:T(8,128)S(1)}, f32[64,256]{1,0:T(8,128)S(1)}, u32[]{:S(2)}, u32[]{:S(2)}) collective-permute-start(f32[64,256]{1,0:T(8,128)S(1)} %join.6.refs_0_), channel_id=1, source_target_pairs={{0,24},{4,28},{8,16},{12,20},{16,8},{20,12},{24,0},{28,4},{32,56},... | collective-permute-start | bytes 196616 | tf_op jit(solution)/shard_map/ppermute | solution.py:468
  91.4 1.3 %collective-permute-done.27.refs_3_ = f32[64,256]{1,0:T(8,128)S(1)} collective-permute-done((f32[64,256]{1,0:T(8,128)S(1)}, f32[64,256]{1,0:T(8,128)S(1)}, u32[]{:S(2)}, u32[]{:S(2)}) %collective-permute-start.27) | collective-permute-done | bytes 65568 | tf_op jit(solution)/shard_map/ppermute | solution.py:468
  92.7 2.8 %collective-permute-done.25.refs_1_ = f32[64,256]{1,0:T(8,128)S(1)} collective-permute-done((f32[64,256]{1,0:T(8,128)S(1)}, f32[64,256]{1,0:T(8,128)S(1)}, u32[]{:S(2)}, u32[]{:S(2)}) %collective-permute-start.25) | collective-permute-done | bytes 65568 | tf_op jit(solution)/shard_map/ppermute | solution.py:468
  95.6 1.7 %finish.1 = f32[125,2,512]{2,1,0:T(2,128)} custom-call(s32[1,1]{1,0:T(1,128)} %bitcast.blk_ref, s32[1,1]{1,0:T(1,128)} %bitcast.1.mer_ref, s32[2,5]{1,0:T(2,128)S(1)} %bitcast.11, f32[2,128,512]{2,1,0:T(8,128)S(1)} %get-tuple-element.49.force_ref, bf16[16,512]{1,0:T(8,128)(2,1)S(1)} %collective-permute-done.21.core_ref, ...), custom_call_target="tpu_custom_call" | custom-call | flops 4485000192 | tf_op jit(solution)/shard_map/finish/pallas_call | solution.py:107
  (75 shorter events, 19.9 us)
Async XLA Ops:
  1.9 11.3 %collective-permute-start.2 = (bf16[2,128,512]{2,1,0:T(8,128)(2,1)S(1)}, bf16[2,128,512]{2,1,0:T(8,128)(2,1)}, u32[]{:S(2)}, u32[]{:S(2)}) collective-permute-start(bf16[2,128,512]{2,1,0:T(8,128)(2,1)S(1)} %get-tuple-element.30.refs_0_), channel_id=1, source_target_pairs={{0,2},{1,3},{2,0},{3,1},{4,6},{5,7},{6,4},{7,5},{8,10},{9,11},{10,... | collective-permute-start | bytes 786440 | tf_op jit(solution)/shard_map/ppermute | solution.py:468
  5.7 11.8 %collective-permute-start = (bf16[2,128,512]{2,1,0:T(8,128)(2,1)S(1)}, bf16[2,128,512]{2,1,0:T(8,128)(2,1)S(1)}, u32[]{:S(2)}, u32[]{:S(2)}) collective-permute-start(bf16[2,128,512]{2,1,0:T(8,128)(2,1)S(1)} %get-tuple-element.30.refs_0_), channel_id=1, source_target_pairs={{0,1},{1,0},{2,3},{3,2},{4,5},{5,4},{6,7},{7,6},{8,9},{9,8},{10,11... | collective-permute-start | bytes 786440 | tf_op jit(solution)/shard_map/ppermute | solution.py:468
  6.1 11.4 %collective-permute-start.1 = (bf16[2,128,512]{2,1,0:T(8,128)(2,1)S(1)}, bf16[2,128,512]{2,1,0:T(8,128)(2,1)S(1)}, u32[]{:S(2)}, u32[]{:S(2)}) collective-permute-start(bf16[2,128,512]{2,1,0:T(8,128)(2,1)S(1)} %get-tuple-element.30.refs_0_), channel_id=1, source_target_pairs={{0,3},{1,2},{2,1},{3,0},{4,7},{5,6},{6,5},{7,4},{8,11},{9,10},{10,... | collective-permute-start | bytes 786440 | tf_op jit(solution)/shard_map/ppermute | solution.py:468
  13.1 4.4 %copy-start = (bf16[125,1024]{1,0:T(8,128)(2,1)S(1)}, bf16[125,1024]{1,0:T(8,128)(2,1)}, u32[]{:S(2)}) copy-start(bf16[125,1024]{1,0:T(8,128)(2,1)} %refs_5_.1) | copy-start | bytes 768004
  13.1 4.4 %copy-start.1 = (s32[1,2,5]{2,1,0:T(2,128)S(1)}, s32[1,2,5]{2,1,0:T(2,128)}, u32[]{:S(2)}) copy-start(s32[1,2,5]{2,1,0:T(2,128)} %param.20) | copy-start | bytes 124
  13.1 4.4 %copy-start.3 = (bf16[1024,256]{1,0:T(8,128)(2,1)S(1)}, bf16[1024,256]{1,0:T(8,128)(2,1)}, u32[]{:S(2)}) copy-start(bf16[1024,256]{1,0:T(8,128)(2,1)} %constant.29.clone.refs_10_.refs_12_) | copy-start | bytes 1572868
  20.4 4.5 %collective-permute-start.3 = (bf16[16,1024]{1,0:T(8,128)(2,1)S(1)}, bf16[16,1024]{1,0:T(8,128)(2,1)S(1)}, u32[]{:S(2)}, u32[]{:S(2)}) collective-permute-start(bf16[16,1024]{1,0:T(8,128)(2,1)S(1)} %get-tuple-element.39), channel_id=1, source_target_pairs={{0,4},{4,0},{8,12},{12,8},{16,20},{20,16},{24,28},{28,24},{32,36},... | collective-permute-start | bytes 98312 | tf_op jit(solution)/shard_map/ppermute | solution.py:468
  21.9 5.2 %collective-permute-start.4 = (bf16[16,1024]{1,0:T(8,128)(2,1)S(1)}, bf16[16,1024]{1,0:T(8,128)(2,1)S(1)}, u32[]{:S(2)}, u32[]{:S(2)}) collective-permute-start(bf16[16,1024]{1,0:T(8,128)(2,1)S(1)} %get-tuple-element.40), channel_id=1, source_target_pairs={{4,8},{8,4},{12,16},{16,12},{20,24},{24,20},{28,32},{32,28},{36,40... | collective-permute-start | bytes 98312 | tf_op jit(solution)/shard_map/ppermute | solution.py:473
  28.9 9.0 %collective-permute-start.13 = (bf16[2,128,256]{2,1,0:T(8,128)(2,1)S(1)}, bf16[2,128,256]{2,1,0:T(8,128)(2,1)S(1)}, u32[]{:S(2)}, u32[]{:S(2)}) collective-permute-start(bf16[2,128,256]{2,1,0:T(8,128)(2,1)S(1)} %analysis.19), channel_id=1, source_target_pairs={{0,3},{1,2},{2,1},{3,0},{4,7},{5,6},{6,5},{7,4},{8,11},{9,10},{10,... | collective-permute-start | bytes 393224 | tf_op jit(solution)/shard_map/ppermute | solution.py:468
  31.8 7.9 %collective-permute-start.12 = (bf16[2,128,256]{2,1,0:T(8,128)(2,1)S(1)}, bf16[2,128,256]{2,1,0:T(8,128)(2,1)S(1)}, u32[]{:S(2)}, u32[]{:S(2)}) collective-permute-start(bf16[2,128,256]{2,1,0:T(8,128)(2,1)S(1)} %analysis.18), channel_id=1, source_target_pairs={{0,1},{1,0},{2,3},{3,2},{4,5},{5,4},{6,7},{7,6},{8,9},{9,8},{10,11... | collective-permute-start | bytes 393224 | tf_op jit(solution)/shard_map/ppermute | solution.py:468
  31.9 7.8 %collective-permute-start.11 = (bf16[2,128,256]{2,1,0:T(8,128)(2,1)S(1)}, bf16[2,128,256]{2,1,0:T(8,128)(2,1)S(1)}, u32[]{:S(2)}, u32[]{:S(2)}) collective-permute-start(bf16[2,128,256]{2,1,0:T(8,128)(2,1)S(1)} %analysis.17), channel_id=1, source_target_pairs={{0,2},{1,3},{2,0},{3,1},{4,6},{5,7},{6,4},{7,5},{8,10},{9,11},{10,... | collective-permute-start | bytes 393224 | tf_op jit(solution)/shard_map/ppermute | solution.py:468
  33.9 9.0 %collective-permute-start.7 = (bf16[2,128,256]{2,1,0:T(8,128)(2,1)S(1)}, bf16[2,128,256]{2,1,0:T(8,128)(2,1)S(1)}, u32[]{:S(2)}, u32[]{:S(2)}) collective-permute-start(bf16[2,128,256]{2,1,0:T(8,128)(2,1)S(1)} %analysis.15), channel_id=1, source_target_pairs={{0,3},{1,2},{2,1},{3,0},{4,7},{5,6},{6,5},{7,4},{8,11},{9,10},{10,... | collective-permute-start | bytes 393224 | tf_op jit(solution)/shard_map/ppermute | solution.py:468
  36.8 6.9 %collective-permute-start.6 = (bf16[2,128,256]{2,1,0:T(8,128)(2,1)S(1)}, bf16[2,128,256]{2,1,0:T(8,128)(2,1)S(1)}, u32[]{:S(2)}, u32[]{:S(2)}) collective-permute-start(bf16[2,128,256]{2,1,0:T(8,128)(2,1)S(1)} %analysis.14), channel_id=1, source_target_pairs={{0,1},{1,0},{2,3},{3,2},{4,5},{5,4},{6,7},{7,6},{8,9},{9,8},{10,11... | collective-permute-start | bytes 393224 | tf_op jit(solution)/shard_map/ppermute | solution.py:468
  37.9 7.4 %collective-permute-start.5 = (bf16[2,128,256]{2,1,0:T(8,128)(2,1)S(1)}, bf16[2,128,256]{2,1,0:T(8,128)(2,1)S(1)}, u32[]{:S(2)}, u32[]{:S(2)}) collective-permute-start(bf16[2,128,256]{2,1,0:T(8,128)(2,1)S(1)} %analysis.13), channel_id=1, source_target_pairs={{0,2},{1,3},{2,0},{3,1},{4,6},{5,7},{6,4},{7,5},{8,10},{9,11},{10,... | collective-permute-start | bytes 393224 | tf_op jit(solution)/shard_map/ppermute | solution.py:468
  39.9 8.6 %collective-permute-start.14 = (bf16[2,128,256]{2,1,0:T(8,128)(2,1)S(1)}, bf16[2,128,256]{2,1,0:T(8,128)(2,1)S(1)}, u32[]{:S(2)}, u32[]{:S(2)}) collective-permute-start(bf16[2,128,256]{2,1,0:T(8,128)(2,1)S(1)} %get-tuple-element.43.refs_0_), channel_id=1, source_target_pairs={{0,2},{1,3},{2,0},{3,1},{4,6},{5,7},{6,4},{7,5},{8,10},{9,11},{10,... | collective-permute-start | bytes 393224 | tf_op jit(solution)/shard_map/ppermute | solution.py:468
  41.4 7.5 %collective-permute-start.15 = (bf16[2,128,256]{2,1,0:T(8,128)(2,1)S(1)}, bf16[2,128,256]{2,1,0:T(8,128)(2,1)S(1)}, u32[]{:S(2)}, u32[]{:S(2)}) collective-permute-start(bf16[2,128,256]{2,1,0:T(8,128)(2,1)S(1)} %get-tuple-element.43.refs_0_), channel_id=1, source_target_pairs={{0,1},{1,0},{2,3},{3,2},{4,5},{5,4},{6,7},{7,6},{8,9},{9,8},{10,11... | collective-permute-start | bytes 393224 | tf_op jit(solution)/shard_map/ppermute | solution.py:468
  42.9 9.7 %collective-permute-start.16 = (bf16[2,128,256]{2,1,0:T(8,128)(2,1)S(1)}, bf16[2,128,256]{2,1,0:T(8,128)(2,1)S(1)}, u32[]{:S(2)}, u32[]{:S(2)}) collective-permute-start(bf16[2,128,256]{2,1,0:T(8,128)(2,1)S(1)} %get-tuple-element.43.refs_0_), channel_id=1, source_target_pairs={{0,3},{1,2},{2,1},{3,0},{4,7},{5,6},{6,5},{7,4},{8,11},{9,10},{10,... | collective-permute-start | bytes 393224 | tf_op jit(solution)/shard_map/ppermute | solution.py:468
  45.4 9.5 %collective-permute-start.10 = (bf16[2,128,256]{2,1,0:T(8,128)(2,1)S(1)}, bf16[2,128,256]{2,1,0:T(8,128)(2,1)S(1)}, u32[]{:S(2)}, u32[]{:S(2)}) collective-permute-start(bf16[2,128,256]{2,1,0:T(8,128)(2,1)S(1)} %get-tuple-element.42.refs_0_), channel_id=1, source_target_pairs={{0,3},{1,2},{2,1},{3,0},{4,7},{5,6},{6,5},{7,4},{8,11},{9,10},{10,... | collective-permute-start | bytes 393224 | tf_op jit(solution)/shard_map/ppermute | solution.py:468
  46.5 8.4 %collective-permute-start.8 = (bf16[2,128,256]{2,1,0:T(8,128)(2,1)S(1)}, bf16[2,128,256]{2,1,0:T(8,128)(2,1)S(1)}, u32[]{:S(2)}, u32[]{:S(2)}) collective-permute-start(bf16[2,128,256]{2,1,0:T(8,128)(2,1)S(1)} %get-tuple-element.42.refs_0_), channel_id=1, source_target_pairs={{0,2},{1,3},{2,0},{3,1},{4,6},{5,7},{6,4},{7,5},{8,10},{9,11},{10,... | collective-permute-start | bytes 393224 | tf_op jit(solution)/shard_map/ppermute | solution.py:468
  48.5 6.4 %collective-permute-start.9 = (bf16[2,128,256]{2,1,0:T(8,128)(2,1)S(1)}, bf16[2,128,256]{2,1,0:T(8,128)(2,1)S(1)}, u32[]{:S(2)}, u32[]{:S(2)}) collective-permute-start(bf16[2,128,256]{2,1,0:T(8,128)(2,1)S(1)} %get-tuple-element.42.refs_0_), channel_id=1, source_target_pairs={{0,1},{1,0},{2,3},{3,2},{4,5},{5,4},{6,7},{7,6},{8,9},{9,8},{10,11... | collective-permute-start | bytes 393224 | tf_op jit(solution)/shard_map/ppermute | solution.py:468
  58.5 4.5 %collective-permute-start.19 = (f32[8,256]{1,0:T(8,128)S(1)}, f32[8,256]{1,0:T(8,128)S(1)}, u32[]{:S(2)}, u32[]{:S(2)}) collective-permute-start(f32[8,256]{1,0:T(8,128)S(1)} %get-tuple-element.47.refs_0_), channel_id=1, source_target_pairs={{0,32},{4,36},{8,40},{12,44},{16,48},{20,52},{24,56},{28,60},{32,0... | collective-permute-start | bytes 24584 | tf_op jit(solution)/shard_map/ppermute | solution.py:468
  60.7 10.3 %collective-permute-start.17 = (bf16[2,128,512]{2,1,0:T(8,128)(2,1)S(1)}, bf16[2,128,512]{2,1,0:T(8,128)(2,1)S(1)}, u32[]{:S(2)}, u32[]{:S(2)}) collective-permute-start(bf16[2,128,512]{2,1,0:T(8,128)(2,1)S(1)} %analysis.21), channel_id=1, source_target_pairs={{0,2},{1,3},{2,0},{3,1},{4,6},{5,7},{6,4},{7,5},{8,10},{9,11},{10,... | collective-permute-start | bytes 786440 | tf_op jit(solution)/shard_map/ppermute | solution.py:468
  62.5 11.3 %collective-permute-start.18 = (bf16[2,128,512]{2,1,0:T(8,128)(2,1)S(1)}, bf16[2,128,512]{2,1,0:T(8,128)(2,1)S(1)}, u32[]{:S(2)}, u32[]{:S(2)}) collective-permute-start(bf16[2,128,512]{2,1,0:T(8,128)(2,1)S(1)} %analysis.22), channel_id=1, source_target_pairs={{0,1},{1,0},{2,3},{3,2},{4,5},{5,4},{6,7},{7,6},{8,9},{9,8},{10,11... | collective-permute-start | bytes 786440 | tf_op jit(solution)/shard_map/ppermute | solution.py:468
  63.8 9.9 %collective-permute-start.20 = (bf16[2,128,512]{2,1,0:T(8,128)(2,1)S(1)}, bf16[2,128,512]{2,1,0:T(8,128)(2,1)S(1)}, u32[]{:S(2)}, u32[]{:S(2)}) collective-permute-start(bf16[2,128,512]{2,1,0:T(8,128)(2,1)S(1)} %analysis.23), channel_id=1, source_target_pairs={{0,3},{1,2},{2,1},{3,0},{4,7},{5,6},{6,5},{7,4},{8,11},{9,10},{10,... | collective-permute-start | bytes 786440 | tf_op jit(solution)/shard_map/ppermute | solution.py:468
  64.9 6.1 %collective-permute-start.23 = (f32[16,256]{1,0:T(8,128)S(1)}, f32[16,256]{1,0:T(8,128)S(1)}, u32[]{:S(2)}, u32[]{:S(2)}) collective-permute-start(f32[16,256]{1,0:T(8,128)S(1)} %join.4.refs_0_), channel_id=1, source_target_pairs={{0,224},{4,228},{8,232},{12,236},{16,240},{20,244},{24,248},{28,25... | collective-permute-start | bytes 49160 | tf_op jit(solution)/shard_map/ppermute | solution.py:468
  71.0 13.9 %collective-permute-start.24 = (f32[32,256]{1,0:T(8,128)S(1)}, f32[32,256]{1,0:T(8,128)S(1)}, u32[]{:S(2)}, u32[]{:S(2)}) collective-permute-start(f32[32,256]{1,0:T(8,128)S(1)} %join.5.refs_0_), channel_id=1, source_target_pairs={{0,64},{4,68},{8,72},{12,76},{16,80},{20,84},{24,88},{28,92},{32,9... | collective-permute-start | bytes 98312 | tf_op jit(solution)/shard_map/ppermute | solution.py:468
  74.5 10.4 %collective-permute-start.21 = (bf16[16,512]{1,0:T(8,128)(2,1)S(1)}, bf16[16,512]{1,0:T(8,128)(2,1)S(1)}, u32[]{:S(2)}, u32[]{:S(2)}) collective-permute-start(bf16[16,512]{1,0:T(8,128)(2,1)S(1)} %get-tuple-element.50), channel_id=1, source_target_pairs={{0,4},{4,0},{8,12},{12,8},{16,20},{20,16},{24,28},{28,24},{32,36},... | collective-permute-start | bytes 49160 | tf_op jit(solution)/shard_map/ppermute | solution.py:468
  83.0 5.0 %collective-permute-start.22 = (bf16[16,512]{1,0:T(8,128)(2,1)S(1)}, bf16[16,512]{1,0:T(8,128)(2,1)S(1)}, u32[]{:S(2)}, u32[]{:S(2)}) collective-permute-start(bf16[16,512]{1,0:T(8,128)(2,1)S(1)} %get-tuple-element.51), channel_id=1, source_target_pairs={{4,8},{8,4},{12,16},{16,12},{20,24},{24,20},{28,32},{32,28},{36,40... | collective-permute-start | bytes 49160 | tf_op jit(solution)/shard_map/ppermute | solution.py:473
  88.0 4.7 %collective-permute-start.27 = (f32[64,256]{1,0:T(8,128)S(1)}, f32[64,256]{1,0:T(8,128)S(1)}, u32[]{:S(2)}, u32[]{:S(2)}) collective-permute-start(f32[64,256]{1,0:T(8,128)S(1)} %join.6.refs_0_), channel_id=1, source_target_pairs={{0,24},{4,28},{8,16},{12,20},{16,8},{20,12},{24,0},{28,4},{32,56},... | collective-permute-start | bytes 196616 | tf_op jit(solution)/shard_map/ppermute | solution.py:468
  90.8 4.7 %collective-permute-start.25 = (f32[64,256]{1,0:T(8,128)S(1)}, f32[64,256]{1,0:T(8,128)S(1)}, u32[]{:S(2)}, u32[]{:S(2)}) collective-permute-start(f32[64,256]{1,0:T(8,128)S(1)} %join.6.refs_0_), channel_id=1, source_target_pairs={{0,16},{4,20},{8,24},{12,28},{16,0},{20,4},{24,8},{28,12},{32,48},... | collective-permute-start | bytes 196616 | tf_op jit(solution)/shard_map/ppermute | solution.py:468
  90.8 4.7 %collective-permute-start.26 = (f32[64,256]{1,0:T(8,128)S(1)}, f32[64,256]{1,0:T(8,128)S(1)}, u32[]{:S(2)}, u32[]{:S(2)}) collective-permute-start(f32[64,256]{1,0:T(8,128)S(1)} %join.6.refs_0_), channel_id=1, source_target_pairs={{0,8},{4,12},{8,0},{12,4},{16,24},{20,28},{24,16},{28,20},{32,40},... | collective-permute-start | bytes 196616 | tf_op jit(solution)/shard_map/ppermute | solution.py:468
  95.5 2.2 %collective-permute-start.28 = (f32[256,256]{1,0:T(8,128)S(1)}, f32[256,256]{1,0:T(8,128)S(1)}, u32[]{:S(2)}, u32[]{:S(2)}) collective-permute-start(f32[256,256]{1,0:T(8,128)S(1)} %join.7.rows_ref), channel_id=1, source_target_pairs={{0,4},{4,0},{8,12},{12,8},{16,20},{20,16},{24,28},{28,24},{32,36},... | collective-permute-start | bytes 786440 | tf_op jit(solution)/shard_map/ppermute | solution.py:468
  (5 other events, 16.6 us)
